TPU v7x, 128 devices: a whole 4x4x4 slice. The times are simulated.
128 devices in a mesh: grp: 4 (over z_hi, core), dev: 32 (over z_lo, y, x).
Axes of the slice: x: 4, y: 4, z: 4 (z_hi: 2, z_lo: 2; z = z_hi * 2 + z_lo), core: 2. Of those that a mesh axis runs over, the one named last changes fastest.
Arguments:
- records: bfloat16 [1024, 16384], P('grp', 'dev'), may hold values from -30 to 30
- channel_map: int32 [4, 256], P('grp'), may hold values from 0 to 255, each once within a row
- source_offset: int32 [2, 128], P(None, ('grp', 'dev')), may hold values from 0 to 6
Outputs:
- correlations: bfloat16 [1, 512, 1024, 1024], P(None, None, ('grp', 'dev'))
All inputs are finite; a program needn't handle non-finite values.
Results may differ from a plain program's by a relative error of at most 0.0075.
Values may be sent and summed in bfloat16 or wider, within the bound.
No kernel may reach another device: no remote copies, remote signals or barrier semaphores. Data moves between devices by JAX's collectives and lax.ppermute only.
A program may use at most 192 MiB of HBM per device.

v0:
```python
import math

import jax
import jax.numpy as jnp
from jax import lax
from jax.sharding import PartitionSpec as P

W = 2048
NLAG = 1024
STACKS = 1
SEGS = 8
SRC_DEV = 2
STEPS = 2


def tables(width, bin_count, lag_count):
    sample_index = jnp.arange(width, dtype=jnp.int32)[:, None]
    bin_index = jnp.arange(bin_count, dtype=jnp.int32)[None, :]
    phase_turns = sample_index * bin_index % width
    angles = phase_turns.astype(jnp.float32) * (2.0 * math.pi / width)
    forward = jnp.concatenate([jnp.cos(angles), -jnp.sin(angles)], axis=1).astype(jnp.bfloat16)
    lag_turns = (jnp.arange(lag_count, dtype=jnp.int32) - lag_count // 2) % width
    inv_turns = jnp.arange(bin_count, dtype=jnp.int32)[:, None] * lag_turns[None, :] % width
    inv_angles = inv_turns.astype(jnp.float32) * (2.0 * math.pi / width)
    inverse = jnp.concatenate([jnp.cos(inv_angles), -jnp.sin(inv_angles)], axis=0).astype(
        jnp.bfloat16
    )
    return (forward, inverse)


def whiten(spectra, kept_bins):
    real_part = spectra[:, :kept_bins]
    imag_part = spectra[:, kept_bins:]
    powers = real_part * real_part + imag_part * imag_part
    padded = jnp.pad(powers, ((0, 0), (4, 4)))
    smooth = padded[:, 0:kept_bins]
    for offset_bin in range(1, 9):
        smooth = smooth + padded[:, offset_bin : offset_bin + kept_bins]
    smooth = smooth / 9.0
    water_level = jnp.mean(powers, axis=1, keepdims=True)
    inv_norm = lax.rsqrt(smooth + water_level + 1e-05)
    return jnp.concatenate([real_part * inv_norm, imag_part * inv_norm], axis=1)


def correlate(sources, resident, inverse, kept_bins):
    source_count = sources.shape[0]
    channels = resident.shape[0]
    src_view = sources.reshape(source_count, STACKS, SEGS, 2 * kept_bins)
    res_view = resident.reshape(channels, STACKS, SEGS, 2 * kept_bins)
    src_re, src_im = (src_view[..., :kept_bins], src_view[..., kept_bins:])
    res_re, res_im = (res_view[..., :kept_bins], res_view[..., kept_bins:])
    form = "sqgk,cqgk->qsck"
    real_part = jnp.einsum(form, src_re, res_re, preferred_element_type=jnp.float32)
    real_part = real_part + jnp.einsum(form, src_im, res_im, preferred_element_type=jnp.float32)
    imag_part = jnp.einsum(form, src_im, res_re, preferred_element_type=jnp.float32)
    imag_part = imag_part - jnp.einsum(form, src_re, res_im, preferred_element_type=jnp.float32)
    factor = 2.0 / math.sqrt(SEGS * kept_bins)
    cross_spec = (factor * jnp.concatenate([real_part, imag_part], axis=-1)).astype(jnp.bfloat16)
    lagged = jnp.dot(
        cross_spec.reshape(-1, 2 * kept_bins), inverse, preferred_element_type=jnp.float32
    )
    return lagged.astype(jnp.bfloat16).reshape(STACKS, source_count, channels, -1)


def local(records, channel_map, source_offset):
    kept_bins = W // 2
    forward, inverse = tables(W, kept_bins, NLAG)
    ordered = jnp.take(records, channel_map[0], axis=0)
    regrouped = lax.all_to_all(ordered, "dev", split_axis=0, concat_axis=1, tiled=True)
    channels = regrouped.shape[0]
    spectra = jnp.dot(regrouped.reshape(-1, W), forward, preferred_element_type=jnp.float32)
    whitened = whiten(spectra, kept_bins).astype(jnp.bfloat16).reshape(channels, STACKS * SEGS, W)
    results = []
    for step_index in range(STEPS):
        own_block = lax.dynamic_slice_in_dim(whitened, source_offset[step_index, 0], SRC_DEV, 0)
        arrived = lax.all_gather(own_block, ("grp", "dev"), axis=0, tiled=True)
        results.append(correlate(arrived, whitened, inverse, kept_bins))
    return jnp.concatenate(results, axis=1)


def solution(mesh):
    return jax.shard_map(
        local,
        mesh=mesh,
        in_specs=(P("grp", "dev"), P("grp", None), P(None, ("grp", "dev"))),
        out_specs=P(None, None, ("grp", "dev"), None),
        check_vma=False,
    )
```

profile of v0, /device:TPU:1, one launch (start us, length us, event | category | flops | bytes accessed | tf_op | source)
XLA Modules:
  0.0 836.4 jit_solution(215738174881408550)
XLA Ops:
  6.5 0.7 compare_select_fusion.1
  7.8 1.3 reduce.3
  9.2 1.2 gather_fusion
  10.4 0.8 bitcast_select_fusion
  11.2 9.2 %all-to-all-start = ((bf16[32,8,512]{2,1,0:T(8,128)(2,1)}), bf16[32,8,512]{2,1,0:T(8,128)(2,1)S(1)}, u32[]{:S(2)}, u32[]{:S(2)}) async-start(bf16[32,8,512]{2,1,0:T(8,128)(2,1)} %bitcast_select_fusion), calls=%async_computation | async-start | bytes 524288 | tf_op jit(solution)/shard_map/all_to_all | solution.py:69
  20.5 34.9 %negate_convert_fusion = (bf16[2048,1024]{1,0:T(8,128)(2,1)}, bf16[2048,1024]{1,0:T(8,128)(2,1)}) fusion(), kind=kLoop, calls=%fused_computation.24 | loop fusion | flops 35651584 | bytes 8388608 | tf_op jit(solution)/shard_map/convert.11
  55.4 0.6 fusion.65
  60.2 4.4 fusion.9
  64.7 0.6 fusion.48
  65.4 0.7 fusion.51
  66.8 18.3 %cosine_convert_fusion.1 = (bf16[1024,1024]{1,0:T(8,128)(2,1)}, bf16[1024,1024]{1,0:T(8,128)(2,1)}) fusion(s32[1024]{0:T(1024)S(1)} %add_select_fusion.2), kind=kLoop, calls=%fused_computation.43 | loop fusion | flops 17825792 | bytes 4198400 | tf_op jit(solution)/shard_map/convert
  85.1 1.5 copy.32
  86.6 2.3 copy.33
  88.9 293.8 %all-gather.3.cloned.1.call-done = bf16[256,8,2048]{2,1,0:T(8,128)(2,1)} async-done(((bf16[2,8,2048]{2,1,0:T(8,128)(2,1)}), bf16[256,8,2048]{2,1,0:T(8,128)(2,1)}) %all-gather.3.cloned.1.call-update) | async-done | bytes 8388624 | tf_op jit(solution)/shard_map/all_gather | solution.py:76
  382.7 13.4 %copy.31 = bf16[256,8,2048]{0,1,2:T(8,128)(2,1)} copy(bf16[256,8,2048]{2,1,0:T(8,128)(2,1)} %all-gather.3.cloned.1.call-done) | data formatting | bytes 16777216 | tf_op jit(solution)/shard_map/all_gather | solution.py:76
  396.1 7.2 fusion.29
  403.3 4.5 fusion.28
  407.8 289.0 %all-gather.5.cloned.1.call-done = bf16[256,8,2048]{2,1,0:T(8,128)(2,1)} async-done(((bf16[2,8,2048]{2,1,0:T(8,128)(2,1)}), bf16[256,8,2048]{2,1,0:T(8,128)(2,1)}) %all-gather.5.cloned.1.call-update) | async-done | bytes 8388624 | tf_op jit(solution)/shard_map/all_gather | solution.py:76
  696.8 13.3 %copy.38 = bf16[256,8,2048]{0,1,2:T(8,128)(2,1)} copy(bf16[256,8,2048]{2,1,0:T(8,128)(2,1)} %all-gather.5.cloned.1.call-done) | data formatting | bytes 16777216 | tf_op jit(solution)/shard_map/all_gather | solution.py:76
  710.1 7.8 fusion.33
  717.9 4.7 fusion.32
  722.6 7.8 add_bitcast_fusion.1
  730.5 8.8 %copy.34 = f32[1,256,8,1024]{3,2,1,0:T(8,128)} copy(f32[1,256,8,1024]{1,2,3,0:T(8,128)} %add_bitcast_fusion.1) | data formatting | bytes 16777216 | tf_op jit(solution)/shard_map/add | solution.py:54
  739.2 9.1 %subtract_bitcast_fusion.1 = f32[1,256,8,1024]{1,2,3,0:T(8,128)} fusion(f32[1024,8,256]{2,1,0:T(8,128)} %fusion.28, bf16[8,8,1024]{1,0,2:T(8,128)(2,1)S(1)} %copy.32, bf16[256,1,8,2048]{0,2,3,1:T(8,128)(2,1)} %bitcast.76), kind=kOutput, calls=%fused_computation.22 | convolution fusion | flops 35651584 | bytes 21102592 | tf_op jit(solution)/shard_map/sqgk,cqgk->qsck/dot_general | solution.py:55
  748.4 8.8 %copy.37 = f32[1,256,8,1024]{3,2,1,0:T(8,128)} copy(f32[1,256,8,1024]{1,2,3,0:T(8,128)} %subtract_bitcast_fusion.1) | data formatting | bytes 16777216 | tf_op jit(solution)/shard_map/sub | solution.py:56
  757.2 9.7 %add_bitcast_fusion = f32[1,256,8,1024]{1,2,3,0:T(8,128)} fusion(f32[1024,8,256]{2,1,0:T(8,128)} %fusion.33, bf16[8,8,1024]{1,0,2:T(8,128)(2,1)} %copy.33, bf16[256,1,8,2048]{0,2,3,1:T(8,128)(2,1)} %bitcast.72), kind=kOutput, calls=%fused_computation.19 | convolution fusion | flops 35651584 | bytes 23068672 | tf_op jit(solution)/shard_map/sqgk,cqgk->qsck/dot_general | solution.py:54
  766.9 8.8 %copy.41 = f32[1,256,8,1024]{3,2,1,0:T(8,128)} copy(f32[1,256,8,1024]{1,2,3,0:T(8,128)} %add_bitcast_fusion) | data formatting | bytes 16777216 | tf_op jit(solution)/shard_map/add | solution.py:54
  775.6 9.1 %subtract_bitcast_fusion = f32[1,256,8,1024]{1,2,3,0:T(8,128)} fusion(f32[1024,8,256]{2,1,0:T(8,128)} %fusion.32, bf16[8,8,1024]{1,0,2:T(8,128)(2,1)S(1)} %copy.32, bf16[256,1,8,2048]{0,2,3,1:T(8,128)(2,1)} %bitcast.73), kind=kOutput, calls=%fused_computation.18 | convolution fusion | flops 35651584 | bytes 21102592 | tf_op jit(solution)/shard_map/sqgk,cqgk->qsck/dot_general | solution.py:55
  784.8 8.9 %copy.44 = f32[1,256,8,1024]{3,2,1,0:T(8,128)} copy(f32[1,256,8,1024]{1,2,3,0:T(8,128)} %subtract_bitcast_fusion) | data formatting | bytes 16777216 | tf_op jit(solution)/shard_map/sub | solution.py:56
  793.6 14.5 %convert_bitcast_fusion.1 = bf16[1,256,8,1024]{3,2,1,0:T(8,128)(2,1)} fusion(f32[2048,1024]{1,0:T(8,128)} %bitcast.82, f32[2048,1024]{1,0:T(8,128)} %bitcast.81, bf16[1024,1024]{1,0:T(8,128)(2,1)} %get-tuple-element.12, bf16[1024,1024]{1,0:T(8,128)(2,1)S(1)} %copy-done.6), kind=kOutput, calls=%fused_computation.41 | convolution fusion | flops 8613003264 | bytes 25165824 | tf_op jit(solution)/shard_map/dot_general | solution.py:59
  808.2 13.8 %convert_bitcast_fusion = bf16[1,256,8,1024]{3,2,1,0:T(8,128)(2,1)} fusion(f32[2048,1024]{1,0:T(8,128)} %bitcast.84, f32[2048,1024]{1,0:T(8,128)} %bitcast.83, bf16[1024,1024]{1,0:T(8,128)(2,1)S(1)} %copy-done.7, bf16[1024,1024]{1,0:T(8,128)(2,1)S(1)} %copy-done.6), kind=kOutput, calls=%fused_computation.40 | convolution fusion | flops 8613003264 | bytes 25165824 | tf_op jit(solution)/shard_map/dot_general | solution.py:59
  822.0 7.6 pad_maximum_fusion
  (38 shorter events, 1.9 us)
Async XLA Ops:
  6.5 2.7 copy-start
  6.5 48.9 %copy-start.8 = (s32[2,1]{0,1:T(1,128)S(1)}, s32[2,1]{0,1:T(1,128)}, u32[]{:S(2)}) copy-start(s32[2,1]{0,1:T(1,128)} %param.5) | copy-start | bytes 28
  11.2 48.7 %all-to-all-start = ((bf16[32,8,512]{2,1,0:T(8,128)(2,1)}), bf16[32,8,512]{2,1,0:T(8,128)(2,1)S(1)}, u32[]{:S(2)}, u32[]{:S(2)}) async-start(bf16[32,8,512]{2,1,0:T(8,128)(2,1)} %bitcast_select_fusion), calls=%async_computation | async-start | bytes 524288 | tf_op jit(solution)/shard_map/all_to_all | solution.py:69
  20.5 362.2 %all-gather.3.cloned.1.call-start = ((), (), s32[]{:S(2)}) async-start(), calls=%async_computation.1 | async-start | bytes 8454144 | tf_op jit(solution)/shard_map/all_gather | solution.py:76
  66.0 630.7 %all-gather.5.cloned.1.call-start = ((), (), s32[]{:S(2)}) async-start(), calls=%async_computation.2 | async-start | bytes 8454144 | tf_op jit(solution)/shard_map/all_gather | solution.py:76
  396.1 7.2 copy-start.3
  396.1 7.2 copy-start.4
  710.1 7.8 copy-start.2
  710.1 7.8 copy-start.5
  710.1 12.5 %slice-start = ((s8[8388608]{0:T(1024)(128)(4,1)}), s8[4194304]{0:T(1024)(128)(4,1)S(1)}, s32[]{:S(2)}) async-start(s8[8388608]{0:T(1024)(128)(4,1)} %bitcast.78), calls=%async_computation.3 | async-start | bytes 8388608
  717.9 4.7 slice-start.1
  784.8 8.9 %copy-start.6 = (bf16[1024,1024]{1,0:T(8,128)(2,1)S(1)}, bf16[1024,1024]{1,0:T(8,128)(2,1)}, u32[]{:S(2)}) copy-start(bf16[1024,1024]{1,0:T(8,128)(2,1)} %get-tuple-element.11) | copy-start | bytes 6291460
  793.6 14.5 %copy-start.7 = (bf16[1024,1024]{1,0:T(8,128)(2,1)S(1)}, bf16[1024,1024]{1,0:T(8,128)(2,1)}, u32[]{:S(2)}) copy-start(bf16[1024,1024]{1,0:T(8,128)(2,1)} %get-tuple-element.12) | copy-start | bytes 6291460
  808.2 21.4 %copy-start.1 = (bf16[256,512]{1,0:T(8,128)(2,1)S(1)}, bf16[256,512]{1,0:T(8,128)(2,1)}, u32[]{:S(2)}) copy-start(bf16[256,512]{1,0:T(8,128)(2,1)} %param.3) | copy-start | bytes 786436
Sparse Core Ops, SparseCore 0:
  66.2 316.4 all-gather.2
  384.4 312.3 all-gather.4
where the time goes:
time: 838 us; the launch traced here: 836 us
  waiting for transfers between devices  583 us (70%)
  matrix products  92.7 us (11%)
  local copies, waits for them, and re-layouts  68.4 us (8%)
  other arithmetic  65.2 us (8%)
  between operations  17.3 us (2%)
  starting transfers between devices  9.49 us (1%)
    all_gather x2, waiting for transfers between devices, local(): arrived = lax.all_gather(own_block, ('grp', 'dev'), axis=0, tiled=True)  583 us
    another operation x3, other arithmetic  53.8 us
    dot_general x2, matrix products, correlate(): jnp.dot(cross_spec.reshape(-1, 2 * kept_bins), inverse, preferred_element...  28.4 us
    all_gather x2, local copies, waits for them, and re-layouts, local(): arrived = lax.all_gather(own_block, ('grp', 'dev'), axis=0, tiled=True)  26.7 us
    dot_general x2, matrix products, correlate(): jnp.einsum(form, src_im, res_re, preferred_element_type=jnp.float32)  18.2 us
    sub x2, local copies, waits for them, and re-layouts, correlate(): imag_part - jnp.einsum(form, src_re, res_im, preferred_element_type=jnp.f...  17.7 us
    dot_general x2, matrix products, correlate(): jnp.einsum(form, src_im, res_im, preferred_element_type=jnp.float32)  17.5 us
    add x2, local copies, waits for them, and re-layouts, correlate(): real_part + jnp.einsum(form, src_im, res_im, preferred_element_type=jnp.f...  17.5 us
  transfers between devices with their start and end apart: 3, of which 2 were waited for; matrix products, arithmetic and copies ran while one was open for 10% of the time, Pallas kernels for 0%

commit v1 on v0

v1 whole, which is shorter than its diff:
```python
import math

import jax
import jax.numpy as jnp
import numpy as np
from jax import lax
from jax.experimental import pallas as pl
from jax.experimental.pallas import tpu as pltpu
from jax.sharding import PartitionSpec as P

W = 2048
BINS = 1024
NLAG = 1024
SEGS = 8
CH_DEV = 8
SRC_DEV = 2
STEPS = 2
KIN = 16
BLK = SEGS * 2 * KIN
NBLK = BINS // KIN
WIDE = NBLK * BLK
HALF = WIDE // 2
AXES = ("grp", "dev")
MIB = 1 << 20
FACTOR = 2.0 / math.sqrt(SEGS * BINS)
OFFSETS = (0, -1, 1, 2)


def tables():
    turns = (np.arange(W)[:, None] * np.arange(BINS)[None, :]) % W
    angles = turns.astype(np.float32) * np.float32(2.0 * math.pi / W)
    forward = np.concatenate([np.cos(angles), -np.sin(angles)], axis=1)
    lag_turns = (np.arange(NLAG) - NLAG // 2) % W
    inv_turns = (np.arange(BINS)[:, None] * lag_turns[None, :]) % W
    inv_angles = inv_turns.astype(np.float32) * np.float32(2.0 * math.pi / W)
    inverse = np.concatenate([np.cos(inv_angles), -np.sin(inv_angles)], axis=0)
    return forward.astype(jnp.bfloat16), inverse.astype(jnp.bfloat16)


def chunk_transpose(vs):
    vs = list(vs)
    axis = vs[0].ndim - 1
    chunk = lax.broadcasted_iota(jnp.int32, vs[0].shape, axis) // 16
    for bit in (1, 2, 4):
        low = (chunk & bit) == 0
        for i in range(8):
            if i & bit == 0:
                a, b = vs[i], vs[i | bit]
                vs[i] = jnp.where(low, a, pltpu.roll(b, 16 * bit, axis))
                vs[i | bit] = jnp.where(low, pltpu.roll(a, 128 - 16 * bit, axis), b)
    return vs


def front_kernel(meta, rec, table, white, keep, send, spec, scr):
    total = None
    for q in range(4):
        x = rec[:, q].astype(jnp.float32).reshape(SEGS * CH_DEV, 512).astype(jnp.bfloat16)
        part = jnp.dot(x, table[q * 512 : (q + 1) * 512, :], preferred_element_type=jnp.float32)
        total = part if total is None else total + part
    re, im = total[:, :BINS], total[:, BINS:]
    power = re * re + im * im
    water = jnp.sum(power, axis=1, keepdims=True) * (1.0 / BINS)
    wide = jnp.concatenate([power, jnp.zeros((SEGS * CH_DEV, 128), jnp.float32)], axis=1)
    run = wide
    for shift in (1, 2, 4):
        run = run + pltpu.roll(run, shift, 1)
    run = run + pltpu.roll(wide, 8, 1)
    smooth = pltpu.roll(run, BINS + 128 - 4, 1)[:, :BINS] * (1.0 / 9.0)
    scale = lax.rsqrt(smooth + water + 1e-5)
    spec[:, :BINS] = re * scale
    spec[:, BINS:] = im * scale
    for kv in range(8):
        for h in range(2):
            vs = [
                spec[g * 8 : g * 8 + 8, ri * BINS + kv * 128 : ri * BINS + kv * 128 + 128]
                for g in range(4 * h, 4 * h + 4)
                for ri in range(2)
            ]
            for j, w in enumerate(chunk_transpose(vs)):
                at = (kv * 8 + j) * BLK + h * 128
                scr[:, at : at + 128] = w
    white[...] = scr[...].astype(jnp.bfloat16)
    core = meta[0]
    pair = lax.broadcasted_iota(jnp.int32, (CH_DEV, HALF), 0) // 2
    for out, half in ((keep, core), (send, 1 - core)):
        x = scr[:, pl.ds(pl.multiple_of(half * HALF, HALF), HALF)]
        a = jnp.where(pair == 2 * core, pltpu.roll(x, meta[1], 0), 0.0)
        b = jnp.where(pair == 2 * core + 1, pltpu.roll(x, meta[2], 0), 0.0)
        out[...] = (a + b).astype(jnp.bfloat16)


def front(meta, rec, table):
    vmem = pl.BlockSpec(memory_space=pltpu.VMEM)
    return pl.pallas_call(
        front_kernel,
        out_shape=(
            jax.ShapeDtypeStruct((CH_DEV, WIDE), jnp.bfloat16),
            jax.ShapeDtypeStruct((CH_DEV, HALF), jnp.bfloat16),
            jax.ShapeDtypeStruct((CH_DEV, HALF), jnp.bfloat16),
        ),
        in_specs=[pl.BlockSpec(memory_space=pltpu.SMEM), vmem, vmem],
        out_specs=(vmem, vmem, vmem),
        scratch_shapes=[
            pltpu.VMEM((SEGS * CH_DEV, 2 * BINS), jnp.float32),
            pltpu.VMEM((CH_DEV, WIDE), jnp.float32),
        ],
        compiler_params=pltpu.CompilerParams(vmem_limit_bytes=32 * MIB),
        name="front",
    )(meta, rec, table)


def corr_kernel(
    first, meta, b_ref, m0, m1, m2, m3, sib, e_hbm, *rest
):
    out, rows_scr, x_scr, e_scr, ov, yf, yb, sems = rest if first else rest[1:]
    e_copy = pltpu.make_async_copy(e_hbm, e_scr, sems.at[0])
    e_copy.start()
    core = meta[0]
    own = b_ref[...].astype(jnp.float32)
    lane = lax.broadcasted_iota(jnp.int32, (CH_DEV, WIDE), 1)
    turned = jnp.where(
        (lane & 16) == 0, -pltpu.roll(own, WIDE - 16, 1), pltpu.roll(own, 16, 1)
    )
    rows_scr[0:8, :] = own
    rows_scr[8:16, :] = turned
    diag = lax.broadcasted_iota(jnp.int32, (KIN, BLK), 0) == (
        lax.broadcasted_iota(jnp.int32, (KIN, BLK), 1) & 15
    )

    def group(j, mine):
        half = core if mine else 1 - core
        g = half * 4 + j
        for i in range(8):
            lanes = pl.ds(pl.multiple_of((j * 8 + i) * BLK, BLK), BLK)
            if mine:
                a = jnp.concatenate([m[:, lanes] for m in (m0, m1, m2, m3)], axis=0)
            else:
                a = sib[:, lanes]
            r = rows_scr[:, pl.ds(pl.multiple_of((g * 8 + i) * BLK, BLK), BLK)]
            block = jnp.where(diag[None], r[:, None, :], 0.0).astype(jnp.bfloat16)
            block = block.reshape(2 * CH_DEV * KIN, BLK)
            prod = lax.dot_general(
                a, block, (((1,), (1,)), ((), ())), preferred_element_type=jnp.float32
            )
            ov[i] = prod * FACTOR
        for ri in range(2):
            at = pl.ds(pl.multiple_of(ri * BINS + g * 128, 128), 128)
            for rb in range(8):
                if mine:
                    vs = [ov[i, rb * 16 : rb * 16 + 16, ri * 128 : ri * 128 + 128] for i in range(8)]
                else:
                    n0, n1 = 2 * rb, 2 * rb + 1
                    s0 = ((n0 % 4) * 4 + n0 // 4) * 8
                    s1 = ((n1 % 4) * 4 + n1 // 4) * 8
                    vs = [
                        jnp.concatenate(
                            [
                                ov[i, s0 : s0 + 8, ri * 128 : ri * 128 + 128],
                                ov[i, s1 : s1 + 8, ri * 128 : ri * 128 + 128],
                            ],
                            axis=0,
                        )
                        for i in range(8)
                    ]
                for c, w in enumerate(chunk_transpose(vs)):
                    x_scr[c * 128 + rb * 16 : c * 128 + rb * 16 + 16, at] = w.astype(jnp.bfloat16)

    @pl.loop(0, 4)
    def _(j):
        group(j, True)

    @pl.loop(0, 4)
    def _(j):
        group(j, False)

    e_copy.wait()

    @pl.loop(0, 4)
    def _(n):
        lanes = pl.ds(pl.multiple_of(n * 256, 256), 256)
        y = jnp.dot(x_scr[...], e_scr[:, lanes], preferred_element_type=jnp.float32)
        for c in range(CH_DEV):
            for h in range(2):
                yf[h, pl.ds(c, 128, stride=8), :] = y[c * 128 : c * 128 + 128, h * 128 : h * 128 + 128]
        for h in range(2):
            lanes = pl.ds(pl.multiple_of(n * 256 + h * 128, 128), 128)
            yb[:, lanes] = yf[h].astype(jnp.bfloat16)

    def copy(n):
        return pltpu.make_async_copy(
            yb.at[pl.ds(pl.multiple_of(n * 16, 16), 16)],
            out.at[pl.ds(pl.multiple_of(meta[1 + n] * 16, 16), 16)],
            sems.at[1],
        )

    @pl.loop(0, 64)
    def _(n):
        copy(n).start()

    @pl.loop(0, 64)
    def _(n):
        copy(n).wait()


def corr(meta, white, mine, sib, inverse, out):
    first = out is None
    vmem = pl.BlockSpec(memory_space=pltpu.VMEM)
    anym = pl.BlockSpec(memory_space=pl.ANY)
    args = [meta, white, *mine, sib, inverse] + ([] if first else [out])
    return pl.pallas_call(
        lambda *refs: corr_kernel(first, *refs),
        out_shape=jax.ShapeDtypeStruct((STEPS * 256 * CH_DEV, NLAG), jnp.bfloat16),
        in_specs=[pl.BlockSpec(memory_space=pltpu.SMEM)] + [vmem] * 6 + [anym] * (len(args) - 7),
        out_specs=anym,
        scratch_shapes=[
            pltpu.VMEM((16, WIDE), jnp.float32),
            pltpu.VMEM((1024, 2 * BINS), jnp.bfloat16),
            pltpu.VMEM((2 * BINS, NLAG), jnp.bfloat16),
            pltpu.VMEM((8, 128, 256), jnp.float32),
            pltpu.VMEM((2, 1024, 128), jnp.float32),
            pltpu.VMEM((1024, NLAG), jnp.bfloat16),
            pltpu.SemaphoreType.DMA((2,)),
        ],
        input_output_aliases={} if first else {8: 0},
        compiler_params=pltpu.CompilerParams(vmem_limit_bytes=40 * MIB),
        cost_estimate=pl.CostEstimate(
            flops=7 * 1024 * 2048 * 1024, bytes_accessed=12 * MIB, transcendentals=0
        ),
        name="corr",
    )(*args)


def device(x, y, z, core):
    return ((z // 2) * 2 + core) * 32 + (z % 2) * 16 + y * 4 + x


def line_pairs(axes, step):
    pairs = []
    for core in range(2):
        for n in range(64):
            at = {"x": n % 4, "y": n // 4 % 4, "z": n // 16}
            to = dict(at)
            to[axes[core]] = (at[axes[core]] + step) % 4
            pairs.append((device(**at, core=core), device(**to, core=core)))
    return pairs


CORE_PAIRS = [
    (device(n % 4, n // 4 % 4, n // 16, core), device(n % 4, n // 4 % 4, n // 16, 1 - core))
    for core in range(2)
    for n in range(64)
]


def line(block, axes):
    return [block] + [lax.ppermute(block, AXES, line_pairs(axes, s)) for s in (1, -1, 2)]


def local(records, channel_map, source_offset):
    forward, inverse = tables()
    forward, inverse = jnp.asarray(forward), jnp.asarray(inverse)
    grp, dev = lax.axis_index("grp"), lax.axis_index("dev")
    core = grp % 2
    x0, y0, z0 = dev % 4, dev // 4 % 4, (grp // 2) * 2 + dev // 16

    pick = (channel_map[0][:, None] == jnp.arange(256, dtype=jnp.int32)[None, :]).astype(jnp.bfloat16)
    ordered = jnp.dot(pick, records, preferred_element_type=jnp.float32).astype(jnp.bfloat16)
    regrouped = lax.all_to_all(ordered.reshape(32, 8, 512), "dev", split_axis=0, concat_axis=0, tiled=True)

    turns = (4 * core + 2 * jnp.arange(2, dtype=jnp.int32) - source_offset[:, 0]) % 8
    front_meta = jnp.stack([core, turns[0], turns[1]])
    white, keep, send = front(front_meta, regrouped.reshape(8, 4, 8, 512), forward)
    block = keep + lax.ppermute(send, AXES, CORE_PAIRS)

    near = jnp.concatenate(line(block[None], "xz"), axis=0)
    lines = line(near, "yy")
    off = jnp.array(OFFSETS, jnp.int32)
    outer, inner = jnp.meshgrid(off, off, indexing="ij")
    xs = (x0 + jnp.where(core == 0, inner, outer)) % 4
    zs = (z0 + jnp.where(core == 0, outer, inner)) % 4
    out = None
    for k in range(4):
        ys = (y0 + OFFSETS[k]) % 4
        chip = (zs // 2) * 64 + (zs % 2) * 16 + ys * 4 + xs
        place = chip.reshape(16, 1, 1) + jnp.arange(2)[None, :, None] * 32 + jnp.arange(2)[None, None, :] * 128
        meta = jnp.concatenate([core[None], place.reshape(64)]).astype(jnp.int32)
        mine = line(lines[k], "zx")
        sib = lax.ppermute(jnp.concatenate(mine, axis=0), AXES, CORE_PAIRS)
        out = corr(meta, white, [m.reshape(32, HALF) for m in mine], sib.reshape(128, HALF), inverse, out)
    return out.reshape(1, STEPS * 256, CH_DEV, NLAG)


def solution(mesh):
    return jax.shard_map(
        local,
        mesh=mesh,
        in_specs=(P("grp", "dev"), P("grp", None), P(None, ("grp", "dev"))),
        out_specs=P(None, None, ("grp", "dev"), None),
        check_vma=False,
    )
```

time: 838 us -> 176 us (0.21)
  waiting for transfers between devices: 583 us -> 28.8 us
  matrix products: 92.7 us -> 1.66 us
  Pallas kernels: 0 us -> 66.7 us
  local copies, waits for them, and re-layouts: 68.4 us -> 8.04 us
  other arithmetic: 65.2 us -> 7.09 us
  starting transfers between devices: 9.49 us -> 61.5 us
  between operations: 17.3 us -> 0.55 us
    all_gather x2 -> x0, waiting for transfers between devices: 583 us -> none  [local(): arrived = lax.all_gather(own_block, ('grp', 'dev'), axis=0, tiled=True)]
    dot_general x11 -> x1, matrix products: 92.7 us -> 1.66 us  [local(): jnp.dot(pick, records, preferred_element_type=jnp.float32)]
    pallas_call x0 -> x5, Pallas kernels: none -> 66.7 us  [the longest x4 63.5 us: corr(): pl.pallas_call(lambda *refs: corr_kernel(first, *refs), out_shape=jax.Sha...]
    another operation x3 -> x1, other arithmetic: 53.8 us -> 0.08 us  [local(): front_meta = jnp.stack([core, turns[0], turns[1]])]
    ppermute x0 -> x23, starting transfers between devices: none -> 52.3 us  [the longest x4 29.3 us: local(): sib = lax.ppermute(jnp.concatenate(mine, axis=0), AXES, CORE_PAIRS)]
    all_gather x2 -> x0, local copies, waits for them, and re-layouts: 26.7 us -> none  [local(): arrived = lax.all_gather(own_block, ('grp', 'dev'), axis=0, tiled=True)]
    ppermute x0 -> x23, waiting for transfers between devices: none -> 23.3 us  [the longest x18 22.7 us: line(): lax.ppermute(block, AXES, line_pairs(axes, s))]
    sub x2 -> x0, local copies, waits for them, and re-layouts: 17.7 us -> none  [correlate(): imag_part - jnp.einsum(form, src_re, res_im, preferred_element_type=jnp.f...]
  transfers between devices with their start and end apart: 3 -> 24, of which waited for: 2 -> 7; matrix products, arithmetic and copies ran while one was open for 10% -> 4% of each run, Pallas kernels for 0% -> 27%
where the time goes in v1:
time: 176 us; the launch traced here: 174 us
  Pallas kernels  66.7 us (38%)
  starting transfers between devices  61.5 us (35%)
  waiting for transfers between devices  28.8 us (16%)
  local copies, waits for them, and re-layouts  8.04 us (5%)
  other arithmetic  7.09 us (4%)
    pallas_call x4, Pallas kernels, corr(): pl.pallas_call(lambda *refs: corr_kernel(first, *refs), out_shape=jax.Sha...  63.5 us
    ppermute x4, starting transfers between devices, local(): sib = lax.ppermute(jnp.concatenate(mine, axis=0), AXES, CORE_PAIRS)  29.3 us
    ppermute x18, waiting for transfers between devices, line(): lax.ppermute(block, AXES, line_pairs(axes, s))  22.7 us
    ppermute x18, starting transfers between devices, line(): lax.ppermute(block, AXES, line_pairs(axes, s))  20.8 us
    all_to_all x1, starting transfers between devices, local(): lax.all_to_all(ordered.reshape(32, 8, 512), 'dev', split_axis=0, concat_a...  9.23 us
    unnamed x15, local copies, waits for them, and re-layouts  7.4 us
    all_to_all x1, waiting for transfers between devices, local(): lax.all_to_all(ordered.reshape(32, 8, 512), 'dev', split_axis=0, concat_a...  5.54 us
    concatenate x3, other arithmetic, local(): sib = lax.ppermute(jnp.concatenate(mine, axis=0), AXES, CORE_PAIRS)  4.86 us
  transfers between devices with their start and end apart: 24, of which 7 were waited for; matrix products, arithmetic and copies ran while one was open for 4% of the time, Pallas kernels for 27%

profile of v1, /device:TPU:1, one launch (start us, length us, event | category | flops | bytes accessed | tf_op | source)
XLA Modules:
  0.0 174.4 jit_solution(5701829781631746564)
XLA Ops:
  0.0 0.9 copy-done
  1.0 1.7 fusion
  2.6 9.2 %all-to-all-start = ((bf16[32,8,512]{2,1,0:T(8,128)(2,1)}), bf16[32,8,512]{2,1,0:T(8,128)(2,1)S(1)}, u32[]{:S(2)}, u32[]{:S(2)}) async-start(bf16[32,8,512]{2,1,0:T(8,128)(2,1)} %fusion), calls=%async_computation | async-start | bytes 524288 | tf_op jit(solution)/shard_map/all_to_all | solution.py:268
  14.1 5.5 %all-to-all-done = bf16[32,8,512]{2,1,0:T(8,128)(2,1)S(1)} async-done(((bf16[32,8,512]{2,1,0:T(8,128)(2,1)}), bf16[32,8,512]{2,1,0:T(8,128)(2,1)S(1)}, u32[]{:S(2)}, u32[]{:S(2)}) %all-to-all-start) | async-done | bytes 262176 | tf_op jit(solution)/shard_map/all_to_all | solution.py:268
  19.7 3.4 %copy-done.1 = bf16[2048,2048]{1,0:T(8,128)(2,1)S(1)} copy-done((bf16[2048,2048]{1,0:T(8,128)(2,1)S(1)}, bf16[2048,2048]{1,0:T(8,128)(2,1)}, u32[]{:S(2)}) %copy-start.1) | copy-done | bytes 8388632
  23.1 3.1 %front.1 = (bf16[8,16384]{1,0:T(8,128)(2,1)S(1)}, bf16[8,8192]{1,0:T(8,128)(2,1)S(1)}, bf16[8,8192]{1,0:T(8,128)(2,1)S(1)}) custom-call(s32[3]{0:T(128)S(1)} %pad_add_fusion.1.meta, bf16[8,4,8,512]{3,2,1,0:T(8,128)(2,1)S(1)} %bitcast.35, bf16[2048,2048]{1,0:T(8,128)(2,1)S(1)} %copy-done.1), custom_call_target="tpu_custom_call" | custom-call | tf_op jit(solution)/shard_map/front/pallas_call | solution.py:94
  26.2 2.2 %collective-permute-start = (bf16[8,8192]{1,0:T(8,128)(2,1)S(1)}, bf16[8,8192]{1,0:T(8,128)(2,1)S(1)}, u32[]{:S(2)}, u32[]{:S(2)}) collective-permute-start(bf16[8,8192]{1,0:T(8,128)(2,1)S(1)} %get-tuple-element.10), channel_id=1, source_target_pairs={{0,32},{1,33},{2,34},{3,35},{4,36},{5,37},{6,38},{7,39},{8,40},{9,... | collective-permute-start | bytes 393224 | tf_op jit(solution)/shard_map/ppermute | solution.py:273
  30.1 2.2 %collective-permute-start.2 = (bf16[1,8,8192]{2,1,0:T(8,128)(2,1)S(1)}, bf16[1,8,8192]{2,1,0:T(8,128)(2,1)S(1)}, u32[]{:S(2)}, u32[]{:S(2)}) collective-permute-start(bf16[1,8,8192]{2,1,0:T(8,128)(2,1)S(1)} %get-tuple-element.12), channel_id=1, source_target_pairs={{0,3},{1,0},{2,1},{3,2},{4,7},{5,4},{6,5},{7,6},{8,11},{9,8},{10,9... | collective-permute-start | bytes 393224 | tf_op jit(solution)/shard_map/ppermute | solution.py:256
  32.3 1.9 %collective-permute-start.3 = (bf16[1,8,8192]{2,1,0:T(8,128)(2,1)S(1)}, bf16[1,8,8192]{2,1,0:T(8,128)(2,1)S(1)}, u32[]{:S(2)}, u32[]{:S(2)}) collective-permute-start(bf16[1,8,8192]{2,1,0:T(8,128)(2,1)S(1)} %get-tuple-element.12), channel_id=1, source_target_pairs={{0,2},{1,3},{2,0},{3,1},{4,6},{5,7},{6,4},{7,5},{8,10},{9,11},{10,... | collective-permute-start | bytes 393224 | tf_op jit(solution)/shard_map/ppermute | solution.py:256
  35.1 2.8 %collective-permute-done.3 = bf16[1,8,8192]{2,1,0:T(8,128)(2,1)S(1)} collective-permute-done((bf16[1,8,8192]{2,1,0:T(8,128)(2,1)S(1)}, bf16[1,8,8192]{2,1,0:T(8,128)(2,1)S(1)}, u32[]{:S(2)}, u32[]{:S(2)}) %collective-permute-start.3) | collective-permute-done | bytes 131104 | tf_op jit(solution)/shard_map/ppermute | solution.py:256
  38.1 2.7 %collective-permute-start.20 = (bf16[4,8,8192]{2,1,0:T(8,128)(2,1)S(1)}, bf16[4,8,8192]{2,1,0:T(8,128)(2,1)S(1)}, u32[]{:S(2)}, u32[]{:S(2)}) collective-permute-start(bf16[4,8,8192]{2,1,0:T(8,128)(2,1)S(1)} %get-tuple-element.17), channel_id=1, source_target_pairs={{0,80},{1,81},{2,82},{3,83},{4,84},{5,85},{6,86},{7,87},{8,88},{9,... | collective-permute-start | bytes 1572872 | tf_op jit(solution)/shard_map/ppermute | solution.py:256
  41.1 2.4 %collective-permute-start.9 = (bf16[4,8,8192]{2,1,0:T(8,128)(2,1)S(1)}, bf16[4,8,8192]{2,1,0:T(8,128)(2,1)S(1)}, u32[]{:S(2)}, u32[]{:S(2)}) collective-permute-start(bf16[4,8,8192]{2,1,0:T(8,128)(2,1)S(1)} %get-tuple-element.17), channel_id=1, source_target_pairs={{0,12},{1,13},{2,14},{3,15},{4,0},{5,1},{6,2},{7,3},{8,4},{9,5},{1... | collective-permute-start | bytes 1572872 | tf_op jit(solution)/shard_map/ppermute | solution.py:256
  43.5 9.7 %collective-permute-done.19 = bf16[4,8,8192]{2,1,0:T(8,128)(2,1)S(1)} collective-permute-done((bf16[4,8,8192]{2,1,0:T(8,128)(2,1)S(1)}, bf16[4,8,8192]{2,1,0:T(8,128)(2,1)S(1)}, u32[]{:S(2)}, u32[]{:S(2)}) %collective-permute-start.19) | collective-permute-done | bytes 524320 | tf_op jit(solution)/shard_map/ppermute | solution.py:256
  53.2 1.2 collective-permute-start.4
  54.5 2.7 %collective-permute-start.16 = (bf16[4,8,8192]{2,1,0:T(8,128)(2,1)S(1)}, bf16[4,8,8192]{2,1,0:T(8,128)(2,1)S(1)}, u32[]{:S(2)}, u32[]{:S(2)}) collective-permute-start(bf16[4,8,8192]{2,1,0:T(8,128)(2,1)S(1)} %collective-permute-done.14), channel_id=1, source_target_pairs={{0,80},{1,81},{2,82},{3,83},{4,84},{5,85},{6,86},{7,87},{8,88},{9,... | collective-permute-start | bytes 1572872 | tf_op jit(solution)/shard_map/ppermute | solution.py:256
  57.3 1.3 collective-permute-start.17
  58.6 13.7 %collective-permute-start.22 = (bf16[16,8,8192]{2,1,0:T(8,128)(2,1)S(1)}, bf16[16,8,8192]{2,1,0:T(8,128)(2,1)S(1)}, u32[]{:S(2)}, u32[]{:S(2)}) collective-permute-start(bf16[16,8,8192]{2,1,0:T(8,128)(2,1)S(1)} %constant_dynamic-update-slice_fusion), channel_id=1, source_target_pairs={{0,32},{1,33},{2,34},{3,35},{4,36},{5,37},{6,38},{7,39},{8,40},{9,... | collective-permute-start | bytes 6291464 | tf_op jit(solution)/shard_map/ppermute | solution.py:288
  72.7 2.3 %collective-permute-start.11 = (bf16[4,8,8192]{2,1,0:T(8,128)(2,1)S(1)}, bf16[4,8,8192]{2,1,0:T(8,128)(2,1)S(1)}, u32[]{:S(2)}, u32[]{:S(2)}) collective-permute-start(bf16[4,8,8192]{2,1,0:T(8,128)(2,1)S(1)} %collective-permute-done.9), channel_id=1, source_target_pairs={{0,80},{1,81},{2,82},{3,83},{4,84},{5,85},{6,86},{7,87},{8,88},{9,... | collective-permute-start | bytes 1572872 | tf_op jit(solution)/shard_map/ppermute | solution.py:256
  75.0 1.3 collective-permute-start.12
  76.3 1.6 pad_maximum_fusion.2
  78.0 9.5 %collective-permute-done.10 = bf16[4,8,8192]{2,1,0:T(8,128)(2,1)S(1)} collective-permute-done((bf16[4,8,8192]{2,1,0:T(8,128)(2,1)S(1)}, bf16[4,8,8192]{2,1,0:T(8,128)(2,1)S(1)}, u32[]{:S(2)}, u32[]{:S(2)}) %collective-permute-start.10) | collective-permute-done | bytes 524320 | tf_op jit(solution)/shard_map/ppermute | solution.py:256
  87.5 1.3 collective-permute-start.7
  88.8 7.1 %collective-permute-start.18 = (bf16[16,8,8192]{2,1,0:T(8,128)(2,1)}, bf16[16,8,8192]{2,1,0:T(8,128)(2,1)S(1)}, u32[]{:S(2)}, u32[]{:S(2)}) collective-permute-start(bf16[16,8,8192]{2,1,0:T(8,128)(2,1)} %pad_maximum_fusion.2), channel_id=1, source_target_pairs={{0,32},{1,33},{2,34},{3,35},{4,36},{5,37},{6,38},{7,39},{8,40},{9,... | collective-permute-start | bytes 6291464 | tf_op jit(solution)/shard_map/ppermute | solution.py:288
  95.9 1.6 pad_maximum_fusion.1
  97.6 8.5 %collective-permute-start.13 = (bf16[16,8,8192]{2,1,0:T(8,128)(2,1)}, bf16[16,8,8192]{2,1,0:T(8,128)(2,1)S(1)}, u32[]{:S(2)}, u32[]{:S(2)}) collective-permute-start(bf16[16,8,8192]{2,1,0:T(8,128)(2,1)} %pad_maximum_fusion.1), channel_id=1, source_target_pairs={{0,32},{1,33},{2,34},{3,35},{4,36},{5,37},{6,38},{7,39},{8,40},{9,... | collective-permute-start | bytes 6291464 | tf_op jit(solution)/shard_map/ppermute | solution.py:288
  106.0 1.6 pad_maximum_fusion
  107.7 15.9 %corr.4.refs_8_ = bf16[4096,1024]{1,0:T(8,128)(2,1)} custom-call(s32[65]{0:T(128)S(1)} %pad_add_fusion.4.refs_0_, bf16[8,16384]{1,0:T(8,128)(2,1)S(1)} %get-tuple-element.8.refs_1_, bf16[32,8192]{1,0:T(8,128)(2,1)S(1)} %get-tuple-element.16.refs_2_, bf16[32,8192]{1,0:T(8,128)(2,1)S(1)} %bitcast.36, bf16[32,8192]{1,0:T(8,128)(2,1)S(1)} %bitcast.37, ...), custom_call_target="tpu_custom_call" | custom-call | flops 15032385536 | bytes 12582912 | tf_op jit(solution)/shard_map/corr/pallas_call | solution.py:210
  123.6 1.4 copy-done.2
  125.0 1.6 copy-done.3
  126.5 15.9 %corr.5.refs_8_ = bf16[4096,1024]{1,0:T(8,128)(2,1)} custom-call(s32[65]{0:T(128)S(1)} %pad_add_fusion.3.refs_0_, bf16[8,16384]{1,0:T(8,128)(2,1)S(1)} %get-tuple-element.8.refs_1_, bf16[32,8192]{1,0:T(8,128)(2,1)S(1)} %bitcast.41, bf16[32,8192]{1,0:T(8,128)(2,1)S(1)} %bitcast.42, bf16[32,8192]{1,0:T(8,128)(2,1)S(1)} %bitcast.43, ...), custom_call_target="tpu_custom_call", output_to_operand_aliasing={{}: (8, {})} | custom-call | flops 15032385536 | bytes 12582912 | tf_op jit(solution)/shard_map/corr/pallas_call | solution.py:210
  142.4 15.9 %corr.6.refs_8_ = bf16[4096,1024]{1,0:T(8,128)(2,1)} custom-call(s32[65]{0:T(128)S(1)} %pad_add_fusion.2.refs_0_, bf16[8,16384]{1,0:T(8,128)(2,1)S(1)} %get-tuple-element.8.refs_1_, bf16[32,8192]{1,0:T(8,128)(2,1)S(1)} %bitcast.39, bf16[32,8192]{1,0:T(8,128)(2,1)S(1)} %bitcast.45, bf16[32,8192]{1,0:T(8,128)(2,1)S(1)} %bitcast.46, ...), custom_call_target="tpu_custom_call", output_to_operand_aliasing={{}: (8, {})} | custom-call | flops 15032385536 | bytes 12582912 | tf_op jit(solution)/shard_map/corr/pallas_call | solution.py:210
  158.4 15.9 %corr.7 = bf16[4096,1024]{1,0:T(8,128)(2,1)} custom-call(s32[65]{0:T(128)S(1)} %pad_add_fusion.refs_0_, bf16[8,16384]{1,0:T(8,128)(2,1)S(1)} %get-tuple-element.8.refs_1_, bf16[32,8192]{1,0:T(8,128)(2,1)S(1)} %bitcast.40, bf16[32,8192]{1,0:T(8,128)(2,1)S(1)} %bitcast.47, bf16[32,8192]{1,0:T(8,128)(2,1)S(1)} %bitcast.49, ...), custom_call_target="tpu_custom_call", output_to_operand_aliasing={{}: (8, {})} | custom-call | flops 15032385536 | bytes 12582912 | tf_op jit(solution)/shard_map/corr/pallas_call | solution.py:210
  (62 shorter events, 5.7 us)
Async XLA Ops:
  0.0 1.0 copy-start
  2.6 17.1 %all-to-all-start = ((bf16[32,8,512]{2,1,0:T(8,128)(2,1)}), bf16[32,8,512]{2,1,0:T(8,128)(2,1)S(1)}, u32[]{:S(2)}, u32[]{:S(2)}) async-start(bf16[32,8,512]{2,1,0:T(8,128)(2,1)} %fusion), calls=%async_computation | async-start | bytes 524288 | tf_op jit(solution)/shard_map/all_to_all | solution.py:268
  19.7 3.4 %copy-start.1 = (bf16[2048,2048]{1,0:T(8,128)(2,1)S(1)}, bf16[2048,2048]{1,0:T(8,128)(2,1)}, u32[]{:S(2)}) copy-start(bf16[2048,2048]{1,0:T(8,128)(2,1)} %constant.155.clone.table) | copy-start | bytes 25165828
  26.2 3.2 %collective-permute-start = (bf16[8,8192]{1,0:T(8,128)(2,1)S(1)}, bf16[8,8192]{1,0:T(8,128)(2,1)S(1)}, u32[]{:S(2)}, u32[]{:S(2)}) collective-permute-start(bf16[8,8192]{1,0:T(8,128)(2,1)S(1)} %get-tuple-element.10), channel_id=1, source_target_pairs={{0,32},{1,33},{2,34},{3,35},{4,36},{5,37},{6,38},{7,39},{8,40},{9,... | collective-permute-start | bytes 393224 | tf_op jit(solution)/shard_map/ppermute | solution.py:273
  29.4 5.5 %collective-permute-start.1 = (bf16[1,8,8192]{2,1,0:T(8,128)(2,1)S(1)}, bf16[1,8,8192]{2,1,0:T(8,128)(2,1)S(1)}, u32[]{:S(2)}, u32[]{:S(2)}) collective-permute-start(bf16[1,8,8192]{2,1,0:T(8,128)(2,1)S(1)} %get-tuple-element.12), channel_id=1, source_target_pairs={{0,1},{1,2},{2,3},{3,0},{4,5},{5,6},{6,7},{7,4},{8,9},{9,10},{10,1... | collective-permute-start | bytes 393224 | tf_op jit(solution)/shard_map/ppermute | solution.py:256
  30.1 5.0 %collective-permute-start.2 = (bf16[1,8,8192]{2,1,0:T(8,128)(2,1)S(1)}, bf16[1,8,8192]{2,1,0:T(8,128)(2,1)S(1)}, u32[]{:S(2)}, u32[]{:S(2)}) collective-permute-start(bf16[1,8,8192]{2,1,0:T(8,128)(2,1)S(1)} %get-tuple-element.12), channel_id=1, source_target_pairs={{0,3},{1,0},{2,1},{3,2},{4,7},{5,4},{6,5},{7,6},{8,11},{9,8},{10,9... | collective-permute-start | bytes 393224 | tf_op jit(solution)/shard_map/ppermute | solution.py:256
  32.3 5.6 %collective-permute-start.3 = (bf16[1,8,8192]{2,1,0:T(8,128)(2,1)S(1)}, bf16[1,8,8192]{2,1,0:T(8,128)(2,1)S(1)}, u32[]{:S(2)}, u32[]{:S(2)}) collective-permute-start(bf16[1,8,8192]{2,1,0:T(8,128)(2,1)S(1)} %get-tuple-element.12), channel_id=1, source_target_pairs={{0,2},{1,3},{2,0},{3,1},{4,6},{5,7},{6,4},{7,5},{8,10},{9,11},{10,... | collective-permute-start | bytes 393224 | tf_op jit(solution)/shard_map/ppermute | solution.py:256
  38.0 15.2 %collective-permute-start.19 = (bf16[4,8,8192]{2,1,0:T(8,128)(2,1)S(1)}, bf16[4,8,8192]{2,1,0:T(8,128)(2,1)S(1)}, u32[]{:S(2)}, u32[]{:S(2)}) collective-permute-start(bf16[4,8,8192]{2,1,0:T(8,128)(2,1)S(1)} %get-tuple-element.17), channel_id=1, source_target_pairs={{0,16},{1,17},{2,18},{3,19},{4,20},{5,21},{6,22},{7,23},{8,24},{9,... | collective-permute-start | bytes 1572872 | tf_op jit(solution)/shard_map/ppermute | solution.py:256
  38.1 16.4 %collective-permute-start.20 = (bf16[4,8,8192]{2,1,0:T(8,128)(2,1)S(1)}, bf16[4,8,8192]{2,1,0:T(8,128)(2,1)S(1)}, u32[]{:S(2)}, u32[]{:S(2)}) collective-permute-start(bf16[4,8,8192]{2,1,0:T(8,128)(2,1)S(1)} %get-tuple-element.17), channel_id=1, source_target_pairs={{0,80},{1,81},{2,82},{3,83},{4,84},{5,85},{6,86},{7,87},{8,88},{9,... | collective-permute-start | bytes 1572872 | tf_op jit(solution)/shard_map/ppermute | solution.py:256
  40.8 16.5 %collective-permute-start.21 = (bf16[4,8,8192]{2,1,0:T(8,128)(2,1)S(1)}, bf16[4,8,8192]{2,1,0:T(8,128)(2,1)S(1)}, u32[]{:S(2)}, u32[]{:S(2)}) collective-permute-start(bf16[4,8,8192]{2,1,0:T(8,128)(2,1)S(1)} %get-tuple-element.17), channel_id=1, source_target_pairs={{0,64},{1,65},{2,66},{3,67},{4,68},{5,69},{6,70},{7,71},{8,72},{9,... | collective-permute-start | bytes 1572872 | tf_op jit(solution)/shard_map/ppermute | solution.py:256
  40.8 13.7 %collective-permute-start.14 = (bf16[4,8,8192]{2,1,0:T(8,128)(2,1)S(1)}, bf16[4,8,8192]{2,1,0:T(8,128)(2,1)S(1)}, u32[]{:S(2)}, u32[]{:S(2)}) collective-permute-start(bf16[4,8,8192]{2,1,0:T(8,128)(2,1)S(1)} %get-tuple-element.17), channel_id=1, source_target_pairs={{0,4},{1,5},{2,6},{3,7},{4,8},{5,9},{6,10},{7,11},{8,12},{9,13},{1... | collective-permute-start | bytes 1572872 | tf_op jit(solution)/shard_map/ppermute | solution.py:256
  41.1 17.5 %collective-permute-start.9 = (bf16[4,8,8192]{2,1,0:T(8,128)(2,1)S(1)}, bf16[4,8,8192]{2,1,0:T(8,128)(2,1)S(1)}, u32[]{:S(2)}, u32[]{:S(2)}) collective-permute-start(bf16[4,8,8192]{2,1,0:T(8,128)(2,1)S(1)} %get-tuple-element.17), channel_id=1, source_target_pairs={{0,12},{1,13},{2,14},{3,15},{4,0},{5,1},{6,2},{7,3},{8,4},{9,5},{1... | collective-permute-start | bytes 1572872 | tf_op jit(solution)/shard_map/ppermute | solution.py:256
  53.2 19.1 %collective-permute-start.4 = (bf16[4,8,8192]{2,1,0:T(8,128)(2,1)S(1)}, bf16[4,8,8192]{2,1,0:T(8,128)(2,1)S(1)}, u32[]{:S(2)}, u32[]{:S(2)}) collective-permute-start(bf16[4,8,8192]{2,1,0:T(8,128)(2,1)S(1)} %get-tuple-element.17), channel_id=1, source_target_pairs={{0,8},{1,9},{2,10},{3,11},{4,12},{5,13},{6,14},{7,15},{8,0},{9,1},... | collective-permute-start | bytes 1572872 | tf_op jit(solution)/shard_map/ppermute | solution.py:256
  54.4 18.3 %collective-permute-start.15 = (bf16[4,8,8192]{2,1,0:T(8,128)(2,1)S(1)}, bf16[4,8,8192]{2,1,0:T(8,128)(2,1)S(1)}, u32[]{:S(2)}, u32[]{:S(2)}) collective-permute-start(bf16[4,8,8192]{2,1,0:T(8,128)(2,1)S(1)} %collective-permute-done.14), channel_id=1, source_target_pairs={{0,16},{1,17},{2,18},{3,19},{4,20},{5,21},{6,22},{7,23},{8,24},{9,... | collective-permute-start | bytes 1572872 | tf_op jit(solution)/shard_map/ppermute | solution.py:256
  54.5 20.5 %collective-permute-start.16 = (bf16[4,8,8192]{2,1,0:T(8,128)(2,1)S(1)}, bf16[4,8,8192]{2,1,0:T(8,128)(2,1)S(1)}, u32[]{:S(2)}, u32[]{:S(2)}) collective-permute-start(bf16[4,8,8192]{2,1,0:T(8,128)(2,1)S(1)} %collective-permute-done.14), channel_id=1, source_target_pairs={{0,80},{1,81},{2,82},{3,83},{4,84},{5,85},{6,86},{7,87},{8,88},{9,... | collective-permute-start | bytes 1572872 | tf_op jit(solution)/shard_map/ppermute | solution.py:256
  57.3 19.0 %collective-permute-start.17 = (bf16[4,8,8192]{2,1,0:T(8,128)(2,1)S(1)}, bf16[4,8,8192]{2,1,0:T(8,128)(2,1)S(1)}, u32[]{:S(2)}, u32[]{:S(2)}) collective-permute-start(bf16[4,8,8192]{2,1,0:T(8,128)(2,1)S(1)} %collective-permute-done.14), channel_id=1, source_target_pairs={{0,64},{1,65},{2,66},{3,67},{4,68},{5,69},{6,70},{7,71},{8,72},{9,... | collective-permute-start | bytes 1572872 | tf_op jit(solution)/shard_map/ppermute | solution.py:256
  58.6 49.1 %collective-permute-start.22 = (bf16[16,8,8192]{2,1,0:T(8,128)(2,1)S(1)}, bf16[16,8,8192]{2,1,0:T(8,128)(2,1)S(1)}, u32[]{:S(2)}, u32[]{:S(2)}) collective-permute-start(bf16[16,8,8192]{2,1,0:T(8,128)(2,1)S(1)} %constant_dynamic-update-slice_fusion), channel_id=1, source_target_pairs={{0,32},{1,33},{2,34},{3,35},{4,36},{5,37},{6,38},{7,39},{8,40},{9,... | collective-permute-start | bytes 6291464 | tf_op jit(solution)/shard_map/ppermute | solution.py:288
  72.3 15.2 %collective-permute-start.10 = (bf16[4,8,8192]{2,1,0:T(8,128)(2,1)S(1)}, bf16[4,8,8192]{2,1,0:T(8,128)(2,1)S(1)}, u32[]{:S(2)}, u32[]{:S(2)}) collective-permute-start(bf16[4,8,8192]{2,1,0:T(8,128)(2,1)S(1)} %collective-permute-done.9), channel_id=1, source_target_pairs={{0,16},{1,17},{2,18},{3,19},{4,20},{5,21},{6,22},{7,23},{8,24},{9,... | collective-permute-start | bytes 1572872 | tf_op jit(solution)/shard_map/ppermute | solution.py:256
  72.7 14.8 %collective-permute-start.11 = (bf16[4,8,8192]{2,1,0:T(8,128)(2,1)S(1)}, bf16[4,8,8192]{2,1,0:T(8,128)(2,1)S(1)}, u32[]{:S(2)}, u32[]{:S(2)}) collective-permute-start(bf16[4,8,8192]{2,1,0:T(8,128)(2,1)S(1)} %collective-permute-done.9), channel_id=1, source_target_pairs={{0,80},{1,81},{2,82},{3,83},{4,84},{5,85},{6,86},{7,87},{8,88},{9,... | collective-permute-start | bytes 1572872 | tf_op jit(solution)/shard_map/ppermute | solution.py:256
  75.0 13.8 %collective-permute-start.12 = (bf16[4,8,8192]{2,1,0:T(8,128)(2,1)S(1)}, bf16[4,8,8192]{2,1,0:T(8,128)(2,1)S(1)}, u32[]{:S(2)}, u32[]{:S(2)}) collective-permute-start(bf16[4,8,8192]{2,1,0:T(8,128)(2,1)S(1)} %collective-permute-done.9), channel_id=1, source_target_pairs={{0,64},{1,65},{2,66},{3,67},{4,68},{5,69},{6,70},{7,71},{8,72},{9,... | collective-permute-start | bytes 1572872 | tf_op jit(solution)/shard_map/ppermute | solution.py:256
  76.3 21.2 %collective-permute-start.5 = (bf16[4,8,8192]{2,1,0:T(8,128)(2,1)S(1)}, bf16[4,8,8192]{2,1,0:T(8,128)(2,1)S(1)}, u32[]{:S(2)}, u32[]{:S(2)}) collective-permute-start(bf16[4,8,8192]{2,1,0:T(8,128)(2,1)S(1)} %collective-permute-done.4), channel_id=1, source_target_pairs={{0,16},{1,17},{2,18},{3,19},{4,20},{5,21},{6,22},{7,23},{8,24},{9,... | collective-permute-start | bytes 1572872 | tf_op jit(solution)/shard_map/ppermute | solution.py:256
  87.5 18.6 %collective-permute-start.6 = (bf16[4,8,8192]{2,1,0:T(8,128)(2,1)S(1)}, bf16[4,8,8192]{2,1,0:T(8,128)(2,1)S(1)}, u32[]{:S(2)}, u32[]{:S(2)}) collective-permute-start(bf16[4,8,8192]{2,1,0:T(8,128)(2,1)S(1)} %collective-permute-done.4), channel_id=1, source_target_pairs={{0,80},{1,81},{2,82},{3,83},{4,84},{5,85},{6,86},{7,87},{8,88},{9,... | collective-permute-start | bytes 1572872 | tf_op jit(solution)/shard_map/ppermute | solution.py:256
  87.5 18.6 %collective-permute-start.7 = (bf16[4,8,8192]{2,1,0:T(8,128)(2,1)S(1)}, bf16[4,8,8192]{2,1,0:T(8,128)(2,1)S(1)}, u32[]{:S(2)}, u32[]{:S(2)}) collective-permute-start(bf16[4,8,8192]{2,1,0:T(8,128)(2,1)S(1)} %collective-permute-done.4), channel_id=1, source_target_pairs={{0,64},{1,65},{2,66},{3,67},{4,68},{5,69},{6,70},{7,71},{8,72},{9,... | collective-permute-start | bytes 1572872 | tf_op jit(solution)/shard_map/ppermute | solution.py:256
  88.8 34.8 %collective-permute-start.18 = (bf16[16,8,8192]{2,1,0:T(8,128)(2,1)}, bf16[16,8,8192]{2,1,0:T(8,128)(2,1)S(1)}, u32[]{:S(2)}, u32[]{:S(2)}) collective-permute-start(bf16[16,8,8192]{2,1,0:T(8,128)(2,1)} %pad_maximum_fusion.2), channel_id=1, source_target_pairs={{0,32},{1,33},{2,34},{3,35},{4,36},{5,37},{6,38},{7,39},{8,40},{9,... | collective-permute-start | bytes 6291464 | tf_op jit(solution)/shard_map/ppermute | solution.py:288
  97.5 10.1 %copy-start.4 = (bf16[2048,1024]{1,0:T(8,128)(2,1)S(1)}, bf16[2048,1024]{1,0:T(8,128)(2,1)}, u32[]{:S(2)}) copy-start(bf16[2048,1024]{1,0:T(8,128)(2,1)} %constant.156.clone.refs_7_) | copy-start | bytes 12582916
  97.6 44.9 %collective-permute-start.13 = (bf16[16,8,8192]{2,1,0:T(8,128)(2,1)}, bf16[16,8,8192]{2,1,0:T(8,128)(2,1)S(1)}, u32[]{:S(2)}, u32[]{:S(2)}) collective-permute-start(bf16[16,8,8192]{2,1,0:T(8,128)(2,1)} %pad_maximum_fusion.1), channel_id=1, source_target_pairs={{0,32},{1,33},{2,34},{3,35},{4,36},{5,37},{6,38},{7,39},{8,40},{9,... | collective-permute-start | bytes 6291464 | tf_op jit(solution)/shard_map/ppermute | solution.py:288
  107.7 50.7 %collective-permute-start.8 = (bf16[16,8,8192]{2,1,0:T(8,128)(2,1)}, bf16[16,8,8192]{2,1,0:T(8,128)(2,1)S(1)}, u32[]{:S(2)}, u32[]{:S(2)}) collective-permute-start(bf16[16,8,8192]{2,1,0:T(8,128)(2,1)} %pad_maximum_fusion), channel_id=1, source_target_pairs={{0,32},{1,33},{2,34},{3,35},{4,36},{5,37},{6,38},{7,39},{8,40},{9,... | collective-permute-start | bytes 6291464 | tf_op jit(solution)/shard_map/ppermute | solution.py:288
  123.6 1.4 copy-start.2
  125.0 1.6 copy-start.3

commit v2 on v1

--- a/solution.py
+++ b/solution.py
@@ -20,6 +20,9 @@
 NBLK = BINS // KIN
 WIDE = NBLK * BLK
 HALF = WIDE // 2
+GROUP = 8 * BLK
+NB = 1
+CB = 8 // NB
 AXES = ("grp", "dev")
 MIB = 1 << 20
 FACTOR = 2.0 / math.sqrt(SEGS * BINS)
@@ -51,9 +54,16 @@
     return vs
 
 
-def front_kernel(meta, rec, table, white, keep, send, spec, scr):
+def front_kernel(meta, rec, table_hbm, white, keep, send, spec, scr, table, sems):
+    def load(q):
+        rows = pl.ds(q * 512, 512)
+        return pltpu.make_async_copy(table_hbm.at[rows], table.at[rows], sems.at[q])
+
+    for q in range(4):
+        load(q).start()
     total = None
     for q in range(4):
+        load(q).wait()
         x = rec[:, q].astype(jnp.float32).reshape(SEGS * CH_DEV, 512).astype(jnp.bfloat16)
         part = jnp.dot(x, table[q * 512 : (q + 1) * 512, :], preferred_element_type=jnp.float32)
         total = part if total is None else total + part
@@ -98,21 +108,34 @@
             jax.ShapeDtypeStruct((CH_DEV, HALF), jnp.bfloat16),
             jax.ShapeDtypeStruct((CH_DEV, HALF), jnp.bfloat16),
         ),
-        in_specs=[pl.BlockSpec(memory_space=pltpu.SMEM), vmem, vmem],
+        in_specs=[pl.BlockSpec(memory_space=pltpu.SMEM), vmem, pl.BlockSpec(memory_space=pltpu.MemorySpace.HBM)],
         out_specs=(vmem, vmem, vmem),
         scratch_shapes=[
             pltpu.VMEM((SEGS * CH_DEV, 2 * BINS), jnp.float32),
             pltpu.VMEM((CH_DEV, WIDE), jnp.float32),
+            pltpu.VMEM((W, 2 * BINS), jnp.bfloat16),
+            pltpu.SemaphoreType.DMA((4,)),
         ],
-        compiler_params=pltpu.CompilerParams(vmem_limit_bytes=32 * MIB),
+        compiler_params=pltpu.CompilerParams(vmem_limit_bytes=60 * MIB),
         name="front",
     )(meta, rec, table)
 
 
-def corr_kernel(
-    first, meta, b_ref, m0, m1, m2, m3, sib, e_hbm, *rest
-):
-    out, rows_scr, x_scr, e_scr, ov, yf, yb, sems = rest if first else rest[1:]
+def corr_kernel(first, meta, b_ref, *refs):
+    mine, sib, e_hbm = refs[:4], refs[4:8], refs[8]
+    out, rows_scr, a_scr, x_scr, e_scr, ov, yf, yb, a_sems, sems = refs[9 if first else 10 :]
+
+    def load(j, half, n):
+        return pltpu.make_async_copy(
+            (mine, sib)[half][n].at[:, pl.ds(pl.multiple_of(j * GROUP, GROUP), GROUP)],
+            a_scr.at[half, j, pl.ds(n * 32, 32)],
+            a_sems.at[half, j],
+        )
+
+    for j in range(4):
+        for half in range(2):
+            for n in range(4):
+                load(j, half, n).start()
     e_copy = pltpu.make_async_copy(e_hbm, e_scr, sems.at[0])
     e_copy.start()
     core = meta[0]
@@ -121,70 +144,63 @@
     turned = jnp.where(
         (lane & 16) == 0, -pltpu.roll(own, WIDE - 16, 1), pltpu.roll(own, 16, 1)
     )
-    rows_scr[0:8, :] = own
-    rows_scr[8:16, :] = turned
+    for p in range(NB):
+        rows_scr[p, 0:CB, :] = own[CB * p : CB * p + CB]
+        rows_scr[p, CB : 2 * CB, :] = turned[CB * p : CB * p + CB]
     diag = lax.broadcasted_iota(jnp.int32, (KIN, BLK), 0) == (
         lax.broadcasted_iota(jnp.int32, (KIN, BLK), 1) & 15
     )
 
-    def group(j, mine):
-        half = core if mine else 1 - core
-        g = half * 4 + j
+    def group(p, j, half):
+        g = (core if half == 0 else 1 - core) * 4 + j
         for i in range(8):
-            lanes = pl.ds(pl.multiple_of((j * 8 + i) * BLK, BLK), BLK)
-            if mine:
-                a = jnp.concatenate([m[:, lanes] for m in (m0, m1, m2, m3)], axis=0)
-            else:
-                a = sib[:, lanes]
-            r = rows_scr[:, pl.ds(pl.multiple_of((g * 8 + i) * BLK, BLK), BLK)]
+            a = a_scr[half, j, :, i * BLK : i * BLK + BLK]
+            if half == 1:
+                a = jnp.concatenate(
+                    [a[32 * n + 8 * o : 32 * n + 8 * o + 8] for o in range(4) for n in range(4)], axis=0
+                )
+            r = rows_scr[p, :, pl.ds(pl.multiple_of((g * 8 + i) * BLK, BLK), BLK)]
             block = jnp.where(diag[None], r[:, None, :], 0.0).astype(jnp.bfloat16)
-            block = block.reshape(2 * CH_DEV * KIN, BLK)
             prod = lax.dot_general(
-                a, block, (((1,), (1,)), ((), ())), preferred_element_type=jnp.float32
+                block.reshape(2 * CB * KIN, BLK), a, (((1,), (1,)), ((), ())), preferred_element_type=jnp.float32
             )
-            ov[i] = prod * FACTOR
+            prod = (prod * FACTOR).astype(jnp.bfloat16)
+            ov[half, :, i * KIN : (i + 1) * KIN, :] = prod.reshape(2 * CB, KIN, 128)
         for ri in range(2):
             at = pl.ds(pl.multiple_of(ri * BINS + g * 128, 128), 128)
-            for rb in range(8):
-                if mine:
-                    vs = [ov[i, rb * 16 : rb * 16 + 16, ri * 128 : ri * 128 + 128] for i in range(8)]
-                else:
-                    n0, n1 = 2 * rb, 2 * rb + 1
-                    s0 = ((n0 % 4) * 4 + n0 // 4) * 8
-                    s1 = ((n1 % 4) * 4 + n1 // 4) * 8
-                    vs = [
-                        jnp.concatenate(
-                            [
-                                ov[i, s0 : s0 + 8, ri * 128 : ri * 128 + 128],
-                                ov[i, s1 : s1 + 8, ri * 128 : ri * 128 + 128],
-                            ],
-                            axis=0,
-                        )
-                        for i in range(8)
-                    ]
-                for c, w in enumerate(chunk_transpose(vs)):
-                    x_scr[c * 128 + rb * 16 : c * 128 + rb * 16 + 16, at] = w.astype(jnp.bfloat16)
-
-    @pl.loop(0, 4)
-    def _(j):
-        group(j, True)
-
-    @pl.loop(0, 4)
-    def _(j):
-        group(j, False)
-
-    e_copy.wait()
-
-    @pl.loop(0, 4)
-    def _(n):
-        lanes = pl.ds(pl.multiple_of(n * 256, 256), 256)
-        y = jnp.dot(x_scr[...], e_scr[:, lanes], preferred_element_type=jnp.float32)
-        for c in range(CH_DEV):
+            for c in range(CB):
+                x_scr[p % 2, c * 128 : c * 128 + 128, at] = ov[half, ri * CB + c].T
+
+    def lags(p, n):
+        y = jnp.dot(
+            x_scr[p % 2],
+            e_scr[:, pl.ds(pl.multiple_of(n * 256, 256), 256)],
+            preferred_element_type=jnp.float32,
+        )
+        for c in range(CB):
             for h in range(2):
-                yf[h, pl.ds(c, 128, stride=8), :] = y[c * 128 : c * 128 + 128, h * 128 : h * 128 + 128]
-        for h in range(2):
-            lanes = pl.ds(pl.multiple_of(n * 256 + h * 128, 128), 128)
-            yb[:, lanes] = yf[h].astype(jnp.bfloat16)
+                yf[2 * n + h, pl.ds(CB * p + c, 128, stride=8), :] = y[c * 128 : c * 128 + 128, h * 128 : h * 128 + 128]
+
+    for p in range(NB + 1):
+
+        @pl.loop(0, 4)
+        def _(j):
+            if p == 0:
+                for half in range(2):
+                    for n in range(4):
+                        load(j, half, n).wait()
+            if p > 0:
+                lags(p - 1, j)
+            if p < NB:
+                group(p, j, 0)
+                group(p, j, 1)
+            if p == NB:
+                for h in range(2):
+                    lanes = pl.ds(pl.multiple_of(j * 256 + h * 128, 128), 128)
+                    yb[:, lanes] = yf[2 * j + h].astype(jnp.bfloat16)
+
+        if p == 0:
+            e_copy.wait()
 
     def copy(n):
         return pltpu.make_async_copy(
@@ -205,24 +221,26 @@
 def corr(meta, white, mine, sib, inverse, out):
     first = out is None
     vmem = pl.BlockSpec(memory_space=pltpu.VMEM)
-    anym = pl.BlockSpec(memory_space=pl.ANY)
-    args = [meta, white, *mine, sib, inverse] + ([] if first else [out])
+    hbm = pl.BlockSpec(memory_space=pltpu.MemorySpace.HBM)
+    args = [meta, white, *mine, *sib, inverse] + ([] if first else [out])
     return pl.pallas_call(
         lambda *refs: corr_kernel(first, *refs),
         out_shape=jax.ShapeDtypeStruct((STEPS * 256 * CH_DEV, NLAG), jnp.bfloat16),
-        in_specs=[pl.BlockSpec(memory_space=pltpu.SMEM)] + [vmem] * 6 + [anym] * (len(args) - 7),
-        out_specs=anym,
+        in_specs=[pl.BlockSpec(memory_space=pltpu.SMEM), vmem] + [hbm] * (len(args) - 2),
+        out_specs=hbm,
         scratch_shapes=[
-            pltpu.VMEM((16, WIDE), jnp.float32),
-            pltpu.VMEM((1024, 2 * BINS), jnp.bfloat16),
+            pltpu.VMEM((NB, 2 * CB, WIDE), jnp.float32),
+            pltpu.VMEM((2, 4, 128, GROUP), jnp.bfloat16),
+            pltpu.VMEM((min(NB, 2), CB * 128, 2 * BINS), jnp.bfloat16),
             pltpu.VMEM((2 * BINS, NLAG), jnp.bfloat16),
-            pltpu.VMEM((8, 128, 256), jnp.float32),
-            pltpu.VMEM((2, 1024, 128), jnp.float32),
+            pltpu.VMEM((2, 2 * CB, 128, 128), jnp.bfloat16),
+            pltpu.VMEM((8, 1024, 128), jnp.float32),
             pltpu.VMEM((1024, NLAG), jnp.bfloat16),
+            pltpu.SemaphoreType.DMA((2, 4)),
             pltpu.SemaphoreType.DMA((2,)),
         ],
-        input_output_aliases={} if first else {8: 0},
-        compiler_params=pltpu.CompilerParams(vmem_limit_bytes=40 * MIB),
+        input_output_aliases={} if first else {11: 0},
+        compiler_params=pltpu.CompilerParams(vmem_limit_bytes=60 * MIB),
         cost_estimate=pl.CostEstimate(
             flops=7 * 1024 * 2048 * 1024, bytes_accessed=12 * MIB, transcendentals=0
         ),
@@ -273,20 +291,35 @@
     block = keep + lax.ppermute(send, AXES, CORE_PAIRS)
 
     near = jnp.concatenate(line(block[None], "xz"), axis=0)
-    lines = line(near, "yy")
+    mine = line(near, "zx")
+    ahead, behind = (lax.ppermute(near, AXES, line_pairs("yy", s)) for s in (1, -1))
     off = jnp.array(OFFSETS, jnp.int32)
     outer, inner = jnp.meshgrid(off, off, indexing="ij")
     xs = (x0 + jnp.where(core == 0, inner, outer)) % 4
     zs = (z0 + jnp.where(core == 0, outer, inner)) % 4
     out = None
+    after = lax.optimization_barrier
     for k in range(4):
         ys = (y0 + OFFSETS[k]) % 4
         chip = (zs // 2) * 64 + (zs % 2) * 16 + ys * 4 + xs
         place = chip.reshape(16, 1, 1) + jnp.arange(2)[None, :, None] * 32 + jnp.arange(2)[None, None, :] * 128
         meta = jnp.concatenate([core[None], place.reshape(64)]).astype(jnp.int32)
-        mine = line(lines[k], "zx")
-        sib = lax.ppermute(jnp.concatenate(mine, axis=0), AXES, CORE_PAIRS)
-        out = corr(meta, white, [m.reshape(32, HALF) for m in mine], sib.reshape(128, HALF), inverse, out)
+        now = mine
+        if k > 0:
+            out, *now = after((out, *now))
+        sib = [lax.ppermute(m, AXES, CORE_PAIRS) for m in now]
+        if k == 0:
+            near, ahead, *now = after((near, ahead, *now))
+            mine = line(ahead, "zx")
+            across = lax.ppermute(near, AXES, line_pairs("yy", 2))
+        elif k == 1:
+            behind, *now = after((behind, *now))
+            mine = line(behind, "zx")
+        elif k == 2:
+            across, *now = after((across, *now))
+            mine = line(across, "zx")
+        flat = lambda ms: [m.reshape(32, HALF) for m in ms]
+        out = corr(meta, white, flat(now), flat(sib), inverse, out)
     return out.reshape(1, STEPS * 256, CH_DEV, NLAG)
 
 

time: 176 us -> 136 us (0.77)
  starting transfers between devices: 61.5 us -> 44.1 us
  Pallas kernels: 66.7 us -> 58.9 us
  waiting for transfers between devices: 28.8 us -> 22.9 us
  local copies, waits for them, and re-layouts: 8.04 us -> 2.77 us
  other arithmetic: 7.09 us -> 5.03 us
    ppermute x4 -> x19, starting transfers between devices: 29.3 us -> 17.2 us  [the longest x16 15.3 us: local(): sib = [lax.ppermute(m, AXES, CORE_PAIRS) for m in now]]
    pallas_call x4, Pallas kernels: 63.5 us -> 52.1 us  [corr(): pl.pallas_call(lambda *refs: corr_kernel(first, *refs), out_shape=jax.Sha...]
    ppermute x18 -> x15, waiting for transfers between devices: 22.7 us -> 11.7 us  [line(): lax.ppermute(block, AXES, line_pairs(axes, s))]
    ppermute x18 -> x15, starting transfers between devices: 20.8 us -> 15.5 us  [line(): lax.ppermute(block, AXES, line_pairs(axes, s))]
    unnamed x15 -> x34, local copies, waits for them, and re-layouts: 7.4 us -> 2.16 us
    concatenate x3 -> x1, other arithmetic: 4.86 us -> 0.07 us  [local(): near = jnp.concatenate(line(block[None], 'xz'), axis=0)]
    pallas_call x1, Pallas kernels: 3.14 us -> 6.76 us  [front(): pl.pallas_call(front_kernel, out_shape=(jax.ShapeDtypeStruct((CH_DEV, WID...]
    ppermute x4 -> x19, waiting for transfers between devices: 0.01 us -> 3.47 us  [the longest x16 3.46 us: local(): sib = [lax.ppermute(m, AXES, CORE_PAIRS) for m in now]]
  transfers between devices with their start and end apart: 24 -> 36, of which waited for: 7 -> 12; matrix products, arithmetic and copies ran while one was open for 4% -> 3% of each run, Pallas kernels for 27% -> 29%
where the time goes in v2:
time: 136 us
  Pallas kernels  58.9 us (43%)
  starting transfers between devices  44.1 us (32%)
  waiting for transfers between devices  22.9 us (17%)
  other arithmetic  5.03 us (4%)
  local copies, waits for them, and re-layouts  2.77 us (2%)
  matrix products  1.66 us (1%)
    pallas_call x4, Pallas kernels, corr(): pl.pallas_call(lambda *refs: corr_kernel(first, *refs), out_shape=jax.Sha...  52.1 us
    ppermute x15, starting transfers between devices, line(): lax.ppermute(block, AXES, line_pairs(axes, s))  15.5 us
    ppermute x16, starting transfers between devices, local(): sib = [lax.ppermute(m, AXES, CORE_PAIRS) for m in now]  15.3 us
    ppermute x15, waiting for transfers between devices, line(): lax.ppermute(block, AXES, line_pairs(axes, s))  11.7 us
    all_to_all x1, starting transfers between devices, local(): lax.all_to_all(ordered.reshape(32, 8, 512), 'dev', split_axis=0, concat_a...  9.23 us
    pallas_call x1, Pallas kernels, front(): pl.pallas_call(front_kernel, out_shape=(jax.ShapeDtypeStruct((CH_DEV, WID...  6.76 us
    all_to_all x1, waiting for transfers between devices, local(): lax.all_to_all(ordered.reshape(32, 8, 512), 'dev', split_axis=0, concat_a...  6.58 us
    ppermute x16, waiting for transfers between devices, local(): sib = [lax.ppermute(m, AXES, CORE_PAIRS) for m in now]  3.46 us
  transfers between devices with their start and end apart: 36, of which 12 were waited for; matrix products, arithmetic and copies ran while one was open for 3% of the time, Pallas kernels for 29%

profile of v2, /device:TPU:1, one launch (start us, length us, event | category | flops | bytes accessed | tf_op | source)
XLA Modules:
  0.0 135.8 jit_solution(8667541455200736854)
XLA Ops:
  0.0 0.9 copy-done
  1.0 1.7 %fusion = bf16[32,8,512]{2,1,0:T(8,128)(2,1)} fusion(bf16[256,512]{1,0:T(8,128)(2,1)S(1)} %copy-done, s32[256]{0:T(256)} %bitcast.47), kind=kOutput, calls=%fused_computation.1 | convolution fusion | flops 67305472 | bytes 525312 | tf_op jit(solution)/shard_map/dot_general | solution.py:285
  2.6 9.2 %all-to-all-start = ((bf16[32,8,512]{2,1,0:T(8,128)(2,1)}), bf16[32,8,512]{2,1,0:T(8,128)(2,1)S(1)}, u32[]{:S(2)}, u32[]{:S(2)}) async-start(bf16[32,8,512]{2,1,0:T(8,128)(2,1)} %fusion), calls=%async_computation | async-start | bytes 524288 | tf_op jit(solution)/shard_map/all_to_all | solution.py:286
  11.9 0.7 and_select_fusion
  13.1 6.6 %all-to-all-done = bf16[32,8,512]{2,1,0:T(8,128)(2,1)S(1)} async-done(((bf16[32,8,512]{2,1,0:T(8,128)(2,1)}), bf16[32,8,512]{2,1,0:T(8,128)(2,1)S(1)}, u32[]{:S(2)}, u32[]{:S(2)}) %all-to-all-start) | async-done | bytes 262176 | tf_op jit(solution)/shard_map/all_to_all | solution.py:286
  19.7 0.7 copy-done.1
  20.4 6.8 %front.1 = (bf16[8,16384]{1,0:T(8,128)(2,1)}, bf16[8,8192]{1,0:T(8,128)(2,1)}, bf16[8,8192]{1,0:T(8,128)(2,1)}) custom-call(s32[3]{0:T(128)} %pad_add_fusion.1.meta, bf16[8,4,8,512]{3,2,1,0:T(8,128)(2,1)} %bitcast.45, bf16[2048,2048]{1,0:T(8,128)(2,1)} %constant.155.clone.table_hbm), custom_call_target="tpu_custom_call" | custom-call | tf_op jit(solution)/shard_map/front/pallas_call | solution.py:104
  27.2 2.2 %collective-permute-start = (bf16[8,8192]{1,0:T(8,128)(2,1)}, bf16[8,8192]{1,0:T(8,128)(2,1)S(1)}, u32[]{:S(2)}, u32[]{:S(2)}) collective-permute-start(bf16[8,8192]{1,0:T(8,128)(2,1)} %get-tuple-element.41), channel_id=1, source_target_pairs={{0,32},{1,33},{2,34},{3,35},{4,36},{5,37},{6,38},{7,39},{8,40},{9,... | collective-permute-start | bytes 393224 | tf_op jit(solution)/shard_map/ppermute | solution.py:291
  29.3 1.2 collective-permute-done
  30.5 0.9 add_bitcast_fusion
  31.4 3.4 %collective-permute-start.3 = (bf16[1,8,8192]{2,1,0:T(8,128)(2,1)S(1)}, bf16[1,8,8192]{2,1,0:T(8,128)(2,1)S(1)}, u32[]{:S(2)}, u32[]{:S(2)}) collective-permute-start(bf16[1,8,8192]{2,1,0:T(8,128)(2,1)S(1)} %add_bitcast_fusion), channel_id=1, source_target_pairs={{0,2},{1,3},{2,0},{3,1},{4,6},{5,7},{6,4},{7,5},{8,10},{9,11},{10,... | collective-permute-start | bytes 393224 | tf_op jit(solution)/shard_map/ppermute | solution.py:274
  34.8 1.5 %collective-permute-start.1 = (bf16[1,8,8192]{2,1,0:T(8,128)(2,1)S(1)}, bf16[1,8,8192]{2,1,0:T(8,128)(2,1)S(1)}, u32[]{:S(2)}, u32[]{:S(2)}) collective-permute-start(bf16[1,8,8192]{2,1,0:T(8,128)(2,1)S(1)} %add_bitcast_fusion), channel_id=1, source_target_pairs={{0,1},{1,2},{2,3},{3,0},{4,5},{5,6},{6,7},{7,4},{8,9},{9,10},{10,1... | collective-permute-start | bytes 393224 | tf_op jit(solution)/shard_map/ppermute | solution.py:274
  36.5 0.9 collective-permute-done.3
  37.5 1.2 collective-permute-done.2
  38.6 1.5 %collective-permute-done.1 = bf16[1,8,8192]{2,1,0:T(8,128)(2,1)S(1)} collective-permute-done((bf16[1,8,8192]{2,1,0:T(8,128)(2,1)S(1)}, bf16[1,8,8192]{2,1,0:T(8,128)(2,1)S(1)}, u32[]{:S(2)}, u32[]{:S(2)}) %collective-permute-start.1) | collective-permute-done | bytes 131104 | tf_op jit(solution)/shard_map/ppermute | solution.py:274
  40.3 2.7 %collective-permute-start.6 = (bf16[4,8,8192]{2,1,0:T(8,128)(2,1)S(1)}, bf16[4,8,8192]{2,1,0:T(8,128)(2,1)S(1)}, u32[]{:S(2)}, u32[]{:S(2)}) collective-permute-start(bf16[4,8,8192]{2,1,0:T(8,128)(2,1)S(1)} %pad_maximum_fusion), channel_id=1, source_target_pairs={{0,80},{1,81},{2,82},{3,83},{4,84},{5,85},{6,86},{7,87},{8,88},{9,... | collective-permute-start | bytes 1572872 | tf_op jit(solution)/shard_map/ppermute | solution.py:274
  43.3 4.1 %collective-permute-start.10 = (bf16[4,8,8192]{2,1,0:T(8,128)(2,1)S(1)}, bf16[4,8,8192]{2,1,0:T(8,128)(2,1)}, u32[]{:S(2)}, u32[]{:S(2)}) collective-permute-start(bf16[4,8,8192]{2,1,0:T(8,128)(2,1)S(1)} %pad_maximum_fusion), channel_id=1, source_target_pairs={{0,32},{1,33},{2,34},{3,35},{4,36},{5,37},{6,38},{7,39},{8,40},{9,... | collective-permute-start | bytes 1572872 | tf_op jit(solution)/shard_map/ppermute | solution.py:310
  47.4 8.0 %collective-permute-done.5 = bf16[4,8,8192]{2,1,0:T(8,128)(2,1)S(1)} collective-permute-done((bf16[4,8,8192]{2,1,0:T(8,128)(2,1)S(1)}, bf16[4,8,8192]{2,1,0:T(8,128)(2,1)S(1)}, u32[]{:S(2)}, u32[]{:S(2)}) %collective-permute-start.5) | collective-permute-done | bytes 524320 | tf_op jit(solution)/shard_map/ppermute | solution.py:274
  56.0 2.6 %collective-permute-start.13 = (bf16[4,8,8192]{2,1,0:T(8,128)(2,1)S(1)}, bf16[4,8,8192]{2,1,0:T(8,128)(2,1)}, u32[]{:S(2)}, u32[]{:S(2)}) collective-permute-start(bf16[4,8,8192]{2,1,0:T(8,128)(2,1)S(1)} %collective-permute-done.7), channel_id=1, source_target_pairs={{0,32},{1,33},{2,34},{3,35},{4,36},{5,37},{6,38},{7,39},{8,40},{9,... | collective-permute-start | bytes 1572872 | tf_op jit(solution)/shard_map/ppermute | solution.py:310
  58.9 0.7 pad_add_fusion.4.refs_0_
  60.1 2.7 %collective-permute-start.15 = (bf16[4,8,8192]{2,1,0:T(8,128)(2,1)S(1)}, bf16[4,8,8192]{2,1,0:T(8,128)(2,1)}, u32[]{:S(2)}, u32[]{:S(2)}) collective-permute-start(bf16[4,8,8192]{2,1,0:T(8,128)(2,1)S(1)} %collective-permute-done.4), channel_id=1, source_target_pairs={{0,80},{1,81},{2,82},{3,83},{4,84},{5,85},{6,86},{7,87},{8,88},{9,... | collective-permute-start | bytes 1572872 | tf_op jit(solution)/shard_map/ppermute | solution.py:274
  62.9 13.0 %corr.4.refs_11_ = bf16[4096,1024]{1,0:T(8,128)(2,1)} custom-call(s32[65]{0:T(128)} %pad_add_fusion.4.refs_0_, bf16[8,16384]{1,0:T(8,128)(2,1)} %get-tuple-element.39.refs_1_, bf16[32,8192]{1,0:T(8,128)(2,1)} %bitcast.46, bf16[32,8192]{1,0:T(8,128)(2,1)} %bitcast.51, bf16[32,8192]{1,0:T(8,128)(2,1)} %bitcast.52, bf16[32,8192]{1,0:T(8,128)(2,1)} %bitcast.53, ...), custom_call_target="tpu_custom_call" | custom-call | flops 15032385536 | bytes 12582912 | tf_op jit(solution)/shard_map/corr/pallas_call | solution.py:226
  75.9 2.1 %collective-permute-start.17 = (bf16[4,8,8192]{2,1,0:T(8,128)(2,1)S(1)}, bf16[4,8,8192]{2,1,0:T(8,128)(2,1)S(1)}, u32[]{:S(2)}, u32[]{:S(2)}) collective-permute-start(bf16[4,8,8192]{2,1,0:T(8,128)(2,1)S(1)} %collective-permute-done.4), channel_id=1, source_target_pairs={{0,32},{1,33},{2,34},{3,35},{4,36},{5,37},{6,38},{7,39},{8,40},{9,... | collective-permute-start | bytes 1572872 | tf_op jit(solution)/shard_map/ppermute | solution.py:310
  79.4 1.0 collective-permute-start.8
  80.7 2.4 %collective-permute-start.22 = (bf16[4,8,8192]{2,1,0:T(8,128)(2,1)S(1)}, bf16[4,8,8192]{2,1,0:T(8,128)(2,1)S(1)}, u32[]{:S(2)}, u32[]{:S(2)}) collective-permute-start(bf16[4,8,8192]{2,1,0:T(8,128)(2,1)S(1)} %collective-permute-done.9), channel_id=1, source_target_pairs={{0,80},{1,81},{2,82},{3,83},{4,84},{5,85},{6,86},{7,87},{8,88},{9,... | collective-permute-start | bytes 1572872 | tf_op jit(solution)/shard_map/ppermute | solution.py:274
  83.5 13.0 %corr.5.refs_11_ = bf16[4096,1024]{1,0:T(8,128)(2,1)} custom-call(s32[65]{0:T(128)} %pad_add_fusion.3.refs_0_, bf16[8,16384]{1,0:T(8,128)(2,1)} %get-tuple-element.39.refs_1_, bf16[32,8192]{1,0:T(8,128)(2,1)} %bitcast.49, bf16[32,8192]{1,0:T(8,128)(2,1)} %bitcast.15.refs_3_, bf16[32,8192]{1,0:T(8,128)(2,1)} %bitcast.16.refs_4_, ...), custom_call_target="tpu_custom_call", output_to_operand_aliasing={{}: (11, {})} | custom-call | flops 15032385536 | bytes 12582912 | tf_op jit(solution)/shard_map/corr/pallas_call | solution.py:226
  96.6 2.4 %collective-permute-start.24 = (bf16[4,8,8192]{2,1,0:T(8,128)(2,1)S(1)}, bf16[4,8,8192]{2,1,0:T(8,128)(2,1)}, u32[]{:S(2)}, u32[]{:S(2)}) collective-permute-start(bf16[4,8,8192]{2,1,0:T(8,128)(2,1)S(1)} %collective-permute-done.9), channel_id=1, source_target_pairs={{0,32},{1,33},{2,34},{3,35},{4,36},{5,37},{6,38},{7,39},{8,40},{9,... | collective-permute-start | bytes 1572872 | tf_op jit(solution)/shard_map/ppermute | solution.py:310
  100.7 2.3 %collective-permute-start.29 = (bf16[4,8,8192]{2,1,0:T(8,128)(2,1)S(1)}, bf16[4,8,8192]{2,1,0:T(8,128)(2,1)S(1)}, u32[]{:S(2)}, u32[]{:S(2)}) collective-permute-start(bf16[4,8,8192]{2,1,0:T(8,128)(2,1)S(1)} %collective-permute-done.8), channel_id=1, source_target_pairs={{0,80},{1,81},{2,82},{3,83},{4,84},{5,85},{6,86},{7,87},{8,88},{9,... | collective-permute-start | bytes 1572872 | tf_op jit(solution)/shard_map/ppermute | solution.py:274
  103.1 13.1 %corr.6.refs_11_ = bf16[4096,1024]{1,0:T(8,128)(2,1)} custom-call(s32[65]{0:T(128)} %pad_add_fusion.2.refs_0_, bf16[8,16384]{1,0:T(8,128)(2,1)} %get-tuple-element.39.refs_1_, bf16[32,8192]{1,0:T(8,128)(2,1)} %bitcast.48, bf16[32,8192]{1,0:T(8,128)(2,1)} %bitcast.54, bf16[32,8192]{1,0:T(8,128)(2,1)} %bitcast.55, ...), custom_call_target="tpu_custom_call", output_to_operand_aliasing={{}: (11, {})} | custom-call | flops 15032385536 | bytes 12582912 | tf_op jit(solution)/shard_map/corr/pallas_call | solution.py:226
  116.3 1.8 %collective-permute-start.31 = (bf16[4,8,8192]{2,1,0:T(8,128)(2,1)S(1)}, bf16[4,8,8192]{2,1,0:T(8,128)(2,1)S(1)}, u32[]{:S(2)}, u32[]{:S(2)}) collective-permute-start(bf16[4,8,8192]{2,1,0:T(8,128)(2,1)S(1)} %collective-permute-done.8), channel_id=1, source_target_pairs={{0,32},{1,33},{2,34},{3,35},{4,36},{5,37},{6,38},{7,39},{8,40},{9,... | collective-permute-start | bytes 1572872 | tf_op jit(solution)/shard_map/ppermute | solution.py:310
  119.6 2.2 %collective-permute-done.32 = bf16[4,8,8192]{2,1,0:T(8,128)(2,1)S(1)} collective-permute-done((bf16[4,8,8192]{2,1,0:T(8,128)(2,1)S(1)}, bf16[4,8,8192]{2,1,0:T(8,128)(2,1)S(1)}, u32[]{:S(2)}, u32[]{:S(2)}) %collective-permute-start.32) | collective-permute-done | bytes 524320 | tf_op jit(solution)/shard_map/ppermute | solution.py:310
  122.7 13.0 %corr.7 = bf16[4096,1024]{1,0:T(8,128)(2,1)} custom-call(s32[65]{0:T(128)} %pad_add_fusion.refs_0_, bf16[8,16384]{1,0:T(8,128)(2,1)} %get-tuple-element.39.refs_1_, bf16[32,8192]{1,0:T(8,128)(2,1)} %bitcast.50, bf16[32,8192]{1,0:T(8,128)(2,1)} %bitcast.56, bf16[32,8192]{1,0:T(8,128)(2,1)} %bitcast.57, ...), custom_call_target="tpu_custom_call", output_to_operand_aliasing={{}: (11, {})} | custom-call | flops 15032385536 | bytes 12582912 | tf_op jit(solution)/shard_map/corr/pallas_call | solution.py:226
  (101 shorter events, 9.0 us)
Async XLA Ops:
  2.6 17.1 %all-to-all-start = ((bf16[32,8,512]{2,1,0:T(8,128)(2,1)}), bf16[32,8,512]{2,1,0:T(8,128)(2,1)S(1)}, u32[]{:S(2)}, u32[]{:S(2)}) async-start(bf16[32,8,512]{2,1,0:T(8,128)(2,1)} %fusion), calls=%async_computation | async-start | bytes 524288 | tf_op jit(solution)/shard_map/all_to_all | solution.py:286
  31.4 6.0 %collective-permute-start.3 = (bf16[1,8,8192]{2,1,0:T(8,128)(2,1)S(1)}, bf16[1,8,8192]{2,1,0:T(8,128)(2,1)S(1)}, u32[]{:S(2)}, u32[]{:S(2)}) collective-permute-start(bf16[1,8,8192]{2,1,0:T(8,128)(2,1)S(1)} %add_bitcast_fusion), channel_id=1, source_target_pairs={{0,2},{1,3},{2,0},{3,1},{4,6},{5,7},{6,4},{7,5},{8,10},{9,11},{10,... | collective-permute-start | bytes 393224 | tf_op jit(solution)/shard_map/ppermute | solution.py:274
  34.8 3.8 %collective-permute-start.2 = (bf16[1,8,8192]{2,1,0:T(8,128)(2,1)S(1)}, bf16[1,8,8192]{2,1,0:T(8,128)(2,1)S(1)}, u32[]{:S(2)}, u32[]{:S(2)}) collective-permute-start(bf16[1,8,8192]{2,1,0:T(8,128)(2,1)S(1)} %add_bitcast_fusion), channel_id=1, source_target_pairs={{0,3},{1,0},{2,1},{3,2},{4,7},{5,4},{6,5},{7,6},{8,11},{9,8},{10,9... | collective-permute-start | bytes 393224 | tf_op jit(solution)/shard_map/ppermute | solution.py:274
  34.8 5.3 %collective-permute-start.1 = (bf16[1,8,8192]{2,1,0:T(8,128)(2,1)S(1)}, bf16[1,8,8192]{2,1,0:T(8,128)(2,1)S(1)}, u32[]{:S(2)}, u32[]{:S(2)}) collective-permute-start(bf16[1,8,8192]{2,1,0:T(8,128)(2,1)S(1)} %add_bitcast_fusion), channel_id=1, source_target_pairs={{0,1},{1,2},{2,3},{3,0},{4,5},{5,6},{6,7},{7,4},{8,9},{9,10},{10,1... | collective-permute-start | bytes 393224 | tf_op jit(solution)/shard_map/ppermute | solution.py:274
  40.2 15.2 %collective-permute-start.5 = (bf16[4,8,8192]{2,1,0:T(8,128)(2,1)S(1)}, bf16[4,8,8192]{2,1,0:T(8,128)(2,1)S(1)}, u32[]{:S(2)}, u32[]{:S(2)}) collective-permute-start(bf16[4,8,8192]{2,1,0:T(8,128)(2,1)S(1)} %pad_maximum_fusion), channel_id=1, source_target_pairs={{0,16},{1,17},{2,18},{3,19},{4,20},{5,21},{6,22},{7,23},{8,24},{9,... | collective-permute-start | bytes 1572872 | tf_op jit(solution)/shard_map/ppermute | solution.py:274
  40.3 15.1 %collective-permute-start.6 = (bf16[4,8,8192]{2,1,0:T(8,128)(2,1)S(1)}, bf16[4,8,8192]{2,1,0:T(8,128)(2,1)S(1)}, u32[]{:S(2)}, u32[]{:S(2)}) collective-permute-start(bf16[4,8,8192]{2,1,0:T(8,128)(2,1)S(1)} %pad_maximum_fusion), channel_id=1, source_target_pairs={{0,80},{1,81},{2,82},{3,83},{4,84},{5,85},{6,86},{7,87},{8,88},{9,... | collective-permute-start | bytes 1572872 | tf_op jit(solution)/shard_map/ppermute | solution.py:274
  43.0 13.0 %collective-permute-start.7 = (bf16[4,8,8192]{2,1,0:T(8,128)(2,1)S(1)}, bf16[4,8,8192]{2,1,0:T(8,128)(2,1)S(1)}, u32[]{:S(2)}, u32[]{:S(2)}) collective-permute-start(bf16[4,8,8192]{2,1,0:T(8,128)(2,1)S(1)} %pad_maximum_fusion), channel_id=1, source_target_pairs={{0,64},{1,65},{2,66},{3,67},{4,68},{5,69},{6,70},{7,71},{8,72},{9,... | collective-permute-start | bytes 1572872 | tf_op jit(solution)/shard_map/ppermute | solution.py:274
  43.0 16.5 %collective-permute-start.4 = (bf16[4,8,8192]{2,1,0:T(8,128)(2,1)S(1)}, bf16[4,8,8192]{2,1,0:T(8,128)(2,1)S(1)}, u32[]{:S(2)}, u32[]{:S(2)}) collective-permute-start(bf16[4,8,8192]{2,1,0:T(8,128)(2,1)S(1)} %pad_maximum_fusion), channel_id=1, source_target_pairs={{0,4},{1,5},{2,6},{3,7},{4,8},{5,9},{6,10},{7,11},{8,12},{9,13},{1... | collective-permute-start | bytes 1572872 | tf_op jit(solution)/shard_map/ppermute | solution.py:295
  43.3 16.8 %collective-permute-start.10 = (bf16[4,8,8192]{2,1,0:T(8,128)(2,1)S(1)}, bf16[4,8,8192]{2,1,0:T(8,128)(2,1)}, u32[]{:S(2)}, u32[]{:S(2)}) collective-permute-start(bf16[4,8,8192]{2,1,0:T(8,128)(2,1)S(1)} %pad_maximum_fusion), channel_id=1, source_target_pairs={{0,32},{1,33},{2,34},{3,35},{4,36},{5,37},{6,38},{7,39},{8,40},{9,... | collective-permute-start | bytes 1572872 | tf_op jit(solution)/shard_map/ppermute | solution.py:310
  55.5 4.7 %collective-permute-start.11 = (bf16[4,8,8192]{2,1,0:T(8,128)(2,1)S(1)}, bf16[4,8,8192]{2,1,0:T(8,128)(2,1)}, u32[]{:S(2)}, u32[]{:S(2)}) collective-permute-start(bf16[4,8,8192]{2,1,0:T(8,128)(2,1)S(1)} %collective-permute-done.5), channel_id=1, source_target_pairs={{0,32},{1,33},{2,34},{3,35},{4,36},{5,37},{6,38},{7,39},{8,40},{9,... | collective-permute-start | bytes 1572872 | tf_op jit(solution)/shard_map/ppermute | solution.py:310
  55.5 7.3 %collective-permute-start.12 = (bf16[4,8,8192]{2,1,0:T(8,128)(2,1)S(1)}, bf16[4,8,8192]{2,1,0:T(8,128)(2,1)}, u32[]{:S(2)}, u32[]{:S(2)}) collective-permute-start(bf16[4,8,8192]{2,1,0:T(8,128)(2,1)S(1)} %collective-permute-done.6), channel_id=1, source_target_pairs={{0,32},{1,33},{2,34},{3,35},{4,36},{5,37},{6,38},{7,39},{8,40},{9,... | collective-permute-start | bytes 1572872 | tf_op jit(solution)/shard_map/ppermute | solution.py:310
  56.0 6.8 %collective-permute-start.13 = (bf16[4,8,8192]{2,1,0:T(8,128)(2,1)S(1)}, bf16[4,8,8192]{2,1,0:T(8,128)(2,1)}, u32[]{:S(2)}, u32[]{:S(2)}) collective-permute-start(bf16[4,8,8192]{2,1,0:T(8,128)(2,1)S(1)} %collective-permute-done.7), channel_id=1, source_target_pairs={{0,32},{1,33},{2,34},{3,35},{4,36},{5,37},{6,38},{7,39},{8,40},{9,... | collective-permute-start | bytes 1572872 | tf_op jit(solution)/shard_map/ppermute | solution.py:310
  59.6 19.8 %collective-permute-start.9 = (bf16[4,8,8192]{2,1,0:T(8,128)(2,1)S(1)}, bf16[4,8,8192]{2,1,0:T(8,128)(2,1)S(1)}, u32[]{:S(2)}, u32[]{:S(2)}) collective-permute-start(bf16[4,8,8192]{2,1,0:T(8,128)(2,1)S(1)} %pad_maximum_fusion), channel_id=1, source_target_pairs={{0,12},{1,13},{2,14},{3,15},{4,0},{5,1},{6,2},{7,3},{8,4},{9,5},{1... | collective-permute-start | bytes 1572872 | tf_op jit(solution)/shard_map/ppermute | solution.py:295
  60.1 15.8 %collective-permute-start.14 = (bf16[4,8,8192]{2,1,0:T(8,128)(2,1)S(1)}, bf16[4,8,8192]{2,1,0:T(8,128)(2,1)}, u32[]{:S(2)}, u32[]{:S(2)}) collective-permute-start(bf16[4,8,8192]{2,1,0:T(8,128)(2,1)S(1)} %collective-permute-done.4), channel_id=1, source_target_pairs={{0,16},{1,17},{2,18},{3,19},{4,20},{5,21},{6,22},{7,23},{8,24},{9,... | collective-permute-start | bytes 1572872 | tf_op jit(solution)/shard_map/ppermute | solution.py:274
  60.1 15.8 %collective-permute-start.15 = (bf16[4,8,8192]{2,1,0:T(8,128)(2,1)S(1)}, bf16[4,8,8192]{2,1,0:T(8,128)(2,1)}, u32[]{:S(2)}, u32[]{:S(2)}) collective-permute-start(bf16[4,8,8192]{2,1,0:T(8,128)(2,1)S(1)} %collective-permute-done.4), channel_id=1, source_target_pairs={{0,80},{1,81},{2,82},{3,83},{4,84},{5,85},{6,86},{7,87},{8,88},{9,... | collective-permute-start | bytes 1572872 | tf_op jit(solution)/shard_map/ppermute | solution.py:274
  62.8 13.1 %collective-permute-start.16 = (bf16[4,8,8192]{2,1,0:T(8,128)(2,1)S(1)}, bf16[4,8,8192]{2,1,0:T(8,128)(2,1)}, u32[]{:S(2)}, u32[]{:S(2)}) collective-permute-start(bf16[4,8,8192]{2,1,0:T(8,128)(2,1)S(1)} %collective-permute-done.4), channel_id=1, source_target_pairs={{0,64},{1,65},{2,66},{3,67},{4,68},{5,69},{6,70},{7,71},{8,72},{9,... | collective-permute-start | bytes 1572872 | tf_op jit(solution)/shard_map/ppermute | solution.py:274
  75.9 4.4 %collective-permute-start.17 = (bf16[4,8,8192]{2,1,0:T(8,128)(2,1)S(1)}, bf16[4,8,8192]{2,1,0:T(8,128)(2,1)S(1)}, u32[]{:S(2)}, u32[]{:S(2)}) collective-permute-start(bf16[4,8,8192]{2,1,0:T(8,128)(2,1)S(1)} %collective-permute-done.4), channel_id=1, source_target_pairs={{0,32},{1,33},{2,34},{3,35},{4,36},{5,37},{6,38},{7,39},{8,40},{9,... | collective-permute-start | bytes 1572872 | tf_op jit(solution)/shard_map/ppermute | solution.py:310
  78.2 4.9 %collective-permute-start.19 = (bf16[4,8,8192]{2,1,0:T(8,128)(2,1)}, bf16[4,8,8192]{2,1,0:T(8,128)(2,1)}, u32[]{:S(2)}, u32[]{:S(2)}) collective-permute-start(bf16[4,8,8192]{2,1,0:T(8,128)(2,1)} %collective-permute-done.15), channel_id=1, source_target_pairs={{0,32},{1,33},{2,34},{3,35},{4,36},{5,37},{6,38},{7,39},{8,40},{9,... | collective-permute-start | bytes 1572872 | tf_op jit(solution)/shard_map/ppermute | solution.py:310
  78.6 5.0 %collective-permute-start.20 = (bf16[4,8,8192]{2,1,0:T(8,128)(2,1)}, bf16[4,8,8192]{2,1,0:T(8,128)(2,1)}, u32[]{:S(2)}, u32[]{:S(2)}) collective-permute-start(bf16[4,8,8192]{2,1,0:T(8,128)(2,1)} %collective-permute-done.16), channel_id=1, source_target_pairs={{0,32},{1,33},{2,34},{3,35},{4,36},{5,37},{6,38},{7,39},{8,40},{9,... | collective-permute-start | bytes 1572872 | tf_op jit(solution)/shard_map/ppermute | solution.py:310
  79.4 21.0 %collective-permute-start.8 = (bf16[4,8,8192]{2,1,0:T(8,128)(2,1)}, bf16[4,8,8192]{2,1,0:T(8,128)(2,1)S(1)}, u32[]{:S(2)}, u32[]{:S(2)}) collective-permute-start(bf16[4,8,8192]{2,1,0:T(8,128)(2,1)} %copy-done.2), channel_id=1, source_target_pairs={{0,8},{1,9},{2,10},{3,11},{4,12},{5,13},{6,14},{7,15},{8,0},{9,1},... | collective-permute-start | bytes 1572872 | tf_op jit(solution)/shard_map/ppermute | solution.py:314
  80.4 16.2 %collective-permute-start.21 = (bf16[4,8,8192]{2,1,0:T(8,128)(2,1)S(1)}, bf16[4,8,8192]{2,1,0:T(8,128)(2,1)S(1)}, u32[]{:S(2)}, u32[]{:S(2)}) collective-permute-start(bf16[4,8,8192]{2,1,0:T(8,128)(2,1)S(1)} %collective-permute-done.9), channel_id=1, source_target_pairs={{0,16},{1,17},{2,18},{3,19},{4,20},{5,21},{6,22},{7,23},{8,24},{9,... | collective-permute-start | bytes 1572872 | tf_op jit(solution)/shard_map/ppermute | solution.py:274
  80.7 15.9 %collective-permute-start.22 = (bf16[4,8,8192]{2,1,0:T(8,128)(2,1)S(1)}, bf16[4,8,8192]{2,1,0:T(8,128)(2,1)S(1)}, u32[]{:S(2)}, u32[]{:S(2)}) collective-permute-start(bf16[4,8,8192]{2,1,0:T(8,128)(2,1)S(1)} %collective-permute-done.9), channel_id=1, source_target_pairs={{0,80},{1,81},{2,82},{3,83},{4,84},{5,85},{6,86},{7,87},{8,88},{9,... | collective-permute-start | bytes 1572872 | tf_op jit(solution)/shard_map/ppermute | solution.py:274
  83.1 13.6 %collective-permute-start.23 = (bf16[4,8,8192]{2,1,0:T(8,128)(2,1)S(1)}, bf16[4,8,8192]{2,1,0:T(8,128)(2,1)}, u32[]{:S(2)}, u32[]{:S(2)}) collective-permute-start(bf16[4,8,8192]{2,1,0:T(8,128)(2,1)S(1)} %collective-permute-done.9), channel_id=1, source_target_pairs={{0,64},{1,65},{2,66},{3,67},{4,68},{5,69},{6,70},{7,71},{8,72},{9,... | collective-permute-start | bytes 1572872 | tf_op jit(solution)/shard_map/ppermute | solution.py:274
  96.6 4.0 %collective-permute-start.24 = (bf16[4,8,8192]{2,1,0:T(8,128)(2,1)S(1)}, bf16[4,8,8192]{2,1,0:T(8,128)(2,1)}, u32[]{:S(2)}, u32[]{:S(2)}) collective-permute-start(bf16[4,8,8192]{2,1,0:T(8,128)(2,1)S(1)} %collective-permute-done.9), channel_id=1, source_target_pairs={{0,32},{1,33},{2,34},{3,35},{4,36},{5,37},{6,38},{7,39},{8,40},{9,... | collective-permute-start | bytes 1572872 | tf_op jit(solution)/shard_map/ppermute | solution.py:310
  99.0 4.0 %collective-permute-start.25 = (bf16[4,8,8192]{2,1,0:T(8,128)(2,1)S(1)}, bf16[4,8,8192]{2,1,0:T(8,128)(2,1)}, u32[]{:S(2)}, u32[]{:S(2)}) collective-permute-start(bf16[4,8,8192]{2,1,0:T(8,128)(2,1)S(1)} %collective-permute-done.21), channel_id=1, source_target_pairs={{0,32},{1,33},{2,34},{3,35},{4,36},{5,37},{6,38},{7,39},{8,40},{9,... | collective-permute-start | bytes 1572872 | tf_op jit(solution)/shard_map/ppermute | solution.py:310
  99.1 4.0 %collective-permute-start.26 = (bf16[4,8,8192]{2,1,0:T(8,128)(2,1)S(1)}, bf16[4,8,8192]{2,1,0:T(8,128)(2,1)}, u32[]{:S(2)}, u32[]{:S(2)}) collective-permute-start(bf16[4,8,8192]{2,1,0:T(8,128)(2,1)S(1)} %collective-permute-done.22), channel_id=1, source_target_pairs={{0,32},{1,33},{2,34},{3,35},{4,36},{5,37},{6,38},{7,39},{8,40},{9,... | collective-permute-start | bytes 1572872 | tf_op jit(solution)/shard_map/ppermute | solution.py:310
  100.3 15.9 %collective-permute-start.28 = (bf16[4,8,8192]{2,1,0:T(8,128)(2,1)S(1)}, bf16[4,8,8192]{2,1,0:T(8,128)(2,1)S(1)}, u32[]{:S(2)}, u32[]{:S(2)}) collective-permute-start(bf16[4,8,8192]{2,1,0:T(8,128)(2,1)S(1)} %collective-permute-done.8), channel_id=1, source_target_pairs={{0,16},{1,17},{2,18},{3,19},{4,20},{5,21},{6,22},{7,23},{8,24},{9,... | collective-permute-start | bytes 1572872 | tf_op jit(solution)/shard_map/ppermute | solution.py:274
  100.7 15.6 %collective-permute-start.29 = (bf16[4,8,8192]{2,1,0:T(8,128)(2,1)S(1)}, bf16[4,8,8192]{2,1,0:T(8,128)(2,1)S(1)}, u32[]{:S(2)}, u32[]{:S(2)}) collective-permute-start(bf16[4,8,8192]{2,1,0:T(8,128)(2,1)S(1)} %collective-permute-done.8), channel_id=1, source_target_pairs={{0,80},{1,81},{2,82},{3,83},{4,84},{5,85},{6,86},{7,87},{8,88},{9,... | collective-permute-start | bytes 1572872 | tf_op jit(solution)/shard_map/ppermute | solution.py:274
  103.0 13.2 %collective-permute-start.30 = (bf16[4,8,8192]{2,1,0:T(8,128)(2,1)S(1)}, bf16[4,8,8192]{2,1,0:T(8,128)(2,1)}, u32[]{:S(2)}, u32[]{:S(2)}) collective-permute-start(bf16[4,8,8192]{2,1,0:T(8,128)(2,1)S(1)} %collective-permute-done.8), channel_id=1, source_target_pairs={{0,64},{1,65},{2,66},{3,67},{4,68},{5,69},{6,70},{7,71},{8,72},{9,... | collective-permute-start | bytes 1572872 | tf_op jit(solution)/shard_map/ppermute | solution.py:274
  118.1 3.8 %collective-permute-start.32 = (bf16[4,8,8192]{2,1,0:T(8,128)(2,1)S(1)}, bf16[4,8,8192]{2,1,0:T(8,128)(2,1)S(1)}, u32[]{:S(2)}, u32[]{:S(2)}) collective-permute-start(bf16[4,8,8192]{2,1,0:T(8,128)(2,1)S(1)} %collective-permute-done.28), channel_id=1, source_target_pairs={{0,32},{1,33},{2,34},{3,35},{4,36},{5,37},{6,38},{7,39},{8,40},{9,... | collective-permute-start | bytes 1572872 | tf_op jit(solution)/shard_map/ppermute | solution.py:310
  118.2 3.8 %collective-permute-start.33 = (bf16[4,8,8192]{2,1,0:T(8,128)(2,1)S(1)}, bf16[4,8,8192]{2,1,0:T(8,128)(2,1)}, u32[]{:S(2)}, u32[]{:S(2)}) collective-permute-start(bf16[4,8,8192]{2,1,0:T(8,128)(2,1)S(1)} %collective-permute-done.29), channel_id=1, source_target_pairs={{0,32},{1,33},{2,34},{3,35},{4,36},{5,37},{6,38},{7,39},{8,40},{9,... | collective-permute-start | bytes 1572872 | tf_op jit(solution)/shard_map/ppermute | solution.py:310
  118.6 3.6 %collective-permute-start.34 = (bf16[4,8,8192]{2,1,0:T(8,128)(2,1)}, bf16[4,8,8192]{2,1,0:T(8,128)(2,1)}, u32[]{:S(2)}, u32[]{:S(2)}) collective-permute-start(bf16[4,8,8192]{2,1,0:T(8,128)(2,1)} %collective-permute-done.30), channel_id=1, source_target_pairs={{0,32},{1,33},{2,34},{3,35},{4,36},{5,37},{6,38},{7,39},{8,40},{9,... | collective-permute-start | bytes 1572872 | tf_op jit(solution)/shard_map/ppermute | solution.py:310
  (21 other events, 176.3 us)

commit v3 on v2

v3 whole, which is shorter than its diff:
```python
import math

import jax
import jax.numpy as jnp
import numpy as np
from jax import lax
from jax.experimental import pallas as pl
from jax.experimental.pallas import tpu as pltpu
from jax.sharding import PartitionSpec as P

W = 2048
BINS = 1024
NLAG = 1024
SEGS = 8
CH_DEV = 8
SRC_DEV = 2
STEPS = 2
KIN = 16
BLK = SEGS * 2 * KIN
NBLK = BINS // KIN
WIDE = NBLK * BLK
HALF = WIDE // 2
GROUP = 8 * BLK
AXES = ("grp", "dev")
MIB = 1 << 20
FACTOR = 2.0 / math.sqrt(SEGS * BINS)
OFFSETS = (0, -1, 1, 2)


def tables():
    turns = (np.arange(W)[:, None] * np.arange(BINS)[None, :]) % W
    angles = turns.astype(np.float32) * np.float32(2.0 * math.pi / W)
    forward = np.concatenate([np.cos(angles), -np.sin(angles)], axis=1)
    inv_turns = (np.arange(BINS)[:, None] * np.arange(NLAG // 2)[None, :]) % W
    inv_angles = inv_turns.astype(np.float32) * np.float32(2.0 * math.pi / W)
    inverse = np.concatenate([np.cos(inv_angles), -np.sin(inv_angles)], axis=0)
    return forward.astype(jnp.bfloat16), inverse.astype(jnp.bfloat16)


def chunk_transpose(vs):
    vs = list(vs)
    axis = vs[0].ndim - 1
    chunk = lax.broadcasted_iota(jnp.int32, vs[0].shape, axis) // 16
    for bit in (1, 2, 4):
        low = (chunk & bit) == 0
        for i in range(8):
            if i & bit == 0:
                a, b = vs[i], vs[i | bit]
                vs[i] = jnp.where(low, a, pltpu.roll(b, 16 * bit, axis))
                vs[i | bit] = jnp.where(low, pltpu.roll(a, 128 - 16 * bit, axis), b)
    return vs


def front_kernel(meta, rec, table_hbm, white, keep, send, spec, scr, table, sems):
    def load(n):
        rows = pl.ds(n * 256, 256)
        return pltpu.make_async_copy(table_hbm.at[rows], table.at[rows], sems.at[n])

    for n in range(8):
        load(n).start()
    total = None
    for q in range(4):
        x = rec[:, q].astype(jnp.float32).reshape(SEGS * CH_DEV, 512).astype(jnp.bfloat16)
        for h in range(2):
            n = 2 * q + h
            load(n).wait()
            part = jnp.dot(
                x[:, h * 256 : h * 256 + 256], table[n * 256 : n * 256 + 256, :], preferred_element_type=jnp.float32
            )
            total = part if total is None else total + part
    re, im = total[:, :BINS], total[:, BINS:]
    power = re * re + im * im
    water = jnp.sum(power, axis=1, keepdims=True) * (1.0 / BINS)
    wide = jnp.concatenate([power, jnp.zeros((SEGS * CH_DEV, 128), jnp.float32)], axis=1)
    run = wide
    for shift in (1, 2, 4):
        run = run + pltpu.roll(run, shift, 1)
    run = run + pltpu.roll(wide, 8, 1)
    smooth = pltpu.roll(run, BINS + 128 - 4, 1)[:, :BINS] * (1.0 / 9.0)
    scale = lax.rsqrt(smooth + water + 1e-5)
    spec[:, :BINS] = re * scale
    spec[:, BINS:] = im * scale
    for kv in range(8):
        for h in range(2):
            vs = [
                spec[g * 8 : g * 8 + 8, ri * BINS + kv * 128 : ri * BINS + kv * 128 + 128]
                for g in range(4 * h, 4 * h + 4)
                for ri in range(2)
            ]
            for j, w in enumerate(chunk_transpose(vs)):
                at = (kv * 8 + j) * BLK + h * 128
                scr[:, at : at + 128] = w
    white[...] = scr[...].astype(jnp.bfloat16)
    core = meta[0]
    pair = lax.broadcasted_iota(jnp.int32, (CH_DEV, HALF), 0) // 2
    for out, half in ((keep, core), (send, 1 - core)):
        x = scr[:, pl.ds(pl.multiple_of(half * HALF, HALF), HALF)]
        a = jnp.where(pair == 2 * core, pltpu.roll(x, meta[1], 0), 0.0)
        b = jnp.where(pair == 2 * core + 1, pltpu.roll(x, meta[2], 0), 0.0)
        out[...] = (a + b).astype(jnp.bfloat16)


def front(meta, rec, table):
    vmem = pl.BlockSpec(memory_space=pltpu.VMEM)
    return pl.pallas_call(
        front_kernel,
        out_shape=(
            jax.ShapeDtypeStruct((CH_DEV, WIDE), jnp.bfloat16),
            jax.ShapeDtypeStruct((CH_DEV, HALF), jnp.bfloat16),
            jax.ShapeDtypeStruct((CH_DEV, HALF), jnp.bfloat16),
        ),
        in_specs=[pl.BlockSpec(memory_space=pltpu.SMEM), vmem, pl.BlockSpec(memory_space=pltpu.MemorySpace.HBM)],
        out_specs=(vmem, vmem, vmem),
        scratch_shapes=[
            pltpu.VMEM((SEGS * CH_DEV, 2 * BINS), jnp.float32),
            pltpu.VMEM((CH_DEV, WIDE), jnp.float32),
            pltpu.VMEM((W, 2 * BINS), jnp.bfloat16),
            pltpu.SemaphoreType.DMA((8,)),
        ],
        compiler_params=pltpu.CompilerParams(vmem_limit_bytes=60 * MIB),
        name="front",
    )(meta, rec, table)


def rows_kernel(white, rows):
    own = white[...].astype(jnp.float32)
    lane = lax.broadcasted_iota(jnp.int32, (CH_DEV, WIDE), 1)
    turned = jnp.where(
        (lane & 16) == 0, -pltpu.roll(own, WIDE - 16, 1), pltpu.roll(own, 16, 1)
    )
    last = jnp.where((lane & 1) == 0, own, turned)
    last = jnp.where((lane & 2) == 0, last, -last)
    parts = [own, turned, last, jnp.zeros_like(own)]
    rows[...] = jnp.concatenate(parts, axis=0).astype(jnp.bfloat16)


def channel_rows(white):
    vmem = pl.BlockSpec(memory_space=pltpu.VMEM)
    return pl.pallas_call(
        rows_kernel,
        out_shape=jax.ShapeDtypeStruct((4 * CH_DEV, WIDE), jnp.bfloat16),
        in_specs=[vmem],
        out_specs=vmem,
        compiler_params=pltpu.CompilerParams(vmem_limit_bytes=16 * MIB),
        name="rows",
    )(white)


def corr_kernel(first, planes, arrays, meta, rows_hbm, *refs):
    pieces, sources = 4 * planes, 128 * planes
    mine, sib, e_hbm = refs[:arrays], refs[arrays : 2 * arrays], refs[2 * arrays]
    out, rows_scr, a_scr, x_scr, e_scr, flip, ov, edge, edge_t, d_scr, yf, yb, a_sems, sems = refs[2 * arrays + (1 if first else 2) :]

    def load(j, half, n):
        lines = (mine, sib)[half]
        if len(lines) == pieces:
            ref, row = lines[n], 0
        elif n % 4 < 3:
            ref, row = lines[n % 4], n // 4 * 32
        else:
            ref, row = lines[3 + n // 4], 0
        return pltpu.make_async_copy(
            ref.at[pl.ds(row, 32), pl.ds(pl.multiple_of(j * GROUP, GROUP), GROUP)],
            a_scr.at[half, j, pl.ds(n * 32, 32)],
            a_sems.at[half, j],
        )

    def load_rows(j, half):
        g = (core if half == 0 else 1 - core) * 4 + j
        return pltpu.make_async_copy(
            rows_hbm.at[:, pl.ds(pl.multiple_of(g * GROUP, GROUP), GROUP)],
            rows_scr.at[half, j],
            a_sems.at[half, j],
        )

    core = meta[0]
    for j in range(4):
        for half in range(2):
            load_rows(j, half).start()
            for n in range(pieces):
                load(j, half, n).start()
    e_copy = pltpu.make_async_copy(e_hbm, e_scr, sems.at[0])
    e_copy.start()
    diag = lax.broadcasted_iota(jnp.int32, (KIN, BLK), 0) == (
        lax.broadcasted_iota(jnp.int32, (KIN, BLK), 1) & 15
    )
    back = lax.broadcasted_iota(jnp.int32, (512, 512), 0) + lax.broadcasted_iota(jnp.int32, (512, 512), 1)
    flip[...] = jnp.where(back == 512, 1.0, 0.0).astype(jnp.bfloat16)
    edge[...] = jnp.zeros((128, sources), jnp.float32)

    def group(j, half):
        g = (core if half == 0 else 1 - core) * 4 + j
        for i in range(8):
            a = a_scr[half, j, :, i * BLK : i * BLK + BLK]
            if half == 1:
                a = jnp.concatenate(
                    [
                        a[128 * k + 32 * n + 8 * o : 128 * k + 32 * n + 8 * o + 8]
                        for k in range(planes)
                        for o in range(4)
                        for n in range(4)
                    ],
                    axis=0,
                )
            r = rows_scr[half, j, :, i * BLK : i * BLK + BLK].astype(jnp.float32)
            block = jnp.where(diag[None], r[:16, None, :], 0.0).astype(jnp.bfloat16)
            block = jnp.concatenate([block.reshape(256, BLK), r[16:].astype(jnp.bfloat16)], axis=0)
            prod = lax.dot_general(
                block, a, (((1,), (1,)), ((), ())), preferred_element_type=jnp.float32
            )
            prod = prod * FACTOR
            edge[0:8, :] += prod[256:264]
            ov[half, :, i * KIN : (i + 1) * KIN, :] = prod[:256].astype(jnp.bfloat16).reshape(16, KIN, sources)
        for ri in range(2):
            at = pl.ds(pl.multiple_of(ri * BINS + g * 128, 128), 128)
            for c in range(CH_DEV):
                x_scr[:, c, :, at] = ov[half, ri * 8 + c].T.reshape(2 * planes, 64, 128)

    @pl.loop(0, 4)
    def _(j):
        for half in range(2):
            load_rows(j, half).wait()
            for n in range(pieces):
                load(j, half, n).wait()
        group(j, 0)
        group(j, 1)

    edge_t[...] = edge[...].T
    e_copy.wait()
    first_lane = lax.broadcasted_iota(jnp.int32, (64, 128), 1) == 0

    def copy(q, n):
        at = q * 32 + n
        return pltpu.make_async_copy(
            yb.at[pl.ds(pl.multiple_of(at * 16, 16), 16)],
            out.at[pl.ds(pl.multiple_of(meta[1 + at] * 16, 16), 16)],
            sems.at[1],
        )

    @pl.loop(0, 2 * planes)
    def _(q):
        x = x_scr[q].reshape(512, 2 * BINS)

        def put(lag, y):
            for h in range(2):
                for c in range(CH_DEV):
                    part = y[c * 64 : c * 64 + 64, h * 128 : h * 128 + 128]
                    if lag + h == 0:
                        at = pl.ds(pl.multiple_of(q * 64, 64), 64)
                        part = jnp.where(first_lane, edge_t[at, c : c + 1], part)
                    yf[lag + h, pl.ds(c, 64, stride=8), :] = part
                at = pl.ds((lag + h) * 128, 128)
                yb[pl.ds(pl.multiple_of(q * 512, 512), 512), at] = yf[lag + h].astype(jnp.bfloat16)

        for n in range(2):
            lanes = pl.ds(n * 256, 256)
            even = jnp.dot(x[:, :BINS], e_scr[:BINS, lanes], preferred_element_type=jnp.float32)
            odd = jnp.dot(x[:, BINS:], e_scr[BINS:, lanes], preferred_element_type=jnp.float32)
            put(4 + 2 * n, even + odd)
            d_scr[:, lanes] = (even - odd).astype(jnp.bfloat16)
        put(2, jnp.dot(d_scr[...], flip[:, 256:], preferred_element_type=jnp.float32))
        put(0, jnp.dot(d_scr[:, 256:], flip[256:, :256], preferred_element_type=jnp.float32))

        @pl.loop(0, 32)
        def _(n):
            copy(q, n).start()

    pltpu.make_async_copy(yb, out.at[pl.ds(0, sources * CH_DEV)], sems.at[1]).wait()


def corr(meta, rows, mine, sib, inverse, out):
    first = out is None
    planes = sum(m.shape[0] for m in mine) // 128
    hbm = pl.BlockSpec(memory_space=pltpu.MemorySpace.HBM)
    args = [meta, rows, *mine, *sib, inverse] + ([] if first else [out])
    return pl.pallas_call(
        lambda *refs: corr_kernel(first, planes, len(mine), *refs),
        out_shape=jax.ShapeDtypeStruct((STEPS * 256 * CH_DEV, NLAG), jnp.bfloat16),
        in_specs=[pl.BlockSpec(memory_space=pltpu.SMEM)] + [hbm] * (len(args) - 1),
        out_specs=hbm,
        scratch_shapes=[
            pltpu.VMEM((2, 4, 32, GROUP), jnp.bfloat16),
            pltpu.VMEM((2, 4, 128 * planes, GROUP), jnp.bfloat16),
            pltpu.VMEM((2 * planes, CH_DEV, 64, 2 * BINS), jnp.bfloat16),
            pltpu.VMEM((2 * BINS, NLAG // 2), jnp.bfloat16),
            pltpu.VMEM((NLAG // 2, NLAG // 2), jnp.bfloat16),
            pltpu.VMEM((2, 16, 128, 128 * planes), jnp.bfloat16),
            pltpu.VMEM((128, 128 * planes), jnp.float32),
            pltpu.VMEM((128 * planes, 128), jnp.float32),
            pltpu.VMEM((512, NLAG // 2), jnp.bfloat16),
            pltpu.VMEM((8, 512, 128), jnp.float32),
            pltpu.VMEM((1024 * planes, NLAG), jnp.bfloat16),
            pltpu.SemaphoreType.DMA((2, 4)),
            pltpu.SemaphoreType.DMA((2,)),
        ],
        input_output_aliases={} if first else {3 + 2 * len(mine): 0},
        compiler_params=pltpu.CompilerParams(vmem_limit_bytes=60 * MIB),
        cost_estimate=pl.CostEstimate(
            flops=planes * 5 * 1024 * 2048 * 1024, bytes_accessed=12 * MIB, transcendentals=0
        ),
        name="corr",
    )(*args)


def device(x, y, z, core):
    return ((z // 2) * 2 + core) * 32 + (z % 2) * 16 + y * 4 + x


def line_pairs(axes, step):
    pairs = []
    for core in range(2):
        for n in range(64):
            at = {"x": n % 4, "y": n // 4 % 4, "z": n // 16}
            to = dict(at)
            to[axes[core]] = (at[axes[core]] + step) % 4
            pairs.append((device(**at, core=core), device(**to, core=core)))
    return pairs


CORE_PAIRS = [
    (device(n % 4, n // 4 % 4, n // 16, core), device(n % 4, n // 4 % 4, n // 16, 1 - core))
    for core in range(2)
    for n in range(64)
]


def line(block, axes):
    return [block] + [lax.ppermute(block, AXES, line_pairs(axes, s)) for s in (1, -1, 2)]


def local(records, channel_map, source_offset):
    forward, inverse = tables()
    forward, inverse = jnp.asarray(forward), jnp.asarray(inverse)
    grp, dev = lax.axis_index("grp"), lax.axis_index("dev")
    core = grp % 2
    x0, y0, z0 = dev % 4, dev // 4 % 4, (grp // 2) * 2 + dev // 16

    pick = (channel_map[0][:, None] == jnp.arange(256, dtype=jnp.int32)[None, :]).astype(jnp.bfloat16)
    ordered = jnp.dot(pick, records, preferred_element_type=jnp.float32).astype(jnp.bfloat16)
    regrouped = lax.all_to_all(ordered.reshape(32, 8, 512), "dev", split_axis=0, concat_axis=0, tiled=True)

    turns = (4 * core + 2 * jnp.arange(2, dtype=jnp.int32) - source_offset[:, 0]) % 8
    front_meta = jnp.stack([core, turns[0], turns[1]])
    white, keep, send = front(front_meta, regrouped.reshape(8, 4, 8, 512), forward)
    rows = channel_rows(white)
    block = keep + lax.ppermute(send, AXES, CORE_PAIRS)

    near = jnp.concatenate(line(block[None], "xz"), axis=0)
    off = jnp.array(OFFSETS, jnp.int32)
    outer, inner = jnp.meshgrid(off, off, indexing="ij")
    xs = (x0 + jnp.where(core == 0, inner, outer)) % 4
    zs = (z0 + jnp.where(core == 0, outer, inner)) % 4

    def places(offsets):
        ys = (y0 + jnp.array(offsets, jnp.int32).reshape(-1, 1, 1)) % 4
        chip = (zs // 2) * 64 + (zs % 2) * 16 + ys * 4 + xs
        place = chip.reshape(-1, 1, 1) + jnp.arange(2)[None, :, None] * 32 + jnp.arange(2)[None, None, :] * 128
        return jnp.concatenate([core[None], place.reshape(-1)]).astype(jnp.int32)

    def shift(x, step):
        return lax.ppermute(x, AXES, line_pairs("yy", step))

    def swap(xs):
        return [lax.ppermute(x, AXES, CORE_PAIRS) for x in xs]

    def flat(xs):
        return [x.reshape(-1, HALF) for x in xs]

    after = lax.optimization_barrier
    first = line(near, "zx")
    ahead, behind = shift(near, 1), shift(near, -1)
    near, ahead, *first = after((near, ahead, *first))
    second = line(ahead, "zx")
    across = shift(near, 2)
    behind_far = shift(first[3], -1)
    first_sib = swap(first)
    behind, across, *second = after((behind, across, *second))
    both = jnp.concatenate([behind, across], axis=0)
    rest = [both] + [lax.ppermute(both, AXES, line_pairs("zx", s)) for s in (1, -1)]
    across_far = lax.ppermute(across, AXES, line_pairs("zx", 2))
    second_sib = swap(second)
    out = corr(places((0, -1)), rows, flat(first + second), flat(first_sib + second_sib), inverse, None)
    out, *rest = after((out, *rest, behind_far, across_far))
    out = corr(places((1, 2)), rows, flat(rest), flat(swap(rest)), inverse, out)
    return out.reshape(1, STEPS * 256, CH_DEV, NLAG)


def solution(mesh):
    return jax.shard_map(
        local,
        mesh=mesh,
        in_specs=(P("grp", "dev"), P("grp", None), P(None, ("grp", "dev"))),
        out_specs=P(None, None, ("grp", "dev"), None),
        check_vma=False,
    )
```

time: 136 us -> 129 us (0.949)
  Pallas kernels: 58.9 us -> 40.6 us
  waiting for transfers between devices: 22.9 us -> 30.3 us
  local copies, waits for them, and re-layouts: 2.77 us -> 5.89 us
  starting transfers between devices: 44.1 us -> 45.5 us
    pallas_call x4 -> x3, Pallas kernels: 52.1 us -> 33.9 us  [the longest x2 33.5 us: corr(): pl.pallas_call(lambda *refs: corr_kernel(first, planes, len(mine), *refs)...]
    ppermute x19 -> x20, starting transfers between devices: 17.2 us -> 23.3 us  [the longest x13 16.3 us: swap(): return [lax.ppermute(x, AXES, CORE_PAIRS) for x in xs]]
    ppermute x19 -> x20, waiting for transfers between devices: 3.47 us -> 8.81 us  [the longest x13 7.24 us: swap(): return [lax.ppermute(x, AXES, CORE_PAIRS) for x in xs]]
    ppermute x15 -> x9, starting transfers between devices: 15.5 us -> 10.8 us  [line(): lax.ppermute(block, AXES, line_pairs(axes, s))]
    unnamed x34 -> x41, local copies, waits for them, and re-layouts: 2.16 us -> 5.41 us
    ppermute x15 -> x9, waiting for transfers between devices: 11.7 us -> 13.8 us  [line(): lax.ppermute(block, AXES, line_pairs(axes, s))]
  transfers between devices with their start and end apart: 36 -> 31, of which waited for: 12 -> 14; matrix products, arithmetic and copies ran while one was open for 3% -> 3% of each run, Pallas kernels for 29% -> 13%
where the time goes in v3:
time: 129 us; the launch traced here: 128 us
  starting transfers between devices  45.5 us (35%)
  Pallas kernels  40.6 us (31%)
  waiting for transfers between devices  30.3 us (23%)
  local copies, waits for them, and re-layouts  5.89 us (5%)
  other arithmetic  3.97 us (3%)
  matrix products  1.66 us (1%)
    pallas_call x2, Pallas kernels, corr(): pl.pallas_call(lambda *refs: corr_kernel(first, planes, len(mine), *refs)...  33.5 us
    ppermute x13, starting transfers between devices, swap(): return [lax.ppermute(x, AXES, CORE_PAIRS) for x in xs]  16.3 us
    ppermute x9, waiting for transfers between devices, line(): lax.ppermute(block, AXES, line_pairs(axes, s))  13.8 us
    ppermute x9, starting transfers between devices, line(): lax.ppermute(block, AXES, line_pairs(axes, s))  10.8 us
    all_to_all x1, starting transfers between devices, local(): lax.all_to_all(ordered.reshape(32, 8, 512), 'dev', split_axis=0, concat_a...  9.22 us
    ppermute x13, waiting for transfers between devices, swap(): return [lax.ppermute(x, AXES, CORE_PAIRS) for x in xs]  7.24 us
    pallas_call x1, Pallas kernels, front(): pl.pallas_call(front_kernel, out_shape=(jax.ShapeDtypeStruct((CH_DEV, WID...  6.63 us
    all_to_all x1, waiting for transfers between devices, local(): lax.all_to_all(ordered.reshape(32, 8, 512), 'dev', split_axis=0, concat_a...  6.5 us
  transfers between devices with their start and end apart: 31, of which 14 were waited for; matrix products, arithmetic and copies ran while one was open for 3% of the time, Pallas kernels for 13%

profile of v3, /device:TPU:1, one launch (start us, length us, event | category | flops | bytes accessed | tf_op | source)
XLA Modules:
  0.0 128.4 jit_solution(15402260457616100336)
XLA Ops:
  1.0 1.7 %fusion = bf16[32,8,512]{2,1,0:T(8,128)(2,1)} fusion(bf16[256,512]{1,0:T(8,128)(2,1)S(1)} %copy-done, s32[256]{0:T(256)} %bitcast.42), kind=kOutput, calls=%fused_computation.1 | convolution fusion | flops 67305472 | bytes 525312 | tf_op jit(solution)/shard_map/dot_general | solution.py:339
  2.6 9.2 %all-to-all-start = ((bf16[32,8,512]{2,1,0:T(8,128)(2,1)}), bf16[32,8,512]{2,1,0:T(8,128)(2,1)S(1)}, u32[]{:S(2)}, u32[]{:S(2)}) async-start(bf16[32,8,512]{2,1,0:T(8,128)(2,1)} %fusion), calls=%async_computation | async-start | bytes 524288 | tf_op jit(solution)/shard_map/all_to_all | solution.py:340
  13.2 6.5 %all-to-all-done = bf16[32,8,512]{2,1,0:T(8,128)(2,1)S(1)} async-done(((bf16[32,8,512]{2,1,0:T(8,128)(2,1)}), bf16[32,8,512]{2,1,0:T(8,128)(2,1)S(1)}, u32[]{:S(2)}, u32[]{:S(2)}) %all-to-all-start) | async-done | bytes 262176 | tf_op jit(solution)/shard_map/all_to_all | solution.py:340
  20.4 6.6 %front.1 = (bf16[8,16384]{1,0:T(8,128)(2,1)}, bf16[8,8192]{1,0:T(8,128)(2,1)}, bf16[8,8192]{1,0:T(8,128)(2,1)}) custom-call(s32[3]{0:T(128)} %pad_add_fusion.2.meta, bf16[8,4,8,512]{3,2,1,0:T(8,128)(2,1)} %bitcast.39, bf16[2048,2048]{1,0:T(8,128)(2,1)} %constant.146.clone.table_hbm), custom_call_target="tpu_custom_call" | custom-call | tf_op jit(solution)/shard_map/front/pallas_call | solution.py:105
  27.0 2.2 %collective-permute-start = (bf16[8,8192]{1,0:T(8,128)(2,1)}, bf16[8,8192]{1,0:T(8,128)(2,1)S(1)}, u32[]{:S(2)}, u32[]{:S(2)}) collective-permute-start(bf16[8,8192]{1,0:T(8,128)(2,1)} %get-tuple-element.28), channel_id=1, source_target_pairs={{0,32},{1,33},{2,34},{3,35},{4,36},{5,37},{6,38},{7,39},{8,40},{9,... | collective-permute-start | bytes 393224 | tf_op jit(solution)/shard_map/ppermute | solution.py:346
  29.2 1.2 collective-permute-done
  31.3 3.4 %collective-permute-start.3 = (bf16[1,8,8192]{2,1,0:T(8,128)(2,1)S(1)}, bf16[1,8,8192]{2,1,0:T(8,128)(2,1)S(1)}, u32[]{:S(2)}, u32[]{:S(2)}) collective-permute-start(bf16[1,8,8192]{2,1,0:T(8,128)(2,1)S(1)} %add_bitcast_fusion), channel_id=1, source_target_pairs={{0,2},{1,3},{2,0},{3,1},{4,6},{5,7},{6,4},{7,5},{8,10},{9,11},{10,... | collective-permute-start | bytes 393224 | tf_op jit(solution)/shard_map/ppermute | solution.py:328
  34.7 1.5 %collective-permute-start.1 = (bf16[1,8,8192]{2,1,0:T(8,128)(2,1)S(1)}, bf16[1,8,8192]{2,1,0:T(8,128)(2,1)S(1)}, u32[]{:S(2)}, u32[]{:S(2)}) collective-permute-start(bf16[1,8,8192]{2,1,0:T(8,128)(2,1)S(1)} %add_bitcast_fusion), channel_id=1, source_target_pairs={{0,1},{1,2},{2,3},{3,0},{4,5},{5,6},{6,7},{7,4},{8,9},{9,10},{10,1... | collective-permute-start | bytes 393224 | tf_op jit(solution)/shard_map/ppermute | solution.py:328
  36.3 1.1 collective-permute-done.3
  37.4 1.2 collective-permute-done.2
  38.5 1.5 %collective-permute-done.1 = bf16[1,8,8192]{2,1,0:T(8,128)(2,1)S(1)} collective-permute-done((bf16[1,8,8192]{2,1,0:T(8,128)(2,1)S(1)}, bf16[1,8,8192]{2,1,0:T(8,128)(2,1)S(1)}, u32[]{:S(2)}, u32[]{:S(2)}) %collective-permute-start.1) | collective-permute-done | bytes 131104 | tf_op jit(solution)/shard_map/ppermute | solution.py:328
  40.1 1.1 collective-permute-start.7
  41.2 1.3 collective-permute-start.6
  43.0 2.7 %collective-permute-start.8 = (bf16[4,8,8192]{2,1,0:T(8,128)(2,1)S(1)}, bf16[4,8,8192]{2,1,0:T(8,128)(2,1)S(1)}, u32[]{:S(2)}, u32[]{:S(2)}) collective-permute-start(bf16[4,8,8192]{2,1,0:T(8,128)(2,1)S(1)} %pad_maximum_fusion), channel_id=1, source_target_pairs={{0,12},{1,13},{2,14},{3,15},{4,0},{5,1},{6,2},{7,3},{8,4},{9,5},{1... | collective-permute-start | bytes 1572872 | tf_op jit(solution)/shard_map/ppermute | solution.py:361
  45.7 4.3 %collective-permute-done.7 = bf16[4,8,8192]{2,1,0:T(8,128)(2,1)S(1)} collective-permute-done((bf16[4,8,8192]{2,1,0:T(8,128)(2,1)S(1)}, bf16[4,8,8192]{2,1,0:T(8,128)(2,1)S(1)}, u32[]{:S(2)}, u32[]{:S(2)}) %collective-permute-start.7) | collective-permute-done | bytes 524320 | tf_op jit(solution)/shard_map/ppermute | solution.py:328
  50.1 4.2 %collective-permute-done.6 = bf16[4,8,8192]{2,1,0:T(8,128)(2,1)} collective-permute-done((bf16[4,8,8192]{2,1,0:T(8,128)(2,1)S(1)}, bf16[4,8,8192]{2,1,0:T(8,128)(2,1)}, u32[]{:S(2)}, u32[]{:S(2)}) %collective-permute-start.6) | collective-permute-done | bytes 524320 | tf_op jit(solution)/shard_map/ppermute | solution.py:328
  54.3 1.5 %collective-permute-done.5 = bf16[4,8,8192]{2,1,0:T(8,128)(2,1)} collective-permute-done((bf16[4,8,8192]{2,1,0:T(8,128)(2,1)S(1)}, bf16[4,8,8192]{2,1,0:T(8,128)(2,1)}, u32[]{:S(2)}, u32[]{:S(2)}) %collective-permute-start.5) | collective-permute-done | bytes 524320 | tf_op jit(solution)/shard_map/ppermute | solution.py:328
  55.7 1.5 %collective-permute-start.12 = (bf16[4,8,8192]{2,1,0:T(8,128)(2,1)}, bf16[4,8,8192]{2,1,0:T(8,128)(2,1)}, u32[]{:S(2)}, u32[]{:S(2)}) collective-permute-start(bf16[4,8,8192]{2,1,0:T(8,128)(2,1)} %collective-permute-done.4), channel_id=1, source_target_pairs={{0,64},{1,65},{2,66},{3,67},{4,68},{5,69},{6,70},{7,71},{8,72},{9,... | collective-permute-start | bytes 1572872 | tf_op jit(solution)/shard_map/ppermute | solution.py:328
  57.2 1.3 collective-permute-start.11
  60.1 0.9 copy-done.2
  61.5 1.0 copy-done.1
  62.5 5.7 %collective-permute-start.13 = (bf16[4,8,8192]{2,1,0:T(8,128)(2,1)S(1)}, bf16[4,8,8192]{2,1,0:T(8,128)(2,1)S(1)}, u32[]{:S(2)}, u32[]{:S(2)}) collective-permute-start(bf16[4,8,8192]{2,1,0:T(8,128)(2,1)S(1)} %pad_maximum_fusion), channel_id=1, source_target_pairs={{0,32},{1,33},{2,34},{3,35},{4,36},{5,37},{6,38},{7,39},{8,40},{9,... | collective-permute-start | bytes 1572872 | tf_op jit(solution)/shard_map/ppermute | solution.py:364
  68.2 1.6 %collective-permute-done.9 = bf16[4,8,8192]{2,1,0:T(8,128)(2,1)S(1)} collective-permute-done((bf16[4,8,8192]{2,1,0:T(8,128)(2,1)S(1)}, bf16[4,8,8192]{2,1,0:T(8,128)(2,1)S(1)}, u32[]{:S(2)}, u32[]{:S(2)}) %collective-permute-start.9) | collective-permute-done | bytes 524320 | tf_op jit(solution)/shard_map/ppermute | solution.py:361
  69.8 5.1 %collective-permute-start.14 = (bf16[4,8,8192]{2,1,0:T(8,128)(2,1)}, bf16[4,8,8192]{2,1,0:T(8,128)(2,1)S(1)}, u32[]{:S(2)}, u32[]{:S(2)}) collective-permute-start(bf16[4,8,8192]{2,1,0:T(8,128)(2,1)} %collective-permute-done.5), channel_id=1, source_target_pairs={{0,32},{1,33},{2,34},{3,35},{4,36},{5,37},{6,38},{7,39},{8,40},{9,... | collective-permute-start | bytes 1572872 | tf_op jit(solution)/shard_map/ppermute | solution.py:364
  77.0 1.1 collective-permute-done.15
  78.9 2.1 %collective-permute-start.24 = (bf16[4,8,8192]{2,1,0:T(8,128)(2,1)S(1)}, bf16[4,8,8192]{2,1,0:T(8,128)(2,1)}, u32[]{:S(2)}, u32[]{:S(2)}) collective-permute-start(bf16[4,8,8192]{2,1,0:T(8,128)(2,1)S(1)} %collective-permute-done.9), channel_id=1, source_target_pairs={{0,64},{1,65},{2,66},{3,67},{4,68},{5,69},{6,70},{7,71},{8,72},{9,... | collective-permute-start | bytes 1572872 | tf_op jit(solution)/shard_map/ppermute | solution.py:380
  81.0 1.8 %collective-permute-start.22 = (bf16[8,8,8192]{2,1,0:T(8,128)(2,1)S(1)}, bf16[8,8,8192]{2,1,0:T(8,128)(2,1)}, u32[]{:S(2)}, u32[]{:S(2)}) collective-permute-start(bf16[8,8,8192]{2,1,0:T(8,128)(2,1)S(1)} %constant_dynamic-update-slice_fusion), channel_id=1, source_target_pairs={{0,80},{1,81},{2,82},{3,83},{4,84},{5,85},{6,86},{7,87},{8,88},{9,... | collective-permute-start | bytes 3145736 | tf_op jit(solution)/shard_map/ppermute | solution.py:379
  83.9 16.8 %corr.2.refs_13_ = bf16[4096,1024]{1,0:T(8,128)(2,1)} custom-call(s32[129]{0:T(256)} %pad_add_fusion.refs_0_, bf16[32,16384]{1,0:T(8,128)(2,1)} %copy-done.1, bf16[32,8192]{1,0:T(8,128)(2,1)} %bitcast.40, bf16[32,8192]{1,0:T(8,128)(2,1)} %bitcast.7.refs_3_, bf16[32,8192]{1,0:T(8,128)(2,1)} %bitcast.8.refs_4_, bf16[32,8192]{1,0:T(8,128)(2,1)} %bitcast.44, ...), custom_call_target="tpu_custom_call" | custom-call | flops 21474836480 | bytes 12582912 | tf_op jit(solution)/shard_map/corr/pallas_call | solution.py:276
  100.7 2.6 %collective-permute-start.25 = (bf16[8,8,8192]{2,1,0:T(8,128)(2,1)S(1)}, bf16[8,8,8192]{2,1,0:T(8,128)(2,1)S(1)}, u32[]{:S(2)}, u32[]{:S(2)}) collective-permute-start(bf16[8,8,8192]{2,1,0:T(8,128)(2,1)S(1)} %constant_dynamic-update-slice_fusion), channel_id=1, source_target_pairs={{0,32},{1,33},{2,34},{3,35},{4,36},{5,37},{6,38},{7,39},{8,40},{9,... | collective-permute-start | bytes 3145736 | tf_op jit(solution)/shard_map/ppermute | solution.py:364
  105.2 2.5 %collective-permute-done.28 = bf16[4,8,8192]{2,1,0:T(8,128)(2,1)S(1)} collective-permute-done((bf16[4,8,8192]{2,1,0:T(8,128)(2,1)S(1)}, bf16[4,8,8192]{2,1,0:T(8,128)(2,1)S(1)}, u32[]{:S(2)}, u32[]{:S(2)}) %collective-permute-start.28) | collective-permute-done | bytes 524320 | tf_op jit(solution)/shard_map/ppermute | solution.py:364
  107.7 2.8 %collective-permute-done.29 = bf16[4,8,8192]{2,1,0:T(8,128)(2,1)} collective-permute-done((bf16[4,8,8192]{2,1,0:T(8,128)(2,1)}, bf16[4,8,8192]{2,1,0:T(8,128)(2,1)}, u32[]{:S(2)}, u32[]{:S(2)}) %collective-permute-start.29) | collective-permute-done | bytes 524320 | tf_op jit(solution)/shard_map/ppermute | solution.py:364
  111.5 16.7 %corr.3 = bf16[4096,1024]{1,0:T(8,128)(2,1)} custom-call(s32[129]{0:T(256)} %pad_add_fusion.1.refs_0_, bf16[32,16384]{1,0:T(8,128)(2,1)} %copy-done.1, bf16[64,8192]{1,0:T(8,128)(2,1)} %bitcast.41, bf16[64,8192]{1,0:T(8,128)(2,1)} %bitcast.23.refs_3_, bf16[64,8192]{1,0:T(8,128)(2,1)} %bitcast.24.refs_4_, ...), custom_call_target="tpu_custom_call", output_to_operand_aliasing={{}: (13, {})} | custom-call | flops 21474836480 | bytes 12582912 | tf_op jit(solution)/shard_map/corr/pallas_call | solution.py:276
  (94 shorter events, 13.2 us)
Async XLA Ops:
  2.6 17.1 %all-to-all-start = ((bf16[32,8,512]{2,1,0:T(8,128)(2,1)}), bf16[32,8,512]{2,1,0:T(8,128)(2,1)S(1)}, u32[]{:S(2)}, u32[]{:S(2)}) async-start(bf16[32,8,512]{2,1,0:T(8,128)(2,1)} %fusion), calls=%async_computation | async-start | bytes 524288 | tf_op jit(solution)/shard_map/all_to_all | solution.py:340
  27.0 3.4 %collective-permute-start = (bf16[8,8192]{1,0:T(8,128)(2,1)}, bf16[8,8192]{1,0:T(8,128)(2,1)S(1)}, u32[]{:S(2)}, u32[]{:S(2)}) collective-permute-start(bf16[8,8192]{1,0:T(8,128)(2,1)} %get-tuple-element.28), channel_id=1, source_target_pairs={{0,32},{1,33},{2,34},{3,35},{4,36},{5,37},{6,38},{7,39},{8,40},{9,... | collective-permute-start | bytes 393224 | tf_op jit(solution)/shard_map/ppermute | solution.py:346
  31.3 6.0 %collective-permute-start.3 = (bf16[1,8,8192]{2,1,0:T(8,128)(2,1)S(1)}, bf16[1,8,8192]{2,1,0:T(8,128)(2,1)S(1)}, u32[]{:S(2)}, u32[]{:S(2)}) collective-permute-start(bf16[1,8,8192]{2,1,0:T(8,128)(2,1)S(1)} %add_bitcast_fusion), channel_id=1, source_target_pairs={{0,2},{1,3},{2,0},{3,1},{4,6},{5,7},{6,4},{7,5},{8,10},{9,11},{10,... | collective-permute-start | bytes 393224 | tf_op jit(solution)/shard_map/ppermute | solution.py:328
  34.7 3.8 %collective-permute-start.2 = (bf16[1,8,8192]{2,1,0:T(8,128)(2,1)S(1)}, bf16[1,8,8192]{2,1,0:T(8,128)(2,1)S(1)}, u32[]{:S(2)}, u32[]{:S(2)}) collective-permute-start(bf16[1,8,8192]{2,1,0:T(8,128)(2,1)S(1)} %add_bitcast_fusion), channel_id=1, source_target_pairs={{0,3},{1,0},{2,1},{3,2},{4,7},{5,4},{6,5},{7,6},{8,11},{9,8},{10,9... | collective-permute-start | bytes 393224 | tf_op jit(solution)/shard_map/ppermute | solution.py:328
  34.7 5.3 %collective-permute-start.1 = (bf16[1,8,8192]{2,1,0:T(8,128)(2,1)S(1)}, bf16[1,8,8192]{2,1,0:T(8,128)(2,1)S(1)}, u32[]{:S(2)}, u32[]{:S(2)}) collective-permute-start(bf16[1,8,8192]{2,1,0:T(8,128)(2,1)S(1)} %add_bitcast_fusion), channel_id=1, source_target_pairs={{0,1},{1,2},{2,3},{3,0},{4,5},{5,6},{6,7},{7,4},{8,9},{9,10},{10,1... | collective-permute-start | bytes 393224 | tf_op jit(solution)/shard_map/ppermute | solution.py:328
  40.1 43.8 %copy-start.4 = (bf16[4,8,8192]{2,1,0:T(8,128)(2,1)}, bf16[4,8,8192]{2,1,0:T(8,128)(2,1)S(1)}, u32[]{:S(2)}) copy-start(bf16[4,8,8192]{2,1,0:T(8,128)(2,1)S(1)} %pad_maximum_fusion) | copy-start | bytes 1572868
  40.1 10.0 %collective-permute-start.7 = (bf16[4,8,8192]{2,1,0:T(8,128)(2,1)S(1)}, bf16[4,8,8192]{2,1,0:T(8,128)(2,1)S(1)}, u32[]{:S(2)}, u32[]{:S(2)}) collective-permute-start(bf16[4,8,8192]{2,1,0:T(8,128)(2,1)S(1)} %pad_maximum_fusion), channel_id=1, source_target_pairs={{0,64},{1,65},{2,66},{3,67},{4,68},{5,69},{6,70},{7,71},{8,72},{9,... | collective-permute-start | bytes 1572872 | tf_op jit(solution)/shard_map/ppermute | solution.py:328
  41.2 13.0 %collective-permute-start.6 = (bf16[4,8,8192]{2,1,0:T(8,128)(2,1)S(1)}, bf16[4,8,8192]{2,1,0:T(8,128)(2,1)}, u32[]{:S(2)}, u32[]{:S(2)}) collective-permute-start(bf16[4,8,8192]{2,1,0:T(8,128)(2,1)S(1)} %pad_maximum_fusion), channel_id=1, source_target_pairs={{0,80},{1,81},{2,82},{3,83},{4,84},{5,85},{6,86},{7,87},{8,88},{9,... | collective-permute-start | bytes 1572872 | tf_op jit(solution)/shard_map/ppermute | solution.py:328
  42.5 13.2 %collective-permute-start.5 = (bf16[4,8,8192]{2,1,0:T(8,128)(2,1)S(1)}, bf16[4,8,8192]{2,1,0:T(8,128)(2,1)}, u32[]{:S(2)}, u32[]{:S(2)}) collective-permute-start(bf16[4,8,8192]{2,1,0:T(8,128)(2,1)S(1)} %pad_maximum_fusion), channel_id=1, source_target_pairs={{0,16},{1,17},{2,18},{3,19},{4,20},{5,21},{6,22},{7,23},{8,24},{9,... | collective-permute-start | bytes 1572872 | tf_op jit(solution)/shard_map/ppermute | solution.py:328
  42.7 13.0 %collective-permute-start.4 = (bf16[4,8,8192]{2,1,0:T(8,128)(2,1)S(1)}, bf16[4,8,8192]{2,1,0:T(8,128)(2,1)}, u32[]{:S(2)}, u32[]{:S(2)}) collective-permute-start(bf16[4,8,8192]{2,1,0:T(8,128)(2,1)S(1)} %pad_maximum_fusion), channel_id=1, source_target_pairs={{0,4},{1,5},{2,6},{3,7},{4,8},{5,9},{6,10},{7,11},{8,12},{9,13},{1... | collective-permute-start | bytes 1572872 | tf_op jit(solution)/shard_map/ppermute | solution.py:361
  43.0 19.5 %collective-permute-start.8 = (bf16[4,8,8192]{2,1,0:T(8,128)(2,1)S(1)}, bf16[4,8,8192]{2,1,0:T(8,128)(2,1)S(1)}, u32[]{:S(2)}, u32[]{:S(2)}) collective-permute-start(bf16[4,8,8192]{2,1,0:T(8,128)(2,1)S(1)} %pad_maximum_fusion), channel_id=1, source_target_pairs={{0,12},{1,13},{2,14},{3,15},{4,0},{5,1},{6,2},{7,3},{8,4},{9,5},{1... | collective-permute-start | bytes 1572872 | tf_op jit(solution)/shard_map/ppermute | solution.py:361
  55.7 19.2 %collective-permute-start.12 = (bf16[4,8,8192]{2,1,0:T(8,128)(2,1)}, bf16[4,8,8192]{2,1,0:T(8,128)(2,1)}, u32[]{:S(2)}, u32[]{:S(2)}) collective-permute-start(bf16[4,8,8192]{2,1,0:T(8,128)(2,1)} %collective-permute-done.4), channel_id=1, source_target_pairs={{0,64},{1,65},{2,66},{3,67},{4,68},{5,69},{6,70},{7,71},{8,72},{9,... | collective-permute-start | bytes 1572872 | tf_op jit(solution)/shard_map/ppermute | solution.py:328
  57.2 17.7 %collective-permute-start.11 = (bf16[4,8,8192]{2,1,0:T(8,128)(2,1)}, bf16[4,8,8192]{2,1,0:T(8,128)(2,1)}, u32[]{:S(2)}, u32[]{:S(2)}) collective-permute-start(bf16[4,8,8192]{2,1,0:T(8,128)(2,1)} %collective-permute-done.4), channel_id=1, source_target_pairs={{0,80},{1,81},{2,82},{3,83},{4,84},{5,85},{6,86},{7,87},{8,88},{9,... | collective-permute-start | bytes 1572872 | tf_op jit(solution)/shard_map/ppermute | solution.py:328
  58.5 16.9 %collective-permute-start.10 = (bf16[4,8,8192]{2,1,0:T(8,128)(2,1)}, bf16[4,8,8192]{2,1,0:T(8,128)(2,1)}, u32[]{:S(2)}, u32[]{:S(2)}) collective-permute-start(bf16[4,8,8192]{2,1,0:T(8,128)(2,1)} %collective-permute-done.4), channel_id=1, source_target_pairs={{0,16},{1,17},{2,18},{3,19},{4,20},{5,21},{6,22},{7,23},{8,24},{9,... | collective-permute-start | bytes 1572872 | tf_op jit(solution)/shard_map/ppermute | solution.py:328
  59.1 10.7 %collective-permute-start.9 = (bf16[4,8,8192]{2,1,0:T(8,128)(2,1)S(1)}, bf16[4,8,8192]{2,1,0:T(8,128)(2,1)S(1)}, u32[]{:S(2)}, u32[]{:S(2)}) collective-permute-start(bf16[4,8,8192]{2,1,0:T(8,128)(2,1)S(1)} %pad_maximum_fusion), channel_id=1, source_target_pairs={{0,8},{1,9},{2,10},{3,11},{4,12},{5,13},{6,14},{7,15},{8,0},{9,1},... | collective-permute-start | bytes 1572872 | tf_op jit(solution)/shard_map/ppermute | solution.py:361
  62.5 13.0 %collective-permute-start.13 = (bf16[4,8,8192]{2,1,0:T(8,128)(2,1)S(1)}, bf16[4,8,8192]{2,1,0:T(8,128)(2,1)S(1)}, u32[]{:S(2)}, u32[]{:S(2)}) collective-permute-start(bf16[4,8,8192]{2,1,0:T(8,128)(2,1)S(1)} %pad_maximum_fusion), channel_id=1, source_target_pairs={{0,32},{1,33},{2,34},{3,35},{4,36},{5,37},{6,38},{7,39},{8,40},{9,... | collective-permute-start | bytes 1572872 | tf_op jit(solution)/shard_map/ppermute | solution.py:364
  69.8 6.9 %collective-permute-start.14 = (bf16[4,8,8192]{2,1,0:T(8,128)(2,1)}, bf16[4,8,8192]{2,1,0:T(8,128)(2,1)S(1)}, u32[]{:S(2)}, u32[]{:S(2)}) collective-permute-start(bf16[4,8,8192]{2,1,0:T(8,128)(2,1)} %collective-permute-done.5), channel_id=1, source_target_pairs={{0,32},{1,33},{2,34},{3,35},{4,36},{5,37},{6,38},{7,39},{8,40},{9,... | collective-permute-start | bytes 1572872 | tf_op jit(solution)/shard_map/ppermute | solution.py:364
  74.9 3.2 %collective-permute-start.15 = (bf16[4,8,8192]{2,1,0:T(8,128)(2,1)}, bf16[4,8,8192]{2,1,0:T(8,128)(2,1)S(1)}, u32[]{:S(2)}, u32[]{:S(2)}) collective-permute-start(bf16[4,8,8192]{2,1,0:T(8,128)(2,1)} %collective-permute-done.6), channel_id=1, source_target_pairs={{0,32},{1,33},{2,34},{3,35},{4,36},{5,37},{6,38},{7,39},{8,40},{9,... | collective-permute-start | bytes 1572872 | tf_op jit(solution)/shard_map/ppermute | solution.py:364
  74.9 3.7 %collective-permute-start.16 = (bf16[4,8,8192]{2,1,0:T(8,128)(2,1)S(1)}, bf16[4,8,8192]{2,1,0:T(8,128)(2,1)S(1)}, u32[]{:S(2)}, u32[]{:S(2)}) collective-permute-start(bf16[4,8,8192]{2,1,0:T(8,128)(2,1)S(1)} %collective-permute-done.7), channel_id=1, source_target_pairs={{0,32},{1,33},{2,34},{3,35},{4,36},{5,37},{6,38},{7,39},{8,40},{9,... | collective-permute-start | bytes 1572872 | tf_op jit(solution)/shard_map/ppermute | solution.py:364
  75.4 3.5 %collective-permute-start.17 = (bf16[4,8,8192]{2,1,0:T(8,128)(2,1)}, bf16[4,8,8192]{2,1,0:T(8,128)(2,1)S(1)}, u32[]{:S(2)}, u32[]{:S(2)}) collective-permute-start(bf16[4,8,8192]{2,1,0:T(8,128)(2,1)} %collective-permute-done.4), channel_id=1, source_target_pairs={{0,32},{1,33},{2,34},{3,35},{4,36},{5,37},{6,38},{7,39},{8,40},{9,... | collective-permute-start | bytes 1572872 | tf_op jit(solution)/shard_map/ppermute | solution.py:364
  75.6 5.4 %collective-permute-start.18 = (bf16[4,8,8192]{2,1,0:T(8,128)(2,1)}, bf16[4,8,8192]{2,1,0:T(8,128)(2,1)S(1)}, u32[]{:S(2)}, u32[]{:S(2)}) collective-permute-start(bf16[4,8,8192]{2,1,0:T(8,128)(2,1)} %collective-permute-done.10), channel_id=1, source_target_pairs={{0,32},{1,33},{2,34},{3,35},{4,36},{5,37},{6,38},{7,39},{8,40},{9,... | collective-permute-start | bytes 1572872 | tf_op jit(solution)/shard_map/ppermute | solution.py:364
  76.7 6.1 %collective-permute-start.19 = (bf16[4,8,8192]{2,1,0:T(8,128)(2,1)}, bf16[4,8,8192]{2,1,0:T(8,128)(2,1)S(1)}, u32[]{:S(2)}, u32[]{:S(2)}) collective-permute-start(bf16[4,8,8192]{2,1,0:T(8,128)(2,1)} %collective-permute-done.11), channel_id=1, source_target_pairs={{0,32},{1,33},{2,34},{3,35},{4,36},{5,37},{6,38},{7,39},{8,40},{9,... | collective-permute-start | bytes 1572872 | tf_op jit(solution)/shard_map/ppermute | solution.py:364
  78.2 4.9 %collective-permute-start.20 = (bf16[4,8,8192]{2,1,0:T(8,128)(2,1)}, bf16[4,8,8192]{2,1,0:T(8,128)(2,1)S(1)}, u32[]{:S(2)}, u32[]{:S(2)}) collective-permute-start(bf16[4,8,8192]{2,1,0:T(8,128)(2,1)} %collective-permute-done.12), channel_id=1, source_target_pairs={{0,32},{1,33},{2,34},{3,35},{4,36},{5,37},{6,38},{7,39},{8,40},{9,... | collective-permute-start | bytes 1572872 | tf_op jit(solution)/shard_map/ppermute | solution.py:364
  78.6 22.1 %collective-permute-start.23 = (bf16[4,8,8192]{2,1,0:T(8,128)(2,1)S(1)}, bf16[4,8,8192]{2,1,0:T(8,128)(2,1)S(1)}, u32[]{:S(2)}, u32[]{:S(2)}) collective-permute-start(bf16[4,8,8192]{2,1,0:T(8,128)(2,1)S(1)} %collective-permute-done.7), channel_id=1, source_target_pairs={{0,12},{1,13},{2,14},{3,15},{4,0},{5,1},{6,2},{7,3},{8,4},{9,5},{1... | collective-permute-start | bytes 1572872 | tf_op jit(solution)/shard_map/ppermute | solution.py:361
  78.9 21.8 %collective-permute-start.24 = (bf16[4,8,8192]{2,1,0:T(8,128)(2,1)S(1)}, bf16[4,8,8192]{2,1,0:T(8,128)(2,1)}, u32[]{:S(2)}, u32[]{:S(2)}) collective-permute-start(bf16[4,8,8192]{2,1,0:T(8,128)(2,1)S(1)} %collective-permute-done.9), channel_id=1, source_target_pairs={{0,64},{1,65},{2,66},{3,67},{4,68},{5,69},{6,70},{7,71},{8,72},{9,... | collective-permute-start | bytes 1572872 | tf_op jit(solution)/shard_map/ppermute | solution.py:380
  81.0 19.7 %collective-permute-start.22 = (bf16[8,8,8192]{2,1,0:T(8,128)(2,1)S(1)}, bf16[8,8,8192]{2,1,0:T(8,128)(2,1)}, u32[]{:S(2)}, u32[]{:S(2)}) collective-permute-start(bf16[8,8,8192]{2,1,0:T(8,128)(2,1)S(1)} %constant_dynamic-update-slice_fusion), channel_id=1, source_target_pairs={{0,80},{1,81},{2,82},{3,83},{4,84},{5,85},{6,86},{7,87},{8,88},{9,... | collective-permute-start | bytes 3145736 | tf_op jit(solution)/shard_map/ppermute | solution.py:379
  82.8 17.9 %collective-permute-start.21 = (bf16[8,8,8192]{2,1,0:T(8,128)(2,1)S(1)}, bf16[8,8,8192]{2,1,0:T(8,128)(2,1)}, u32[]{:S(2)}, u32[]{:S(2)}) collective-permute-start(bf16[8,8,8192]{2,1,0:T(8,128)(2,1)S(1)} %constant_dynamic-update-slice_fusion), channel_id=1, source_target_pairs={{0,16},{1,17},{2,18},{3,19},{4,20},{5,21},{6,22},{7,23},{8,24},{9,... | collective-permute-start | bytes 3145736 | tf_op jit(solution)/shard_map/ppermute | solution.py:379
  100.7 9.8 %collective-permute-start.25 = (bf16[8,8,8192]{2,1,0:T(8,128)(2,1)S(1)}, bf16[8,8,8192]{2,1,0:T(8,128)(2,1)S(1)}, u32[]{:S(2)}, u32[]{:S(2)}) collective-permute-start(bf16[8,8,8192]{2,1,0:T(8,128)(2,1)S(1)} %constant_dynamic-update-slice_fusion), channel_id=1, source_target_pairs={{0,32},{1,33},{2,34},{3,35},{4,36},{5,37},{6,38},{7,39},{8,40},{9,... | collective-permute-start | bytes 3145736 | tf_op jit(solution)/shard_map/ppermute | solution.py:364
  103.4 7.1 %collective-permute-start.26 = (bf16[8,8,8192]{2,1,0:T(8,128)(2,1)}, bf16[8,8,8192]{2,1,0:T(8,128)(2,1)}, u32[]{:S(2)}, u32[]{:S(2)}) collective-permute-start(bf16[8,8,8192]{2,1,0:T(8,128)(2,1)} %collective-permute-done.21), channel_id=1, source_target_pairs={{0,32},{1,33},{2,34},{3,35},{4,36},{5,37},{6,38},{7,39},{8,40},{9,... | collective-permute-start | bytes 3145736 | tf_op jit(solution)/shard_map/ppermute | solution.py:364
  103.4 7.0 %collective-permute-start.27 = (bf16[8,8,8192]{2,1,0:T(8,128)(2,1)}, bf16[8,8,8192]{2,1,0:T(8,128)(2,1)}, u32[]{:S(2)}, u32[]{:S(2)}) collective-permute-start(bf16[8,8,8192]{2,1,0:T(8,128)(2,1)} %collective-permute-done.22), channel_id=1, source_target_pairs={{0,32},{1,33},{2,34},{3,35},{4,36},{5,37},{6,38},{7,39},{8,40},{9,... | collective-permute-start | bytes 3145736 | tf_op jit(solution)/shard_map/ppermute | solution.py:364
  103.9 3.8 %collective-permute-start.28 = (bf16[4,8,8192]{2,1,0:T(8,128)(2,1)S(1)}, bf16[4,8,8192]{2,1,0:T(8,128)(2,1)S(1)}, u32[]{:S(2)}, u32[]{:S(2)}) collective-permute-start(bf16[4,8,8192]{2,1,0:T(8,128)(2,1)S(1)} %collective-permute-done.23), channel_id=1, source_target_pairs={{0,32},{1,33},{2,34},{3,35},{4,36},{5,37},{6,38},{7,39},{8,40},{9,... | collective-permute-start | bytes 1572872 | tf_op jit(solution)/shard_map/ppermute | solution.py:364
  104.0 6.5 %collective-permute-start.29 = (bf16[4,8,8192]{2,1,0:T(8,128)(2,1)}, bf16[4,8,8192]{2,1,0:T(8,128)(2,1)}, u32[]{:S(2)}, u32[]{:S(2)}) collective-permute-start(bf16[4,8,8192]{2,1,0:T(8,128)(2,1)} %collective-permute-done.24), channel_id=1, source_target_pairs={{0,32},{1,33},{2,34},{3,35},{4,36},{5,37},{6,38},{7,39},{8,40},{9,... | collective-permute-start | bytes 1572872 | tf_op jit(solution)/shard_map/ppermute | solution.py:364
  (19 other events, 183.5 us)

commit v4 on v3

--- a/solution.py
+++ b/solution.py
@@ -237,8 +237,7 @@
             sems.at[1],
         )
 
-    @pl.loop(0, 2 * planes)
-    def _(q):
+    for q in range(2 * planes):
         x = x_scr[q].reshape(512, 2 * BINS)
 
         def put(lag, y):
@@ -261,8 +260,7 @@
         put(2, jnp.dot(d_scr[...], flip[:, 256:], preferred_element_type=jnp.float32))
         put(0, jnp.dot(d_scr[:, 256:], flip[256:, :256], preferred_element_type=jnp.float32))
 
-        @pl.loop(0, 32)
-        def _(n):
+        for n in range(32):
             copy(q, n).start()
 
     pltpu.make_async_copy(yb, out.at[pl.ds(0, sources * CH_DEV)], sems.at[1]).wait()
@@ -379,9 +377,12 @@
     rest = [both] + [lax.ppermute(both, AXES, line_pairs("zx", s)) for s in (1, -1)]
     across_far = lax.ppermute(across, AXES, line_pairs("zx", 2))
     second_sib = swap(second)
+    both_sib = swap([both, behind_far])
     out = corr(places((0, -1)), rows, flat(first + second), flat(first_sib + second_sib), inverse, None)
     out, *rest = after((out, *rest, behind_far, across_far))
-    out = corr(places((1, 2)), rows, flat(rest), flat(swap(rest)), inverse, out)
+    far = swap([rest[1], rest[2], rest[4]])
+    rest_sib = [both_sib[0], far[0], far[1], both_sib[1], far[2]]
+    out = corr(places((1, 2)), rows, flat(rest), flat(rest_sib), inverse, out)
     return out.reshape(1, STEPS * 256, CH_DEV, NLAG)
 
 

time: 129 us -> 125 us (0.969)
  Pallas kernels: 40.6 us -> 37.8 us
    pallas_call x2, Pallas kernels: 33.5 us -> 30.8 us  [corr(): pl.pallas_call(lambda *refs: corr_kernel(first, planes, len(mine), *refs)...]
where the time goes in v4:
time: 125 us; the launch traced here: 124 us
  starting transfers between devices  45.6 us (36%)
  Pallas kernels  37.8 us (30%)
  waiting for transfers between devices  29.2 us (23%)
  local copies, waits for them, and re-layouts  5.62 us (4%)
  other arithmetic  3.97 us (3%)
  matrix products  1.66 us (1%)
    pallas_call x2, Pallas kernels, corr(): pl.pallas_call(lambda *refs: corr_kernel(first, planes, len(mine), *refs)...  30.8 us
    ppermute x13, starting transfers between devices, swap(): return [lax.ppermute(x, AXES, CORE_PAIRS) for x in xs]  16.2 us
    ppermute x9, waiting for transfers between devices, line(): lax.ppermute(block, AXES, line_pairs(axes, s))  13.8 us
    ppermute x9, starting transfers between devices, line(): lax.ppermute(block, AXES, line_pairs(axes, s))  10.8 us
    all_to_all x1, starting transfers between devices, local(): lax.all_to_all(ordered.reshape(32, 8, 512), 'dev', split_axis=0, concat_a...  9.22 us
    pallas_call x1, Pallas kernels, front(): pl.pallas_call(front_kernel, out_shape=(jax.ShapeDtypeStruct((CH_DEV, WID...  6.63 us
    all_to_all x1, waiting for transfers between devices, local(): lax.all_to_all(ordered.reshape(32, 8, 512), 'dev', split_axis=0, concat_a...  6.5 us
    ppermute x13, waiting for transfers between devices, swap(): return [lax.ppermute(x, AXES, CORE_PAIRS) for x in xs]  6.11 us
  transfers between devices with their start and end apart: 31, of which 14 were waited for; matrix products, arithmetic and copies ran while one was open for 3% of the time, Pallas kernels for 13%

profile of v4, /device:TPU:1, one launch (start us, length us, event | category | flops | bytes accessed | tf_op | source)
XLA Modules:
  0.0 124.4 jit_solution(14340155192778455364)
XLA Ops:
  1.0 1.7 %fusion = bf16[32,8,512]{2,1,0:T(8,128)(2,1)} fusion(bf16[256,512]{1,0:T(8,128)(2,1)S(1)} %copy-done, s32[256]{0:T(256)} %bitcast.42), kind=kOutput, calls=%fused_computation.1 | convolution fusion | flops 67305472 | bytes 525312 | tf_op jit(solution)/shard_map/dot_general | solution.py:337
  2.6 9.2 %all-to-all-start = ((bf16[32,8,512]{2,1,0:T(8,128)(2,1)}), bf16[32,8,512]{2,1,0:T(8,128)(2,1)S(1)}, u32[]{:S(2)}, u32[]{:S(2)}) async-start(bf16[32,8,512]{2,1,0:T(8,128)(2,1)} %fusion), calls=%async_computation | async-start | bytes 524288 | tf_op jit(solution)/shard_map/all_to_all | solution.py:338
  13.2 6.5 %all-to-all-done = bf16[32,8,512]{2,1,0:T(8,128)(2,1)S(1)} async-done(((bf16[32,8,512]{2,1,0:T(8,128)(2,1)}), bf16[32,8,512]{2,1,0:T(8,128)(2,1)S(1)}, u32[]{:S(2)}, u32[]{:S(2)}) %all-to-all-start) | async-done | bytes 262176 | tf_op jit(solution)/shard_map/all_to_all | solution.py:338
  20.4 6.6 %front.1 = (bf16[8,16384]{1,0:T(8,128)(2,1)}, bf16[8,8192]{1,0:T(8,128)(2,1)}, bf16[8,8192]{1,0:T(8,128)(2,1)}) custom-call(s32[3]{0:T(128)} %pad_add_fusion.2.meta, bf16[8,4,8,512]{3,2,1,0:T(8,128)(2,1)} %bitcast.39, bf16[2048,2048]{1,0:T(8,128)(2,1)} %constant.146.clone.table_hbm), custom_call_target="tpu_custom_call" | custom-call | tf_op jit(solution)/shard_map/front/pallas_call | solution.py:105
  27.0 2.2 %collective-permute-start = (bf16[8,8192]{1,0:T(8,128)(2,1)}, bf16[8,8192]{1,0:T(8,128)(2,1)S(1)}, u32[]{:S(2)}, u32[]{:S(2)}) collective-permute-start(bf16[8,8192]{1,0:T(8,128)(2,1)} %get-tuple-element.28), channel_id=1, source_target_pairs={{0,32},{1,33},{2,34},{3,35},{4,36},{5,37},{6,38},{7,39},{8,40},{9,... | collective-permute-start | bytes 393224 | tf_op jit(solution)/shard_map/ppermute | solution.py:344
  29.2 1.2 collective-permute-done
  31.3 3.4 %collective-permute-start.3 = (bf16[1,8,8192]{2,1,0:T(8,128)(2,1)S(1)}, bf16[1,8,8192]{2,1,0:T(8,128)(2,1)S(1)}, u32[]{:S(2)}, u32[]{:S(2)}) collective-permute-start(bf16[1,8,8192]{2,1,0:T(8,128)(2,1)S(1)} %add_bitcast_fusion), channel_id=1, source_target_pairs={{0,2},{1,3},{2,0},{3,1},{4,6},{5,7},{6,4},{7,5},{8,10},{9,11},{10,... | collective-permute-start | bytes 393224 | tf_op jit(solution)/shard_map/ppermute | solution.py:326
  34.7 1.5 %collective-permute-start.1 = (bf16[1,8,8192]{2,1,0:T(8,128)(2,1)S(1)}, bf16[1,8,8192]{2,1,0:T(8,128)(2,1)S(1)}, u32[]{:S(2)}, u32[]{:S(2)}) collective-permute-start(bf16[1,8,8192]{2,1,0:T(8,128)(2,1)S(1)} %add_bitcast_fusion), channel_id=1, source_target_pairs={{0,1},{1,2},{2,3},{3,0},{4,5},{5,6},{6,7},{7,4},{8,9},{9,10},{10,1... | collective-permute-start | bytes 393224 | tf_op jit(solution)/shard_map/ppermute | solution.py:326
  36.3 1.1 collective-permute-done.3
  37.4 1.2 collective-permute-done.2
  38.5 1.5 %collective-permute-done.1 = bf16[1,8,8192]{2,1,0:T(8,128)(2,1)S(1)} collective-permute-done((bf16[1,8,8192]{2,1,0:T(8,128)(2,1)S(1)}, bf16[1,8,8192]{2,1,0:T(8,128)(2,1)S(1)}, u32[]{:S(2)}, u32[]{:S(2)}) %collective-permute-start.1) | collective-permute-done | bytes 131104 | tf_op jit(solution)/shard_map/ppermute | solution.py:326
  40.1 1.1 collective-permute-start.7
  41.2 1.3 %collective-permute-start.6 = (bf16[4,8,8192]{2,1,0:T(8,128)(2,1)S(1)}, bf16[4,8,8192]{2,1,0:T(8,128)(2,1)}, u32[]{:S(2)}, u32[]{:S(2)}) collective-permute-start(bf16[4,8,8192]{2,1,0:T(8,128)(2,1)S(1)} %pad_maximum_fusion), channel_id=1, source_target_pairs={{0,80},{1,81},{2,82},{3,83},{4,84},{5,85},{6,86},{7,87},{8,88},{9,... | collective-permute-start | bytes 1572872 | tf_op jit(solution)/shard_map/ppermute | solution.py:326
  43.0 2.7 %collective-permute-start.8 = (bf16[4,8,8192]{2,1,0:T(8,128)(2,1)S(1)}, bf16[4,8,8192]{2,1,0:T(8,128)(2,1)S(1)}, u32[]{:S(2)}, u32[]{:S(2)}) collective-permute-start(bf16[4,8,8192]{2,1,0:T(8,128)(2,1)S(1)} %pad_maximum_fusion), channel_id=1, source_target_pairs={{0,12},{1,13},{2,14},{3,15},{4,0},{5,1},{6,2},{7,3},{8,4},{9,5},{1... | collective-permute-start | bytes 1572872 | tf_op jit(solution)/shard_map/ppermute | solution.py:359
  45.7 4.3 %collective-permute-done.7 = bf16[4,8,8192]{2,1,0:T(8,128)(2,1)S(1)} collective-permute-done((bf16[4,8,8192]{2,1,0:T(8,128)(2,1)S(1)}, bf16[4,8,8192]{2,1,0:T(8,128)(2,1)S(1)}, u32[]{:S(2)}, u32[]{:S(2)}) %collective-permute-start.7) | collective-permute-done | bytes 524320 | tf_op jit(solution)/shard_map/ppermute | solution.py:326
  50.1 4.2 %collective-permute-done.6 = bf16[4,8,8192]{2,1,0:T(8,128)(2,1)} collective-permute-done((bf16[4,8,8192]{2,1,0:T(8,128)(2,1)S(1)}, bf16[4,8,8192]{2,1,0:T(8,128)(2,1)}, u32[]{:S(2)}, u32[]{:S(2)}) %collective-permute-start.6) | collective-permute-done | bytes 524320 | tf_op jit(solution)/shard_map/ppermute | solution.py:326
  54.3 1.5 %collective-permute-done.5 = bf16[4,8,8192]{2,1,0:T(8,128)(2,1)} collective-permute-done((bf16[4,8,8192]{2,1,0:T(8,128)(2,1)S(1)}, bf16[4,8,8192]{2,1,0:T(8,128)(2,1)}, u32[]{:S(2)}, u32[]{:S(2)}) %collective-permute-start.5) | collective-permute-done | bytes 524320 | tf_op jit(solution)/shard_map/ppermute | solution.py:326
  55.7 1.5 %collective-permute-start.12 = (bf16[4,8,8192]{2,1,0:T(8,128)(2,1)}, bf16[4,8,8192]{2,1,0:T(8,128)(2,1)}, u32[]{:S(2)}, u32[]{:S(2)}) collective-permute-start(bf16[4,8,8192]{2,1,0:T(8,128)(2,1)} %collective-permute-done.4), channel_id=1, source_target_pairs={{0,64},{1,65},{2,66},{3,67},{4,68},{5,69},{6,70},{7,71},{8,72},{9,... | collective-permute-start | bytes 1572872 | tf_op jit(solution)/shard_map/ppermute | solution.py:326
  57.2 1.3 %collective-permute-start.11 = (bf16[4,8,8192]{2,1,0:T(8,128)(2,1)}, bf16[4,8,8192]{2,1,0:T(8,128)(2,1)}, u32[]{:S(2)}, u32[]{:S(2)}) collective-permute-start(bf16[4,8,8192]{2,1,0:T(8,128)(2,1)} %collective-permute-done.4), channel_id=1, source_target_pairs={{0,80},{1,81},{2,82},{3,83},{4,84},{5,85},{6,86},{7,87},{8,88},{9,... | collective-permute-start | bytes 1572872 | tf_op jit(solution)/shard_map/ppermute | solution.py:326
  60.1 0.9 copy-done.2
  61.5 1.0 copy-done.1
  62.5 5.7 %collective-permute-start.13 = (bf16[4,8,8192]{2,1,0:T(8,128)(2,1)S(1)}, bf16[4,8,8192]{2,1,0:T(8,128)(2,1)S(1)}, u32[]{:S(2)}, u32[]{:S(2)}) collective-permute-start(bf16[4,8,8192]{2,1,0:T(8,128)(2,1)S(1)} %pad_maximum_fusion), channel_id=1, source_target_pairs={{0,32},{1,33},{2,34},{3,35},{4,36},{5,37},{6,38},{7,39},{8,40},{9,... | collective-permute-start | bytes 1572872 | tf_op jit(solution)/shard_map/ppermute | solution.py:362
  68.2 1.6 %collective-permute-done.9 = bf16[4,8,8192]{2,1,0:T(8,128)(2,1)S(1)} collective-permute-done((bf16[4,8,8192]{2,1,0:T(8,128)(2,1)S(1)}, bf16[4,8,8192]{2,1,0:T(8,128)(2,1)S(1)}, u32[]{:S(2)}, u32[]{:S(2)}) %collective-permute-start.9) | collective-permute-done | bytes 524320 | tf_op jit(solution)/shard_map/ppermute | solution.py:359
  69.8 5.1 %collective-permute-start.14 = (bf16[4,8,8192]{2,1,0:T(8,128)(2,1)}, bf16[4,8,8192]{2,1,0:T(8,128)(2,1)S(1)}, u32[]{:S(2)}, u32[]{:S(2)}) collective-permute-start(bf16[4,8,8192]{2,1,0:T(8,128)(2,1)} %collective-permute-done.5), channel_id=1, source_target_pairs={{0,32},{1,33},{2,34},{3,35},{4,36},{5,37},{6,38},{7,39},{8,40},{9,... | collective-permute-start | bytes 1572872 | tf_op jit(solution)/shard_map/ppermute | solution.py:362
  77.0 1.1 collective-permute-done.15
  78.9 2.1 %collective-permute-start.24 = (bf16[4,8,8192]{2,1,0:T(8,128)(2,1)S(1)}, bf16[4,8,8192]{2,1,0:T(8,128)(2,1)}, u32[]{:S(2)}, u32[]{:S(2)}) collective-permute-start(bf16[4,8,8192]{2,1,0:T(8,128)(2,1)S(1)} %collective-permute-done.9), channel_id=1, source_target_pairs={{0,64},{1,65},{2,66},{3,67},{4,68},{5,69},{6,70},{7,71},{8,72},{9,... | collective-permute-start | bytes 1572872 | tf_op jit(solution)/shard_map/ppermute | solution.py:378
  81.0 2.4 %collective-permute-start.25 = (bf16[8,8,8192]{2,1,0:T(8,128)(2,1)S(1)}, bf16[8,8,8192]{2,1,0:T(8,128)(2,1)}, u32[]{:S(2)}, u32[]{:S(2)}) collective-permute-start(bf16[8,8,8192]{2,1,0:T(8,128)(2,1)S(1)} %constant_dynamic-update-slice_fusion), channel_id=1, source_target_pairs={{0,32},{1,33},{2,34},{3,35},{4,36},{5,37},{6,38},{7,39},{8,40},{9,... | collective-permute-start | bytes 3145736 | tf_op jit(solution)/shard_map/ppermute | solution.py:362
  83.4 2.1 %collective-permute-start.22 = (bf16[8,8,8192]{2,1,0:T(8,128)(2,1)S(1)}, bf16[8,8,8192]{2,1,0:T(8,128)(2,1)}, u32[]{:S(2)}, u32[]{:S(2)}) collective-permute-start(bf16[8,8,8192]{2,1,0:T(8,128)(2,1)S(1)} %constant_dynamic-update-slice_fusion), channel_id=1, source_target_pairs={{0,80},{1,81},{2,82},{3,83},{4,84},{5,85},{6,86},{7,87},{8,88},{9,... | collective-permute-start | bytes 3145736 | tf_op jit(solution)/shard_map/ppermute | solution.py:377
  86.3 15.4 %corr.2.refs_13_ = bf16[4096,1024]{1,0:T(8,128)(2,1)} custom-call(s32[129]{0:T(256)} %pad_add_fusion.refs_0_, bf16[32,16384]{1,0:T(8,128)(2,1)} %copy-done.1, bf16[32,8192]{1,0:T(8,128)(2,1)} %bitcast.40, bf16[32,8192]{1,0:T(8,128)(2,1)} %bitcast.7.refs_3_, bf16[32,8192]{1,0:T(8,128)(2,1)} %bitcast.8.refs_4_, bf16[32,8192]{1,0:T(8,128)(2,1)} %bitcast.44, ...), custom_call_target="tpu_custom_call" | custom-call | flops 21474836480 | bytes 12582912 | tf_op jit(solution)/shard_map/corr/pallas_call | solution.py:274
  103.7 2.9 %collective-permute-done.28 = bf16[4,8,8192]{2,1,0:T(8,128)(2,1)S(1)} collective-permute-done((bf16[4,8,8192]{2,1,0:T(8,128)(2,1)S(1)}, bf16[4,8,8192]{2,1,0:T(8,128)(2,1)S(1)}, u32[]{:S(2)}, u32[]{:S(2)}) %collective-permute-start.28) | collective-permute-done | bytes 524320 | tf_op jit(solution)/shard_map/ppermute | solution.py:362
  106.6 1.3 %collective-permute-done.29 = bf16[4,8,8192]{2,1,0:T(8,128)(2,1)} collective-permute-done((bf16[4,8,8192]{2,1,0:T(8,128)(2,1)}, bf16[4,8,8192]{2,1,0:T(8,128)(2,1)}, u32[]{:S(2)}, u32[]{:S(2)}) %collective-permute-start.29) | collective-permute-done | bytes 524320 | tf_op jit(solution)/shard_map/ppermute | solution.py:362
  108.9 15.4 %corr.3 = bf16[4096,1024]{1,0:T(8,128)(2,1)} custom-call(s32[129]{0:T(256)} %pad_add_fusion.1.refs_0_, bf16[32,16384]{1,0:T(8,128)(2,1)} %copy-done.1, bf16[64,8192]{1,0:T(8,128)(2,1)} %bitcast.41, bf16[64,8192]{1,0:T(8,128)(2,1)} %bitcast.23.refs_3_, bf16[64,8192]{1,0:T(8,128)(2,1)} %bitcast.24.refs_4_, ...), custom_call_target="tpu_custom_call", output_to_operand_aliasing={{}: (13, {})} | custom-call | flops 21474836480 | bytes 12582912 | tf_op jit(solution)/shard_map/corr/pallas_call | solution.py:274
  (94 shorter events, 13.0 us)
Async XLA Ops:
  2.6 17.1 %all-to-all-start = ((bf16[32,8,512]{2,1,0:T(8,128)(2,1)}), bf16[32,8,512]{2,1,0:T(8,128)(2,1)S(1)}, u32[]{:S(2)}, u32[]{:S(2)}) async-start(bf16[32,8,512]{2,1,0:T(8,128)(2,1)} %fusion), calls=%async_computation | async-start | bytes 524288 | tf_op jit(solution)/shard_map/all_to_all | solution.py:338
  27.0 3.4 %collective-permute-start = (bf16[8,8192]{1,0:T(8,128)(2,1)}, bf16[8,8192]{1,0:T(8,128)(2,1)S(1)}, u32[]{:S(2)}, u32[]{:S(2)}) collective-permute-start(bf16[8,8192]{1,0:T(8,128)(2,1)} %get-tuple-element.28), channel_id=1, source_target_pairs={{0,32},{1,33},{2,34},{3,35},{4,36},{5,37},{6,38},{7,39},{8,40},{9,... | collective-permute-start | bytes 393224 | tf_op jit(solution)/shard_map/ppermute | solution.py:344
  31.3 6.0 %collective-permute-start.3 = (bf16[1,8,8192]{2,1,0:T(8,128)(2,1)S(1)}, bf16[1,8,8192]{2,1,0:T(8,128)(2,1)S(1)}, u32[]{:S(2)}, u32[]{:S(2)}) collective-permute-start(bf16[1,8,8192]{2,1,0:T(8,128)(2,1)S(1)} %add_bitcast_fusion), channel_id=1, source_target_pairs={{0,2},{1,3},{2,0},{3,1},{4,6},{5,7},{6,4},{7,5},{8,10},{9,11},{10,... | collective-permute-start | bytes 393224 | tf_op jit(solution)/shard_map/ppermute | solution.py:326
  34.7 3.8 %collective-permute-start.2 = (bf16[1,8,8192]{2,1,0:T(8,128)(2,1)S(1)}, bf16[1,8,8192]{2,1,0:T(8,128)(2,1)S(1)}, u32[]{:S(2)}, u32[]{:S(2)}) collective-permute-start(bf16[1,8,8192]{2,1,0:T(8,128)(2,1)S(1)} %add_bitcast_fusion), channel_id=1, source_target_pairs={{0,3},{1,0},{2,1},{3,2},{4,7},{5,4},{6,5},{7,6},{8,11},{9,8},{10,9... | collective-permute-start | bytes 393224 | tf_op jit(solution)/shard_map/ppermute | solution.py:326
  34.7 5.3 %collective-permute-start.1 = (bf16[1,8,8192]{2,1,0:T(8,128)(2,1)S(1)}, bf16[1,8,8192]{2,1,0:T(8,128)(2,1)S(1)}, u32[]{:S(2)}, u32[]{:S(2)}) collective-permute-start(bf16[1,8,8192]{2,1,0:T(8,128)(2,1)S(1)} %add_bitcast_fusion), channel_id=1, source_target_pairs={{0,1},{1,2},{2,3},{3,0},{4,5},{5,6},{6,7},{7,4},{8,9},{9,10},{10,1... | collective-permute-start | bytes 393224 | tf_op jit(solution)/shard_map/ppermute | solution.py:326
  40.1 46.2 %copy-start.4 = (bf16[4,8,8192]{2,1,0:T(8,128)(2,1)}, bf16[4,8,8192]{2,1,0:T(8,128)(2,1)S(1)}, u32[]{:S(2)}) copy-start(bf16[4,8,8192]{2,1,0:T(8,128)(2,1)S(1)} %pad_maximum_fusion) | copy-start | bytes 1572868
  40.1 10.0 %collective-permute-start.7 = (bf16[4,8,8192]{2,1,0:T(8,128)(2,1)S(1)}, bf16[4,8,8192]{2,1,0:T(8,128)(2,1)S(1)}, u32[]{:S(2)}, u32[]{:S(2)}) collective-permute-start(bf16[4,8,8192]{2,1,0:T(8,128)(2,1)S(1)} %pad_maximum_fusion), channel_id=1, source_target_pairs={{0,64},{1,65},{2,66},{3,67},{4,68},{5,69},{6,70},{7,71},{8,72},{9,... | collective-permute-start | bytes 1572872 | tf_op jit(solution)/shard_map/ppermute | solution.py:326
  41.2 13.0 %collective-permute-start.6 = (bf16[4,8,8192]{2,1,0:T(8,128)(2,1)S(1)}, bf16[4,8,8192]{2,1,0:T(8,128)(2,1)}, u32[]{:S(2)}, u32[]{:S(2)}) collective-permute-start(bf16[4,8,8192]{2,1,0:T(8,128)(2,1)S(1)} %pad_maximum_fusion), channel_id=1, source_target_pairs={{0,80},{1,81},{2,82},{3,83},{4,84},{5,85},{6,86},{7,87},{8,88},{9,... | collective-permute-start | bytes 1572872 | tf_op jit(solution)/shard_map/ppermute | solution.py:326
  42.5 13.2 %collective-permute-start.5 = (bf16[4,8,8192]{2,1,0:T(8,128)(2,1)S(1)}, bf16[4,8,8192]{2,1,0:T(8,128)(2,1)}, u32[]{:S(2)}, u32[]{:S(2)}) collective-permute-start(bf16[4,8,8192]{2,1,0:T(8,128)(2,1)S(1)} %pad_maximum_fusion), channel_id=1, source_target_pairs={{0,16},{1,17},{2,18},{3,19},{4,20},{5,21},{6,22},{7,23},{8,24},{9,... | collective-permute-start | bytes 1572872 | tf_op jit(solution)/shard_map/ppermute | solution.py:326
  42.7 13.0 %collective-permute-start.4 = (bf16[4,8,8192]{2,1,0:T(8,128)(2,1)S(1)}, bf16[4,8,8192]{2,1,0:T(8,128)(2,1)}, u32[]{:S(2)}, u32[]{:S(2)}) collective-permute-start(bf16[4,8,8192]{2,1,0:T(8,128)(2,1)S(1)} %pad_maximum_fusion), channel_id=1, source_target_pairs={{0,4},{1,5},{2,6},{3,7},{4,8},{5,9},{6,10},{7,11},{8,12},{9,13},{1... | collective-permute-start | bytes 1572872 | tf_op jit(solution)/shard_map/ppermute | solution.py:359
  43.0 19.5 %collective-permute-start.8 = (bf16[4,8,8192]{2,1,0:T(8,128)(2,1)S(1)}, bf16[4,8,8192]{2,1,0:T(8,128)(2,1)S(1)}, u32[]{:S(2)}, u32[]{:S(2)}) collective-permute-start(bf16[4,8,8192]{2,1,0:T(8,128)(2,1)S(1)} %pad_maximum_fusion), channel_id=1, source_target_pairs={{0,12},{1,13},{2,14},{3,15},{4,0},{5,1},{6,2},{7,3},{8,4},{9,5},{1... | collective-permute-start | bytes 1572872 | tf_op jit(solution)/shard_map/ppermute | solution.py:359
  55.7 19.2 %collective-permute-start.12 = (bf16[4,8,8192]{2,1,0:T(8,128)(2,1)}, bf16[4,8,8192]{2,1,0:T(8,128)(2,1)}, u32[]{:S(2)}, u32[]{:S(2)}) collective-permute-start(bf16[4,8,8192]{2,1,0:T(8,128)(2,1)} %collective-permute-done.4), channel_id=1, source_target_pairs={{0,64},{1,65},{2,66},{3,67},{4,68},{5,69},{6,70},{7,71},{8,72},{9,... | collective-permute-start | bytes 1572872 | tf_op jit(solution)/shard_map/ppermute | solution.py:326
  57.2 17.7 %collective-permute-start.11 = (bf16[4,8,8192]{2,1,0:T(8,128)(2,1)}, bf16[4,8,8192]{2,1,0:T(8,128)(2,1)}, u32[]{:S(2)}, u32[]{:S(2)}) collective-permute-start(bf16[4,8,8192]{2,1,0:T(8,128)(2,1)} %collective-permute-done.4), channel_id=1, source_target_pairs={{0,80},{1,81},{2,82},{3,83},{4,84},{5,85},{6,86},{7,87},{8,88},{9,... | collective-permute-start | bytes 1572872 | tf_op jit(solution)/shard_map/ppermute | solution.py:326
  58.5 16.9 %collective-permute-start.10 = (bf16[4,8,8192]{2,1,0:T(8,128)(2,1)}, bf16[4,8,8192]{2,1,0:T(8,128)(2,1)}, u32[]{:S(2)}, u32[]{:S(2)}) collective-permute-start(bf16[4,8,8192]{2,1,0:T(8,128)(2,1)} %collective-permute-done.4), channel_id=1, source_target_pairs={{0,16},{1,17},{2,18},{3,19},{4,20},{5,21},{6,22},{7,23},{8,24},{9,... | collective-permute-start | bytes 1572872 | tf_op jit(solution)/shard_map/ppermute | solution.py:326
  59.1 10.7 %collective-permute-start.9 = (bf16[4,8,8192]{2,1,0:T(8,128)(2,1)S(1)}, bf16[4,8,8192]{2,1,0:T(8,128)(2,1)S(1)}, u32[]{:S(2)}, u32[]{:S(2)}) collective-permute-start(bf16[4,8,8192]{2,1,0:T(8,128)(2,1)S(1)} %pad_maximum_fusion), channel_id=1, source_target_pairs={{0,8},{1,9},{2,10},{3,11},{4,12},{5,13},{6,14},{7,15},{8,0},{9,1},... | collective-permute-start | bytes 1572872 | tf_op jit(solution)/shard_map/ppermute | solution.py:359
  62.5 13.0 %collective-permute-start.13 = (bf16[4,8,8192]{2,1,0:T(8,128)(2,1)S(1)}, bf16[4,8,8192]{2,1,0:T(8,128)(2,1)S(1)}, u32[]{:S(2)}, u32[]{:S(2)}) collective-permute-start(bf16[4,8,8192]{2,1,0:T(8,128)(2,1)S(1)} %pad_maximum_fusion), channel_id=1, source_target_pairs={{0,32},{1,33},{2,34},{3,35},{4,36},{5,37},{6,38},{7,39},{8,40},{9,... | collective-permute-start | bytes 1572872 | tf_op jit(solution)/shard_map/ppermute | solution.py:362
  69.8 6.9 %collective-permute-start.14 = (bf16[4,8,8192]{2,1,0:T(8,128)(2,1)}, bf16[4,8,8192]{2,1,0:T(8,128)(2,1)S(1)}, u32[]{:S(2)}, u32[]{:S(2)}) collective-permute-start(bf16[4,8,8192]{2,1,0:T(8,128)(2,1)} %collective-permute-done.5), channel_id=1, source_target_pairs={{0,32},{1,33},{2,34},{3,35},{4,36},{5,37},{6,38},{7,39},{8,40},{9,... | collective-permute-start | bytes 1572872 | tf_op jit(solution)/shard_map/ppermute | solution.py:362
  74.9 3.2 %collective-permute-start.15 = (bf16[4,8,8192]{2,1,0:T(8,128)(2,1)}, bf16[4,8,8192]{2,1,0:T(8,128)(2,1)S(1)}, u32[]{:S(2)}, u32[]{:S(2)}) collective-permute-start(bf16[4,8,8192]{2,1,0:T(8,128)(2,1)} %collective-permute-done.6), channel_id=1, source_target_pairs={{0,32},{1,33},{2,34},{3,35},{4,36},{5,37},{6,38},{7,39},{8,40},{9,... | collective-permute-start | bytes 1572872 | tf_op jit(solution)/shard_map/ppermute | solution.py:362
  74.9 3.7 %collective-permute-start.16 = (bf16[4,8,8192]{2,1,0:T(8,128)(2,1)S(1)}, bf16[4,8,8192]{2,1,0:T(8,128)(2,1)S(1)}, u32[]{:S(2)}, u32[]{:S(2)}) collective-permute-start(bf16[4,8,8192]{2,1,0:T(8,128)(2,1)S(1)} %collective-permute-done.7), channel_id=1, source_target_pairs={{0,32},{1,33},{2,34},{3,35},{4,36},{5,37},{6,38},{7,39},{8,40},{9,... | collective-permute-start | bytes 1572872 | tf_op jit(solution)/shard_map/ppermute | solution.py:362
  75.4 3.5 %collective-permute-start.17 = (bf16[4,8,8192]{2,1,0:T(8,128)(2,1)}, bf16[4,8,8192]{2,1,0:T(8,128)(2,1)S(1)}, u32[]{:S(2)}, u32[]{:S(2)}) collective-permute-start(bf16[4,8,8192]{2,1,0:T(8,128)(2,1)} %collective-permute-done.4), channel_id=1, source_target_pairs={{0,32},{1,33},{2,34},{3,35},{4,36},{5,37},{6,38},{7,39},{8,40},{9,... | collective-permute-start | bytes 1572872 | tf_op jit(solution)/shard_map/ppermute | solution.py:362
  75.6 5.4 %collective-permute-start.18 = (bf16[4,8,8192]{2,1,0:T(8,128)(2,1)}, bf16[4,8,8192]{2,1,0:T(8,128)(2,1)S(1)}, u32[]{:S(2)}, u32[]{:S(2)}) collective-permute-start(bf16[4,8,8192]{2,1,0:T(8,128)(2,1)} %collective-permute-done.10), channel_id=1, source_target_pairs={{0,32},{1,33},{2,34},{3,35},{4,36},{5,37},{6,38},{7,39},{8,40},{9,... | collective-permute-start | bytes 1572872 | tf_op jit(solution)/shard_map/ppermute | solution.py:362
  76.7 6.7 %collective-permute-start.19 = (bf16[4,8,8192]{2,1,0:T(8,128)(2,1)}, bf16[4,8,8192]{2,1,0:T(8,128)(2,1)S(1)}, u32[]{:S(2)}, u32[]{:S(2)}) collective-permute-start(bf16[4,8,8192]{2,1,0:T(8,128)(2,1)} %collective-permute-done.11), channel_id=1, source_target_pairs={{0,32},{1,33},{2,34},{3,35},{4,36},{5,37},{6,38},{7,39},{8,40},{9,... | collective-permute-start | bytes 1572872 | tf_op jit(solution)/shard_map/ppermute | solution.py:362
  78.2 7.3 %collective-permute-start.20 = (bf16[4,8,8192]{2,1,0:T(8,128)(2,1)}, bf16[4,8,8192]{2,1,0:T(8,128)(2,1)S(1)}, u32[]{:S(2)}, u32[]{:S(2)}) collective-permute-start(bf16[4,8,8192]{2,1,0:T(8,128)(2,1)} %collective-permute-done.12), channel_id=1, source_target_pairs={{0,32},{1,33},{2,34},{3,35},{4,36},{5,37},{6,38},{7,39},{8,40},{9,... | collective-permute-start | bytes 1572872 | tf_op jit(solution)/shard_map/ppermute | solution.py:362
  78.6 23.1 %collective-permute-start.23 = (bf16[4,8,8192]{2,1,0:T(8,128)(2,1)S(1)}, bf16[4,8,8192]{2,1,0:T(8,128)(2,1)S(1)}, u32[]{:S(2)}, u32[]{:S(2)}) collective-permute-start(bf16[4,8,8192]{2,1,0:T(8,128)(2,1)S(1)} %collective-permute-done.7), channel_id=1, source_target_pairs={{0,12},{1,13},{2,14},{3,15},{4,0},{5,1},{6,2},{7,3},{8,4},{9,5},{1... | collective-permute-start | bytes 1572872 | tf_op jit(solution)/shard_map/ppermute | solution.py:359
  78.9 22.8 %collective-permute-start.24 = (bf16[4,8,8192]{2,1,0:T(8,128)(2,1)S(1)}, bf16[4,8,8192]{2,1,0:T(8,128)(2,1)}, u32[]{:S(2)}, u32[]{:S(2)}) collective-permute-start(bf16[4,8,8192]{2,1,0:T(8,128)(2,1)S(1)} %collective-permute-done.9), channel_id=1, source_target_pairs={{0,64},{1,65},{2,66},{3,67},{4,68},{5,69},{6,70},{7,71},{8,72},{9,... | collective-permute-start | bytes 1572872 | tf_op jit(solution)/shard_map/ppermute | solution.py:378
  81.0 25.6 %collective-permute-start.25 = (bf16[8,8,8192]{2,1,0:T(8,128)(2,1)S(1)}, bf16[8,8,8192]{2,1,0:T(8,128)(2,1)}, u32[]{:S(2)}, u32[]{:S(2)}) collective-permute-start(bf16[8,8,8192]{2,1,0:T(8,128)(2,1)S(1)} %constant_dynamic-update-slice_fusion), channel_id=1, source_target_pairs={{0,32},{1,33},{2,34},{3,35},{4,36},{5,37},{6,38},{7,39},{8,40},{9,... | collective-permute-start | bytes 3145736 | tf_op jit(solution)/shard_map/ppermute | solution.py:362
  83.4 18.4 %collective-permute-start.22 = (bf16[8,8,8192]{2,1,0:T(8,128)(2,1)S(1)}, bf16[8,8,8192]{2,1,0:T(8,128)(2,1)}, u32[]{:S(2)}, u32[]{:S(2)}) collective-permute-start(bf16[8,8,8192]{2,1,0:T(8,128)(2,1)S(1)} %constant_dynamic-update-slice_fusion), channel_id=1, source_target_pairs={{0,80},{1,81},{2,82},{3,83},{4,84},{5,85},{6,86},{7,87},{8,88},{9,... | collective-permute-start | bytes 3145736 | tf_op jit(solution)/shard_map/ppermute | solution.py:377
  85.5 16.3 %collective-permute-start.21 = (bf16[8,8,8192]{2,1,0:T(8,128)(2,1)S(1)}, bf16[8,8,8192]{2,1,0:T(8,128)(2,1)}, u32[]{:S(2)}, u32[]{:S(2)}) collective-permute-start(bf16[8,8,8192]{2,1,0:T(8,128)(2,1)S(1)} %constant_dynamic-update-slice_fusion), channel_id=1, source_target_pairs={{0,16},{1,17},{2,18},{3,19},{4,20},{5,21},{6,22},{7,23},{8,24},{9,... | collective-permute-start | bytes 3145736 | tf_op jit(solution)/shard_map/ppermute | solution.py:377
  101.8 6.1 %collective-permute-start.26 = (bf16[8,8,8192]{2,1,0:T(8,128)(2,1)}, bf16[8,8,8192]{2,1,0:T(8,128)(2,1)S(1)}, u32[]{:S(2)}, u32[]{:S(2)}) collective-permute-start(bf16[8,8,8192]{2,1,0:T(8,128)(2,1)} %collective-permute-done.21), channel_id=1, source_target_pairs={{0,32},{1,33},{2,34},{3,35},{4,36},{5,37},{6,38},{7,39},{8,40},{9,... | collective-permute-start | bytes 3145736 | tf_op jit(solution)/shard_map/ppermute | solution.py:362
  101.9 6.0 %collective-permute-start.27 = (bf16[8,8,8192]{2,1,0:T(8,128)(2,1)}, bf16[8,8,8192]{2,1,0:T(8,128)(2,1)}, u32[]{:S(2)}, u32[]{:S(2)}) collective-permute-start(bf16[8,8,8192]{2,1,0:T(8,128)(2,1)} %collective-permute-done.22), channel_id=1, source_target_pairs={{0,32},{1,33},{2,34},{3,35},{4,36},{5,37},{6,38},{7,39},{8,40},{9,... | collective-permute-start | bytes 3145736 | tf_op jit(solution)/shard_map/ppermute | solution.py:362
  102.4 4.2 %collective-permute-start.28 = (bf16[4,8,8192]{2,1,0:T(8,128)(2,1)S(1)}, bf16[4,8,8192]{2,1,0:T(8,128)(2,1)S(1)}, u32[]{:S(2)}, u32[]{:S(2)}) collective-permute-start(bf16[4,8,8192]{2,1,0:T(8,128)(2,1)S(1)} %collective-permute-done.23), channel_id=1, source_target_pairs={{0,32},{1,33},{2,34},{3,35},{4,36},{5,37},{6,38},{7,39},{8,40},{9,... | collective-permute-start | bytes 1572872 | tf_op jit(solution)/shard_map/ppermute | solution.py:362
  102.5 5.4 %collective-permute-start.29 = (bf16[4,8,8192]{2,1,0:T(8,128)(2,1)}, bf16[4,8,8192]{2,1,0:T(8,128)(2,1)}, u32[]{:S(2)}, u32[]{:S(2)}) collective-permute-start(bf16[4,8,8192]{2,1,0:T(8,128)(2,1)} %collective-permute-done.24), channel_id=1, source_target_pairs={{0,32},{1,33},{2,34},{3,35},{4,36},{5,37},{6,38},{7,39},{8,40},{9,... | collective-permute-start | bytes 1572872 | tf_op jit(solution)/shard_map/ppermute | solution.py:362
  (19 other events, 199.3 us)

commit v5 on v4

--- a/solution.py
+++ b/solution.py
@@ -51,23 +51,12 @@
     return vs
 
 
-def front_kernel(meta, rec, table_hbm, white, keep, send, spec, scr, table, sems):
-    def load(n):
-        rows = pl.ds(n * 256, 256)
-        return pltpu.make_async_copy(table_hbm.at[rows], table.at[rows], sems.at[n])
-
-    for n in range(8):
-        load(n).start()
+def front_kernel(meta, rec, table, white, keep, send, spec, scr):
     total = None
     for q in range(4):
         x = rec[:, q].astype(jnp.float32).reshape(SEGS * CH_DEV, 512).astype(jnp.bfloat16)
-        for h in range(2):
-            n = 2 * q + h
-            load(n).wait()
-            part = jnp.dot(
-                x[:, h * 256 : h * 256 + 256], table[n * 256 : n * 256 + 256, :], preferred_element_type=jnp.float32
-            )
-            total = part if total is None else total + part
+        part = jnp.dot(x, table[q * 512 : (q + 1) * 512, :], preferred_element_type=jnp.float32)
+        total = part if total is None else total + part
     re, im = total[:, :BINS], total[:, BINS:]
     power = re * re + im * im
     water = jnp.sum(power, axis=1, keepdims=True) * (1.0 / BINS)
@@ -109,15 +98,13 @@
             jax.ShapeDtypeStruct((CH_DEV, HALF), jnp.bfloat16),
             jax.ShapeDtypeStruct((CH_DEV, HALF), jnp.bfloat16),
         ),
-        in_specs=[pl.BlockSpec(memory_space=pltpu.SMEM), vmem, pl.BlockSpec(memory_space=pltpu.MemorySpace.HBM)],
+        in_specs=[pl.BlockSpec(memory_space=pltpu.SMEM), vmem, vmem],
         out_specs=(vmem, vmem, vmem),
         scratch_shapes=[
             pltpu.VMEM((SEGS * CH_DEV, 2 * BINS), jnp.float32),
             pltpu.VMEM((CH_DEV, WIDE), jnp.float32),
-            pltpu.VMEM((W, 2 * BINS), jnp.bfloat16),
-            pltpu.SemaphoreType.DMA((8,)),
         ],
-        compiler_params=pltpu.CompilerParams(vmem_limit_bytes=60 * MIB),
+        compiler_params=pltpu.CompilerParams(vmem_limit_bytes=32 * MIB),
         name="front",
     )(meta, rec, table)
 
@@ -334,6 +321,7 @@
     x0, y0, z0 = dev % 4, dev // 4 % 4, (grp // 2) * 2 + dev // 16
 
     pick = (channel_map[0][:, None] == jnp.arange(256, dtype=jnp.int32)[None, :]).astype(jnp.bfloat16)
+    pick = lax.optimization_barrier(pick)
     ordered = jnp.dot(pick, records, preferred_element_type=jnp.float32).astype(jnp.bfloat16)
     regrouped = lax.all_to_all(ordered.reshape(32, 8, 512), "dev", split_axis=0, concat_axis=0, tiled=True)
 

time: 125 us -> 122 us (0.976)
  Pallas kernels: 37.8 us -> 34.3 us
  waiting for transfers between devices: 29.2 us -> 30.7 us
    pallas_call x1, Pallas kernels: 6.63 us -> 3.14 us  [front(): pl.pallas_call(front_kernel, out_shape=(jax.ShapeDtypeStruct((CH_DEV, WID...]
    unnamed x41 -> x35, local copies, waits for them, and re-layouts: 5.14 us -> 6.02 us
  transfers between devices with their start and end apart: 31 -> 31, of which waited for: 14 -> 15; matrix products, arithmetic and copies ran while one was open for 3% -> 2% of each run, Pallas kernels for 13% -> 13%
where the time goes in v5:
time: 122 us
  starting transfers between devices  45.6 us (37%)
  Pallas kernels  34.3 us (28%)
  waiting for transfers between devices  30.7 us (25%)
  local copies, waits for them, and re-layouts  6.51 us (5%)
  other arithmetic  3.26 us (3%)
    pallas_call x2, Pallas kernels, corr(): pl.pallas_call(lambda *refs: corr_kernel(first, planes, len(mine), *refs)...  30.8 us
    ppermute x13, starting transfers between devices, swap(): return [lax.ppermute(x, AXES, CORE_PAIRS) for x in xs]  16.5 us
    ppermute x9, waiting for transfers between devices, line(): lax.ppermute(block, AXES, line_pairs(axes, s))  13.8 us
    ppermute x9, starting transfers between devices, line(): lax.ppermute(block, AXES, line_pairs(axes, s))  10.8 us
    all_to_all x1, starting transfers between devices, local(): lax.all_to_all(ordered.reshape(32, 8, 512), 'dev', split_axis=0, concat_a...  9.22 us
    all_to_all x1, waiting for transfers between devices, local(): lax.all_to_all(ordered.reshape(32, 8, 512), 'dev', split_axis=0, concat_a...  7.08 us
    ppermute x13, waiting for transfers between devices, swap(): return [lax.ppermute(x, AXES, CORE_PAIRS) for x in xs]  6.25 us
    unnamed x35, local copies, waits for them, and re-layouts  6.02 us
  transfers between devices with their start and end apart: 31, of which 15 were waited for; matrix products, arithmetic and copies ran while one was open for 2% of the time, Pallas kernels for 13%

profile of v5, /device:TPU:1, one launch (start us, length us, event | category | flops | bytes accessed | tf_op | source)
XLA Modules:
  0.0 121.7 jit_solution(1331811274925408713)
XLA Ops:
  1.0 0.9 fusion
  1.9 9.2 %all-to-all-start = ((bf16[32,8,512]{2,1,0:T(8,128)(2,1)}), bf16[32,8,512]{2,1,0:T(8,128)(2,1)S(1)}, u32[]{:S(2)}, u32[]{:S(2)}) async-start(bf16[32,8,512]{2,1,0:T(8,128)(2,1)} %fusion), calls=%async_computation | async-start | bytes 524288 | tf_op jit(solution)/shard_map/all_to_all | solution.py:326
  11.9 7.1 %all-to-all-done = bf16[32,8,512]{2,1,0:T(8,128)(2,1)S(1)} async-done(((bf16[32,8,512]{2,1,0:T(8,128)(2,1)}), bf16[32,8,512]{2,1,0:T(8,128)(2,1)S(1)}, u32[]{:S(2)}, u32[]{:S(2)}) %all-to-all-start) | async-done | bytes 262176 | tf_op jit(solution)/shard_map/all_to_all | solution.py:326
  19.0 3.4 %copy-done.1 = bf16[2048,2048]{1,0:T(8,128)(2,1)S(1)} copy-done((bf16[2048,2048]{1,0:T(8,128)(2,1)S(1)}, bf16[2048,2048]{1,0:T(8,128)(2,1)}, u32[]{:S(2)}) %copy-start.1) | copy-done | bytes 8388632
  22.4 3.1 %front.1 = (bf16[8,16384]{1,0:T(8,128)(2,1)S(1)}, bf16[8,8192]{1,0:T(8,128)(2,1)S(1)}, bf16[8,8192]{1,0:T(8,128)(2,1)S(1)}) custom-call(s32[3]{0:T(128)S(1)} %pad_add_fusion.2.meta, bf16[8,4,8,512]{3,2,1,0:T(8,128)(2,1)S(1)} %bitcast.40, bf16[2048,2048]{1,0:T(8,128)(2,1)S(1)} %copy-done.1), custom_call_target="tpu_custom_call" | custom-call | tf_op jit(solution)/shard_map/front/pallas_call | solution.py:94
  25.5 2.2 %collective-permute-start = (bf16[8,8192]{1,0:T(8,128)(2,1)S(1)}, bf16[8,8192]{1,0:T(8,128)(2,1)S(1)}, u32[]{:S(2)}, u32[]{:S(2)}) collective-permute-start(bf16[8,8192]{1,0:T(8,128)(2,1)S(1)} %get-tuple-element.28), channel_id=1, source_target_pairs={{0,32},{1,33},{2,34},{3,35},{4,36},{5,37},{6,38},{7,39},{8,40},{9,... | collective-permute-start | bytes 393224 | tf_op jit(solution)/shard_map/ppermute | solution.py:332
  27.7 1.0 collective-permute-done
  28.7 3.4 %collective-permute-start.3 = (bf16[1,8,8192]{2,1,0:T(8,128)(2,1)S(1)}, bf16[1,8,8192]{2,1,0:T(8,128)(2,1)S(1)}, u32[]{:S(2)}, u32[]{:S(2)}) collective-permute-start(bf16[1,8,8192]{2,1,0:T(8,128)(2,1)S(1)} %add_bitcast_fusion), channel_id=1, source_target_pairs={{0,2},{1,3},{2,0},{3,1},{4,6},{5,7},{6,4},{7,5},{8,10},{9,11},{10,... | collective-permute-start | bytes 393224 | tf_op jit(solution)/shard_map/ppermute | solution.py:313
  32.1 1.5 %collective-permute-start.1 = (bf16[1,8,8192]{2,1,0:T(8,128)(2,1)S(1)}, bf16[1,8,8192]{2,1,0:T(8,128)(2,1)S(1)}, u32[]{:S(2)}, u32[]{:S(2)}) collective-permute-start(bf16[1,8,8192]{2,1,0:T(8,128)(2,1)S(1)} %add_bitcast_fusion), channel_id=1, source_target_pairs={{0,1},{1,2},{2,3},{3,0},{4,5},{5,6},{6,7},{7,4},{8,9},{9,10},{10,1... | collective-permute-start | bytes 393224 | tf_op jit(solution)/shard_map/ppermute | solution.py:313
  33.6 1.1 collective-permute-done.3
  34.7 1.2 collective-permute-done.2
  35.9 1.5 %collective-permute-done.1 = bf16[1,8,8192]{2,1,0:T(8,128)(2,1)S(1)} collective-permute-done((bf16[1,8,8192]{2,1,0:T(8,128)(2,1)S(1)}, bf16[1,8,8192]{2,1,0:T(8,128)(2,1)S(1)}, u32[]{:S(2)}, u32[]{:S(2)}) %collective-permute-start.1) | collective-permute-done | bytes 131104 | tf_op jit(solution)/shard_map/ppermute | solution.py:313
  37.5 1.1 collective-permute-start.7
  38.6 1.3 %collective-permute-start.6 = (bf16[4,8,8192]{2,1,0:T(8,128)(2,1)S(1)}, bf16[4,8,8192]{2,1,0:T(8,128)(2,1)}, u32[]{:S(2)}, u32[]{:S(2)}) collective-permute-start(bf16[4,8,8192]{2,1,0:T(8,128)(2,1)S(1)} %pad_maximum_fusion), channel_id=1, source_target_pairs={{0,80},{1,81},{2,82},{3,83},{4,84},{5,85},{6,86},{7,87},{8,88},{9,... | collective-permute-start | bytes 1572872 | tf_op jit(solution)/shard_map/ppermute | solution.py:313
  40.4 2.7 %collective-permute-start.8 = (bf16[4,8,8192]{2,1,0:T(8,128)(2,1)S(1)}, bf16[4,8,8192]{2,1,0:T(8,128)(2,1)S(1)}, u32[]{:S(2)}, u32[]{:S(2)}) collective-permute-start(bf16[4,8,8192]{2,1,0:T(8,128)(2,1)S(1)} %pad_maximum_fusion), channel_id=1, source_target_pairs={{0,12},{1,13},{2,14},{3,15},{4,0},{5,1},{6,2},{7,3},{8,4},{9,5},{1... | collective-permute-start | bytes 1572872 | tf_op jit(solution)/shard_map/ppermute | solution.py:347
  43.1 4.4 %collective-permute-done.7 = bf16[4,8,8192]{2,1,0:T(8,128)(2,1)} collective-permute-done((bf16[4,8,8192]{2,1,0:T(8,128)(2,1)S(1)}, bf16[4,8,8192]{2,1,0:T(8,128)(2,1)}, u32[]{:S(2)}, u32[]{:S(2)}) %collective-permute-start.7) | collective-permute-done | bytes 524320 | tf_op jit(solution)/shard_map/ppermute | solution.py:313
  47.5 4.1 %collective-permute-done.6 = bf16[4,8,8192]{2,1,0:T(8,128)(2,1)} collective-permute-done((bf16[4,8,8192]{2,1,0:T(8,128)(2,1)S(1)}, bf16[4,8,8192]{2,1,0:T(8,128)(2,1)}, u32[]{:S(2)}, u32[]{:S(2)}) %collective-permute-start.6) | collective-permute-done | bytes 524320 | tf_op jit(solution)/shard_map/ppermute | solution.py:313
  51.6 1.5 %collective-permute-done.5 = bf16[4,8,8192]{2,1,0:T(8,128)(2,1)} collective-permute-done((bf16[4,8,8192]{2,1,0:T(8,128)(2,1)S(1)}, bf16[4,8,8192]{2,1,0:T(8,128)(2,1)}, u32[]{:S(2)}, u32[]{:S(2)}) %collective-permute-start.5) | collective-permute-done | bytes 524320 | tf_op jit(solution)/shard_map/ppermute | solution.py:313
  53.1 1.5 %collective-permute-start.12 = (bf16[4,8,8192]{2,1,0:T(8,128)(2,1)}, bf16[4,8,8192]{2,1,0:T(8,128)(2,1)}, u32[]{:S(2)}, u32[]{:S(2)}) collective-permute-start(bf16[4,8,8192]{2,1,0:T(8,128)(2,1)} %collective-permute-done.4), channel_id=1, source_target_pairs={{0,64},{1,65},{2,66},{3,67},{4,68},{5,69},{6,70},{7,71},{8,72},{9,... | collective-permute-start | bytes 1572872 | tf_op jit(solution)/shard_map/ppermute | solution.py:313
  54.6 1.3 %collective-permute-start.11 = (bf16[4,8,8192]{2,1,0:T(8,128)(2,1)}, bf16[4,8,8192]{2,1,0:T(8,128)(2,1)}, u32[]{:S(2)}, u32[]{:S(2)}) collective-permute-start(bf16[4,8,8192]{2,1,0:T(8,128)(2,1)} %collective-permute-done.4), channel_id=1, source_target_pairs={{0,80},{1,81},{2,82},{3,83},{4,84},{5,85},{6,86},{7,87},{8,88},{9,... | collective-permute-start | bytes 1572872 | tf_op jit(solution)/shard_map/ppermute | solution.py:313
  57.9 1.0 copy-done.2
  58.9 5.7 %collective-permute-start.13 = (bf16[4,8,8192]{2,1,0:T(8,128)(2,1)S(1)}, bf16[4,8,8192]{2,1,0:T(8,128)(2,1)S(1)}, u32[]{:S(2)}, u32[]{:S(2)}) collective-permute-start(bf16[4,8,8192]{2,1,0:T(8,128)(2,1)S(1)} %pad_maximum_fusion), channel_id=1, source_target_pairs={{0,32},{1,33},{2,34},{3,35},{4,36},{5,37},{6,38},{7,39},{8,40},{9,... | collective-permute-start | bytes 1572872 | tf_op jit(solution)/shard_map/ppermute | solution.py:350
  64.6 2.5 %collective-permute-done.9 = bf16[4,8,8192]{2,1,0:T(8,128)(2,1)S(1)} collective-permute-done((bf16[4,8,8192]{2,1,0:T(8,128)(2,1)S(1)}, bf16[4,8,8192]{2,1,0:T(8,128)(2,1)S(1)}, u32[]{:S(2)}, u32[]{:S(2)}) %collective-permute-start.9) | collective-permute-done | bytes 524320 | tf_op jit(solution)/shard_map/ppermute | solution.py:347
  67.1 5.1 %collective-permute-start.14 = (bf16[4,8,8192]{2,1,0:T(8,128)(2,1)}, bf16[4,8,8192]{2,1,0:T(8,128)(2,1)S(1)}, u32[]{:S(2)}, u32[]{:S(2)}) collective-permute-start(bf16[4,8,8192]{2,1,0:T(8,128)(2,1)} %collective-permute-done.5), channel_id=1, source_target_pairs={{0,32},{1,33},{2,34},{3,35},{4,36},{5,37},{6,38},{7,39},{8,40},{9,... | collective-permute-start | bytes 1572872 | tf_op jit(solution)/shard_map/ppermute | solution.py:350
  76.3 1.8 %collective-permute-start.24 = (bf16[4,8,8192]{2,1,0:T(8,128)(2,1)S(1)}, bf16[4,8,8192]{2,1,0:T(8,128)(2,1)}, u32[]{:S(2)}, u32[]{:S(2)}) collective-permute-start(bf16[4,8,8192]{2,1,0:T(8,128)(2,1)S(1)} %collective-permute-done.9), channel_id=1, source_target_pairs={{0,64},{1,65},{2,66},{3,67},{4,68},{5,69},{6,70},{7,71},{8,72},{9,... | collective-permute-start | bytes 1572872 | tf_op jit(solution)/shard_map/ppermute | solution.py:366
  78.1 2.7 %collective-permute-start.25 = (bf16[8,8,8192]{2,1,0:T(8,128)(2,1)S(1)}, bf16[8,8,8192]{2,1,0:T(8,128)(2,1)}, u32[]{:S(2)}, u32[]{:S(2)}) collective-permute-start(bf16[8,8,8192]{2,1,0:T(8,128)(2,1)S(1)} %constant_dynamic-update-slice_fusion), channel_id=1, source_target_pairs={{0,32},{1,33},{2,34},{3,35},{4,36},{5,37},{6,38},{7,39},{8,40},{9,... | collective-permute-start | bytes 3145736 | tf_op jit(solution)/shard_map/ppermute | solution.py:350
  80.8 2.1 %collective-permute-start.22 = (bf16[8,8,8192]{2,1,0:T(8,128)(2,1)S(1)}, bf16[8,8,8192]{2,1,0:T(8,128)(2,1)}, u32[]{:S(2)}, u32[]{:S(2)}) collective-permute-start(bf16[8,8,8192]{2,1,0:T(8,128)(2,1)S(1)} %constant_dynamic-update-slice_fusion), channel_id=1, source_target_pairs={{0,80},{1,81},{2,82},{3,83},{4,84},{5,85},{6,86},{7,87},{8,88},{9,... | collective-permute-start | bytes 3145736 | tf_op jit(solution)/shard_map/ppermute | solution.py:365
  83.7 15.4 %corr.2.refs_13_ = bf16[4096,1024]{1,0:T(8,128)(2,1)} custom-call(s32[129]{0:T(256)} %pad_add_fusion.refs_0_, bf16[32,16384]{1,0:T(8,128)(2,1)} %copy-done.2, bf16[32,8192]{1,0:T(8,128)(2,1)} %bitcast.41, bf16[32,8192]{1,0:T(8,128)(2,1)} %bitcast.7.refs_3_, bf16[32,8192]{1,0:T(8,128)(2,1)} %bitcast.8.refs_4_, bf16[32,8192]{1,0:T(8,128)(2,1)} %bitcast.9.refs_5_, ...), custom_call_target="tpu_custom_call" | custom-call | flops 21474836480 | bytes 12582912 | tf_op jit(solution)/shard_map/corr/pallas_call | solution.py:261
  101.0 3.1 %collective-permute-done.28 = bf16[4,8,8192]{2,1,0:T(8,128)(2,1)} collective-permute-done((bf16[4,8,8192]{2,1,0:T(8,128)(2,1)S(1)}, bf16[4,8,8192]{2,1,0:T(8,128)(2,1)}, u32[]{:S(2)}, u32[]{:S(2)}) %collective-permute-start.28) | collective-permute-done | bytes 524320 | tf_op jit(solution)/shard_map/ppermute | solution.py:350
  104.1 1.1 collective-permute-done.29
  105.2 0.9 copy-done.7
  106.2 15.4 %corr.3 = bf16[4096,1024]{1,0:T(8,128)(2,1)} custom-call(s32[129]{0:T(256)} %pad_add_fusion.1.refs_0_, bf16[32,16384]{1,0:T(8,128)(2,1)} %copy-done.2, bf16[64,8192]{1,0:T(8,128)(2,1)} %bitcast.42, bf16[64,8192]{1,0:T(8,128)(2,1)} %bitcast.23.refs_3_, bf16[64,8192]{1,0:T(8,128)(2,1)} %bitcast.24.refs_4_, ...), custom_call_target="tpu_custom_call", output_to_operand_aliasing={{}: (13, {})} | custom-call | flops 21474836480 | bytes 12582912 | tf_op jit(solution)/shard_map/corr/pallas_call | solution.py:261
  (89 shorter events, 11.0 us)
Async XLA Ops:
  1.9 17.1 %all-to-all-start = ((bf16[32,8,512]{2,1,0:T(8,128)(2,1)}), bf16[32,8,512]{2,1,0:T(8,128)(2,1)S(1)}, u32[]{:S(2)}, u32[]{:S(2)}) async-start(bf16[32,8,512]{2,1,0:T(8,128)(2,1)} %fusion), calls=%async_computation | async-start | bytes 524288 | tf_op jit(solution)/shard_map/all_to_all | solution.py:326
  25.5 3.2 %collective-permute-start = (bf16[8,8192]{1,0:T(8,128)(2,1)S(1)}, bf16[8,8192]{1,0:T(8,128)(2,1)S(1)}, u32[]{:S(2)}, u32[]{:S(2)}) collective-permute-start(bf16[8,8192]{1,0:T(8,128)(2,1)S(1)} %get-tuple-element.28), channel_id=1, source_target_pairs={{0,32},{1,33},{2,34},{3,35},{4,36},{5,37},{6,38},{7,39},{8,40},{9,... | collective-permute-start | bytes 393224 | tf_op jit(solution)/shard_map/ppermute | solution.py:332
  28.7 6.0 %collective-permute-start.3 = (bf16[1,8,8192]{2,1,0:T(8,128)(2,1)S(1)}, bf16[1,8,8192]{2,1,0:T(8,128)(2,1)S(1)}, u32[]{:S(2)}, u32[]{:S(2)}) collective-permute-start(bf16[1,8,8192]{2,1,0:T(8,128)(2,1)S(1)} %add_bitcast_fusion), channel_id=1, source_target_pairs={{0,2},{1,3},{2,0},{3,1},{4,6},{5,7},{6,4},{7,5},{8,10},{9,11},{10,... | collective-permute-start | bytes 393224 | tf_op jit(solution)/shard_map/ppermute | solution.py:313
  32.1 3.8 %collective-permute-start.2 = (bf16[1,8,8192]{2,1,0:T(8,128)(2,1)S(1)}, bf16[1,8,8192]{2,1,0:T(8,128)(2,1)S(1)}, u32[]{:S(2)}, u32[]{:S(2)}) collective-permute-start(bf16[1,8,8192]{2,1,0:T(8,128)(2,1)S(1)} %add_bitcast_fusion), channel_id=1, source_target_pairs={{0,3},{1,0},{2,1},{3,2},{4,7},{5,4},{6,5},{7,6},{8,11},{9,8},{10,9... | collective-permute-start | bytes 393224 | tf_op jit(solution)/shard_map/ppermute | solution.py:313
  32.1 5.3 %collective-permute-start.1 = (bf16[1,8,8192]{2,1,0:T(8,128)(2,1)S(1)}, bf16[1,8,8192]{2,1,0:T(8,128)(2,1)S(1)}, u32[]{:S(2)}, u32[]{:S(2)}) collective-permute-start(bf16[1,8,8192]{2,1,0:T(8,128)(2,1)S(1)} %add_bitcast_fusion), channel_id=1, source_target_pairs={{0,1},{1,2},{2,3},{3,0},{4,5},{5,6},{6,7},{7,4},{8,9},{9,10},{10,1... | collective-permute-start | bytes 393224 | tf_op jit(solution)/shard_map/ppermute | solution.py:313
  37.5 46.2 %copy-start.3 = (bf16[4,8,8192]{2,1,0:T(8,128)(2,1)}, bf16[4,8,8192]{2,1,0:T(8,128)(2,1)S(1)}, u32[]{:S(2)}) copy-start(bf16[4,8,8192]{2,1,0:T(8,128)(2,1)S(1)} %pad_maximum_fusion) | copy-start | bytes 1572868
  37.5 10.1 %collective-permute-start.7 = (bf16[4,8,8192]{2,1,0:T(8,128)(2,1)S(1)}, bf16[4,8,8192]{2,1,0:T(8,128)(2,1)}, u32[]{:S(2)}, u32[]{:S(2)}) collective-permute-start(bf16[4,8,8192]{2,1,0:T(8,128)(2,1)S(1)} %pad_maximum_fusion), channel_id=1, source_target_pairs={{0,64},{1,65},{2,66},{3,67},{4,68},{5,69},{6,70},{7,71},{8,72},{9,... | collective-permute-start | bytes 1572872 | tf_op jit(solution)/shard_map/ppermute | solution.py:313
  38.6 13.0 %collective-permute-start.6 = (bf16[4,8,8192]{2,1,0:T(8,128)(2,1)S(1)}, bf16[4,8,8192]{2,1,0:T(8,128)(2,1)}, u32[]{:S(2)}, u32[]{:S(2)}) collective-permute-start(bf16[4,8,8192]{2,1,0:T(8,128)(2,1)S(1)} %pad_maximum_fusion), channel_id=1, source_target_pairs={{0,80},{1,81},{2,82},{3,83},{4,84},{5,85},{6,86},{7,87},{8,88},{9,... | collective-permute-start | bytes 1572872 | tf_op jit(solution)/shard_map/ppermute | solution.py:313
  39.9 13.2 %collective-permute-start.5 = (bf16[4,8,8192]{2,1,0:T(8,128)(2,1)S(1)}, bf16[4,8,8192]{2,1,0:T(8,128)(2,1)}, u32[]{:S(2)}, u32[]{:S(2)}) collective-permute-start(bf16[4,8,8192]{2,1,0:T(8,128)(2,1)S(1)} %pad_maximum_fusion), channel_id=1, source_target_pairs={{0,16},{1,17},{2,18},{3,19},{4,20},{5,21},{6,22},{7,23},{8,24},{9,... | collective-permute-start | bytes 1572872 | tf_op jit(solution)/shard_map/ppermute | solution.py:313
  40.1 13.0 %collective-permute-start.4 = (bf16[4,8,8192]{2,1,0:T(8,128)(2,1)S(1)}, bf16[4,8,8192]{2,1,0:T(8,128)(2,1)}, u32[]{:S(2)}, u32[]{:S(2)}) collective-permute-start(bf16[4,8,8192]{2,1,0:T(8,128)(2,1)S(1)} %pad_maximum_fusion), channel_id=1, source_target_pairs={{0,4},{1,5},{2,6},{3,7},{4,8},{5,9},{6,10},{7,11},{8,12},{9,13},{1... | collective-permute-start | bytes 1572872 | tf_op jit(solution)/shard_map/ppermute | solution.py:347
  40.4 18.5 %collective-permute-start.8 = (bf16[4,8,8192]{2,1,0:T(8,128)(2,1)S(1)}, bf16[4,8,8192]{2,1,0:T(8,128)(2,1)S(1)}, u32[]{:S(2)}, u32[]{:S(2)}) collective-permute-start(bf16[4,8,8192]{2,1,0:T(8,128)(2,1)S(1)} %pad_maximum_fusion), channel_id=1, source_target_pairs={{0,12},{1,13},{2,14},{3,15},{4,0},{5,1},{6,2},{7,3},{8,4},{9,5},{1... | collective-permute-start | bytes 1572872 | tf_op jit(solution)/shard_map/ppermute | solution.py:347
  53.1 19.2 %collective-permute-start.12 = (bf16[4,8,8192]{2,1,0:T(8,128)(2,1)}, bf16[4,8,8192]{2,1,0:T(8,128)(2,1)}, u32[]{:S(2)}, u32[]{:S(2)}) collective-permute-start(bf16[4,8,8192]{2,1,0:T(8,128)(2,1)} %collective-permute-done.4), channel_id=1, source_target_pairs={{0,64},{1,65},{2,66},{3,67},{4,68},{5,69},{6,70},{7,71},{8,72},{9,... | collective-permute-start | bytes 1572872 | tf_op jit(solution)/shard_map/ppermute | solution.py:313
  54.6 17.7 %collective-permute-start.11 = (bf16[4,8,8192]{2,1,0:T(8,128)(2,1)}, bf16[4,8,8192]{2,1,0:T(8,128)(2,1)}, u32[]{:S(2)}, u32[]{:S(2)}) collective-permute-start(bf16[4,8,8192]{2,1,0:T(8,128)(2,1)} %collective-permute-done.4), channel_id=1, source_target_pairs={{0,80},{1,81},{2,82},{3,83},{4,84},{5,85},{6,86},{7,87},{8,88},{9,... | collective-permute-start | bytes 1572872 | tf_op jit(solution)/shard_map/ppermute | solution.py:313
  55.9 16.9 %collective-permute-start.10 = (bf16[4,8,8192]{2,1,0:T(8,128)(2,1)}, bf16[4,8,8192]{2,1,0:T(8,128)(2,1)}, u32[]{:S(2)}, u32[]{:S(2)}) collective-permute-start(bf16[4,8,8192]{2,1,0:T(8,128)(2,1)} %collective-permute-done.4), channel_id=1, source_target_pairs={{0,16},{1,17},{2,18},{3,19},{4,20},{5,21},{6,22},{7,23},{8,24},{9,... | collective-permute-start | bytes 1572872 | tf_op jit(solution)/shard_map/ppermute | solution.py:313
  56.4 10.7 %collective-permute-start.9 = (bf16[4,8,8192]{2,1,0:T(8,128)(2,1)S(1)}, bf16[4,8,8192]{2,1,0:T(8,128)(2,1)S(1)}, u32[]{:S(2)}, u32[]{:S(2)}) collective-permute-start(bf16[4,8,8192]{2,1,0:T(8,128)(2,1)S(1)} %pad_maximum_fusion), channel_id=1, source_target_pairs={{0,8},{1,9},{2,10},{3,11},{4,12},{5,13},{6,14},{7,15},{8,0},{9,1},... | collective-permute-start | bytes 1572872 | tf_op jit(solution)/shard_map/ppermute | solution.py:347
  58.9 14.0 %collective-permute-start.13 = (bf16[4,8,8192]{2,1,0:T(8,128)(2,1)S(1)}, bf16[4,8,8192]{2,1,0:T(8,128)(2,1)S(1)}, u32[]{:S(2)}, u32[]{:S(2)}) collective-permute-start(bf16[4,8,8192]{2,1,0:T(8,128)(2,1)S(1)} %pad_maximum_fusion), channel_id=1, source_target_pairs={{0,32},{1,33},{2,34},{3,35},{4,36},{5,37},{6,38},{7,39},{8,40},{9,... | collective-permute-start | bytes 1572872 | tf_op jit(solution)/shard_map/ppermute | solution.py:350
  67.1 6.9 %collective-permute-start.14 = (bf16[4,8,8192]{2,1,0:T(8,128)(2,1)}, bf16[4,8,8192]{2,1,0:T(8,128)(2,1)S(1)}, u32[]{:S(2)}, u32[]{:S(2)}) collective-permute-start(bf16[4,8,8192]{2,1,0:T(8,128)(2,1)} %collective-permute-done.5), channel_id=1, source_target_pairs={{0,32},{1,33},{2,34},{3,35},{4,36},{5,37},{6,38},{7,39},{8,40},{9,... | collective-permute-start | bytes 1572872 | tf_op jit(solution)/shard_map/ppermute | solution.py:350
  72.3 2.5 %collective-permute-start.15 = (bf16[4,8,8192]{2,1,0:T(8,128)(2,1)}, bf16[4,8,8192]{2,1,0:T(8,128)(2,1)S(1)}, u32[]{:S(2)}, u32[]{:S(2)}) collective-permute-start(bf16[4,8,8192]{2,1,0:T(8,128)(2,1)} %collective-permute-done.6), channel_id=1, source_target_pairs={{0,32},{1,33},{2,34},{3,35},{4,36},{5,37},{6,38},{7,39},{8,40},{9,... | collective-permute-start | bytes 1572872 | tf_op jit(solution)/shard_map/ppermute | solution.py:350
  72.3 3.2 %collective-permute-start.16 = (bf16[4,8,8192]{2,1,0:T(8,128)(2,1)}, bf16[4,8,8192]{2,1,0:T(8,128)(2,1)S(1)}, u32[]{:S(2)}, u32[]{:S(2)}) collective-permute-start(bf16[4,8,8192]{2,1,0:T(8,128)(2,1)} %collective-permute-done.7), channel_id=1, source_target_pairs={{0,32},{1,33},{2,34},{3,35},{4,36},{5,37},{6,38},{7,39},{8,40},{9,... | collective-permute-start | bytes 1572872 | tf_op jit(solution)/shard_map/ppermute | solution.py:350
  72.8 3.5 %collective-permute-start.17 = (bf16[4,8,8192]{2,1,0:T(8,128)(2,1)}, bf16[4,8,8192]{2,1,0:T(8,128)(2,1)S(1)}, u32[]{:S(2)}, u32[]{:S(2)}) collective-permute-start(bf16[4,8,8192]{2,1,0:T(8,128)(2,1)} %collective-permute-done.4), channel_id=1, source_target_pairs={{0,32},{1,33},{2,34},{3,35},{4,36},{5,37},{6,38},{7,39},{8,40},{9,... | collective-permute-start | bytes 1572872 | tf_op jit(solution)/shard_map/ppermute | solution.py:350
  72.9 5.1 %collective-permute-start.18 = (bf16[4,8,8192]{2,1,0:T(8,128)(2,1)}, bf16[4,8,8192]{2,1,0:T(8,128)(2,1)S(1)}, u32[]{:S(2)}, u32[]{:S(2)}) collective-permute-start(bf16[4,8,8192]{2,1,0:T(8,128)(2,1)} %collective-permute-done.10), channel_id=1, source_target_pairs={{0,32},{1,33},{2,34},{3,35},{4,36},{5,37},{6,38},{7,39},{8,40},{9,... | collective-permute-start | bytes 1572872 | tf_op jit(solution)/shard_map/ppermute | solution.py:350
  74.0 6.7 %collective-permute-start.19 = (bf16[4,8,8192]{2,1,0:T(8,128)(2,1)}, bf16[4,8,8192]{2,1,0:T(8,128)(2,1)S(1)}, u32[]{:S(2)}, u32[]{:S(2)}) collective-permute-start(bf16[4,8,8192]{2,1,0:T(8,128)(2,1)} %collective-permute-done.11), channel_id=1, source_target_pairs={{0,32},{1,33},{2,34},{3,35},{4,36},{5,37},{6,38},{7,39},{8,40},{9,... | collective-permute-start | bytes 1572872 | tf_op jit(solution)/shard_map/ppermute | solution.py:350
  74.8 8.1 %collective-permute-start.20 = (bf16[4,8,8192]{2,1,0:T(8,128)(2,1)}, bf16[4,8,8192]{2,1,0:T(8,128)(2,1)S(1)}, u32[]{:S(2)}, u32[]{:S(2)}) collective-permute-start(bf16[4,8,8192]{2,1,0:T(8,128)(2,1)} %collective-permute-done.12), channel_id=1, source_target_pairs={{0,32},{1,33},{2,34},{3,35},{4,36},{5,37},{6,38},{7,39},{8,40},{9,... | collective-permute-start | bytes 1572872 | tf_op jit(solution)/shard_map/ppermute | solution.py:350
  75.5 23.6 %collective-permute-start.23 = (bf16[4,8,8192]{2,1,0:T(8,128)(2,1)}, bf16[4,8,8192]{2,1,0:T(8,128)(2,1)S(1)}, u32[]{:S(2)}, u32[]{:S(2)}) collective-permute-start(bf16[4,8,8192]{2,1,0:T(8,128)(2,1)} %collective-permute-done.7), channel_id=1, source_target_pairs={{0,12},{1,13},{2,14},{3,15},{4,0},{5,1},{6,2},{7,3},{8,4},{9,5},{1... | collective-permute-start | bytes 1572872 | tf_op jit(solution)/shard_map/ppermute | solution.py:347
  76.3 22.8 %collective-permute-start.24 = (bf16[4,8,8192]{2,1,0:T(8,128)(2,1)S(1)}, bf16[4,8,8192]{2,1,0:T(8,128)(2,1)}, u32[]{:S(2)}, u32[]{:S(2)}) collective-permute-start(bf16[4,8,8192]{2,1,0:T(8,128)(2,1)S(1)} %collective-permute-done.9), channel_id=1, source_target_pairs={{0,64},{1,65},{2,66},{3,67},{4,68},{5,69},{6,70},{7,71},{8,72},{9,... | collective-permute-start | bytes 1572872 | tf_op jit(solution)/shard_map/ppermute | solution.py:366
  78.1 26.0 %collective-permute-start.25 = (bf16[8,8,8192]{2,1,0:T(8,128)(2,1)S(1)}, bf16[8,8,8192]{2,1,0:T(8,128)(2,1)}, u32[]{:S(2)}, u32[]{:S(2)}) collective-permute-start(bf16[8,8,8192]{2,1,0:T(8,128)(2,1)S(1)} %constant_dynamic-update-slice_fusion), channel_id=1, source_target_pairs={{0,32},{1,33},{2,34},{3,35},{4,36},{5,37},{6,38},{7,39},{8,40},{9,... | collective-permute-start | bytes 3145736 | tf_op jit(solution)/shard_map/ppermute | solution.py:350
  80.8 18.4 %collective-permute-start.22 = (bf16[8,8,8192]{2,1,0:T(8,128)(2,1)S(1)}, bf16[8,8,8192]{2,1,0:T(8,128)(2,1)}, u32[]{:S(2)}, u32[]{:S(2)}) collective-permute-start(bf16[8,8,8192]{2,1,0:T(8,128)(2,1)S(1)} %constant_dynamic-update-slice_fusion), channel_id=1, source_target_pairs={{0,80},{1,81},{2,82},{3,83},{4,84},{5,85},{6,86},{7,87},{8,88},{9,... | collective-permute-start | bytes 3145736 | tf_op jit(solution)/shard_map/ppermute | solution.py:365
  82.9 16.3 %collective-permute-start.21 = (bf16[8,8,8192]{2,1,0:T(8,128)(2,1)S(1)}, bf16[8,8,8192]{2,1,0:T(8,128)(2,1)}, u32[]{:S(2)}, u32[]{:S(2)}) collective-permute-start(bf16[8,8,8192]{2,1,0:T(8,128)(2,1)S(1)} %constant_dynamic-update-slice_fusion), channel_id=1, source_target_pairs={{0,16},{1,17},{2,18},{3,19},{4,20},{5,21},{6,22},{7,23},{8,24},{9,... | collective-permute-start | bytes 3145736 | tf_op jit(solution)/shard_map/ppermute | solution.py:365
  99.1 6.1 %collective-permute-start.26 = (bf16[8,8,8192]{2,1,0:T(8,128)(2,1)}, bf16[8,8,8192]{2,1,0:T(8,128)(2,1)S(1)}, u32[]{:S(2)}, u32[]{:S(2)}) collective-permute-start(bf16[8,8,8192]{2,1,0:T(8,128)(2,1)} %collective-permute-done.21), channel_id=1, source_target_pairs={{0,32},{1,33},{2,34},{3,35},{4,36},{5,37},{6,38},{7,39},{8,40},{9,... | collective-permute-start | bytes 3145736 | tf_op jit(solution)/shard_map/ppermute | solution.py:350
  99.2 6.0 %collective-permute-start.27 = (bf16[8,8,8192]{2,1,0:T(8,128)(2,1)}, bf16[8,8,8192]{2,1,0:T(8,128)(2,1)}, u32[]{:S(2)}, u32[]{:S(2)}) collective-permute-start(bf16[8,8,8192]{2,1,0:T(8,128)(2,1)} %collective-permute-done.22), channel_id=1, source_target_pairs={{0,32},{1,33},{2,34},{3,35},{4,36},{5,37},{6,38},{7,39},{8,40},{9,... | collective-permute-start | bytes 3145736 | tf_op jit(solution)/shard_map/ppermute | solution.py:350
  99.7 4.4 %collective-permute-start.28 = (bf16[4,8,8192]{2,1,0:T(8,128)(2,1)S(1)}, bf16[4,8,8192]{2,1,0:T(8,128)(2,1)}, u32[]{:S(2)}, u32[]{:S(2)}) collective-permute-start(bf16[4,8,8192]{2,1,0:T(8,128)(2,1)S(1)} %collective-permute-done.23), channel_id=1, source_target_pairs={{0,32},{1,33},{2,34},{3,35},{4,36},{5,37},{6,38},{7,39},{8,40},{9,... | collective-permute-start | bytes 1572872 | tf_op jit(solution)/shard_map/ppermute | solution.py:350
  99.8 5.4 %collective-permute-start.29 = (bf16[4,8,8192]{2,1,0:T(8,128)(2,1)}, bf16[4,8,8192]{2,1,0:T(8,128)(2,1)}, u32[]{:S(2)}, u32[]{:S(2)}) collective-permute-start(bf16[4,8,8192]{2,1,0:T(8,128)(2,1)} %collective-permute-done.24), channel_id=1, source_target_pairs={{0,32},{1,33},{2,34},{3,35},{4,36},{5,37},{6,38},{7,39},{8,40},{9,... | collective-permute-start | bytes 1572872 | tf_op jit(solution)/shard_map/ppermute | solution.py:350
  (16 other events, 160.4 us)

commit v6 on v5

--- a/solution.py
+++ b/solution.py
@@ -234,6 +234,9 @@
                     if lag + h == 0:
                         at = pl.ds(pl.multiple_of(q * 64, 64), 64)
                         part = jnp.where(first_lane, edge_t[at, c : c + 1], part)
+                    if lag + h == 2:
+                        kept = d_scr[c * 64 : c * 64 + 64, 256:384].astype(jnp.float32)
+                        part = jnp.where(first_lane, kept, part)
                     yf[lag + h, pl.ds(c, 64, stride=8), :] = part
                 at = pl.ds((lag + h) * 128, 128)
                 yb[pl.ds(pl.multiple_of(q * 512, 512), 512), at] = yf[lag + h].astype(jnp.bfloat16)
@@ -244,7 +247,7 @@
             odd = jnp.dot(x[:, BINS:], e_scr[BINS:, lanes], preferred_element_type=jnp.float32)
             put(4 + 2 * n, even + odd)
             d_scr[:, lanes] = (even - odd).astype(jnp.bfloat16)
-        put(2, jnp.dot(d_scr[...], flip[:, 256:], preferred_element_type=jnp.float32))
+        put(2, jnp.dot(d_scr[:, :256], flip[:256, 256:], preferred_element_type=jnp.float32))
         put(0, jnp.dot(d_scr[:, 256:], flip[256:, :256], preferred_element_type=jnp.float32))
 
         for n in range(32):

time: 122 us -> 122 us (level)
  no operation moved by 1% of the time
where the time goes in v6:
time: 122 us; the launch traced here: 121 us
  starting transfers between devices  45.6 us (37%)
  Pallas kernels  34 us (28%)
  waiting for transfers between devices  30.7 us (25%)
  local copies, waits for them, and re-layouts  6.51 us (5%)
  other arithmetic  3.26 us (3%)
    pallas_call x2, Pallas kernels, corr(): pl.pallas_call(lambda *refs: corr_kernel(first, planes, len(mine), *refs)...  30.4 us
    ppermute x13, starting transfers between devices, swap(): return [lax.ppermute(x, AXES, CORE_PAIRS) for x in xs]  16.5 us
    ppermute x9, waiting for transfers between devices, line(): lax.ppermute(block, AXES, line_pairs(axes, s))  13.8 us
    ppermute x9, starting transfers between devices, line(): lax.ppermute(block, AXES, line_pairs(axes, s))  10.8 us
    all_to_all x1, starting transfers between devices, local(): lax.all_to_all(ordered.reshape(32, 8, 512), 'dev', split_axis=0, concat_a...  9.22 us
    all_to_all x1, waiting for transfers between devices, local(): lax.all_to_all(ordered.reshape(32, 8, 512), 'dev', split_axis=0, concat_a...  7.08 us
    ppermute x13, waiting for transfers between devices, swap(): return [lax.ppermute(x, AXES, CORE_PAIRS) for x in xs]  6.25 us
    unnamed x35, local copies, waits for them, and re-layouts  6.02 us
  transfers between devices with their start and end apart: 31, of which 15 were waited for; matrix products, arithmetic and copies ran while one was open for 2% of the time, Pallas kernels for 13%

profile of v6, /device:TPU:1, one launch (start us, length us, event | category | flops | bytes accessed | tf_op | source)
XLA Modules:
  0.0 121.4 jit_solution(1631816248001640668)
XLA Ops:
  1.0 0.9 fusion
  1.9 9.2 %all-to-all-start = ((bf16[32,8,512]{2,1,0:T(8,128)(2,1)}), bf16[32,8,512]{2,1,0:T(8,128)(2,1)S(1)}, u32[]{:S(2)}, u32[]{:S(2)}) async-start(bf16[32,8,512]{2,1,0:T(8,128)(2,1)} %fusion), calls=%async_computation | async-start | bytes 524288 | tf_op jit(solution)/shard_map/all_to_all | solution.py:329
  11.9 7.1 %all-to-all-done = bf16[32,8,512]{2,1,0:T(8,128)(2,1)S(1)} async-done(((bf16[32,8,512]{2,1,0:T(8,128)(2,1)}), bf16[32,8,512]{2,1,0:T(8,128)(2,1)S(1)}, u32[]{:S(2)}, u32[]{:S(2)}) %all-to-all-start) | async-done | bytes 262176 | tf_op jit(solution)/shard_map/all_to_all | solution.py:329
  19.0 3.4 %copy-done.1 = bf16[2048,2048]{1,0:T(8,128)(2,1)S(1)} copy-done((bf16[2048,2048]{1,0:T(8,128)(2,1)S(1)}, bf16[2048,2048]{1,0:T(8,128)(2,1)}, u32[]{:S(2)}) %copy-start.1) | copy-done | bytes 8388632
  22.4 3.1 %front.1 = (bf16[8,16384]{1,0:T(8,128)(2,1)S(1)}, bf16[8,8192]{1,0:T(8,128)(2,1)S(1)}, bf16[8,8192]{1,0:T(8,128)(2,1)S(1)}) custom-call(s32[3]{0:T(128)S(1)} %pad_add_fusion.2.meta, bf16[8,4,8,512]{3,2,1,0:T(8,128)(2,1)S(1)} %bitcast.40, bf16[2048,2048]{1,0:T(8,128)(2,1)S(1)} %copy-done.1), custom_call_target="tpu_custom_call" | custom-call | tf_op jit(solution)/shard_map/front/pallas_call | solution.py:94
  25.5 2.2 %collective-permute-start = (bf16[8,8192]{1,0:T(8,128)(2,1)S(1)}, bf16[8,8192]{1,0:T(8,128)(2,1)S(1)}, u32[]{:S(2)}, u32[]{:S(2)}) collective-permute-start(bf16[8,8192]{1,0:T(8,128)(2,1)S(1)} %get-tuple-element.28), channel_id=1, source_target_pairs={{0,32},{1,33},{2,34},{3,35},{4,36},{5,37},{6,38},{7,39},{8,40},{9,... | collective-permute-start | bytes 393224 | tf_op jit(solution)/shard_map/ppermute | solution.py:335
  27.7 1.0 collective-permute-done
  28.7 3.4 %collective-permute-start.3 = (bf16[1,8,8192]{2,1,0:T(8,128)(2,1)S(1)}, bf16[1,8,8192]{2,1,0:T(8,128)(2,1)S(1)}, u32[]{:S(2)}, u32[]{:S(2)}) collective-permute-start(bf16[1,8,8192]{2,1,0:T(8,128)(2,1)S(1)} %add_bitcast_fusion), channel_id=1, source_target_pairs={{0,2},{1,3},{2,0},{3,1},{4,6},{5,7},{6,4},{7,5},{8,10},{9,11},{10,... | collective-permute-start | bytes 393224 | tf_op jit(solution)/shard_map/ppermute | solution.py:316
  32.1 1.5 %collective-permute-start.1 = (bf16[1,8,8192]{2,1,0:T(8,128)(2,1)S(1)}, bf16[1,8,8192]{2,1,0:T(8,128)(2,1)S(1)}, u32[]{:S(2)}, u32[]{:S(2)}) collective-permute-start(bf16[1,8,8192]{2,1,0:T(8,128)(2,1)S(1)} %add_bitcast_fusion), channel_id=1, source_target_pairs={{0,1},{1,2},{2,3},{3,0},{4,5},{5,6},{6,7},{7,4},{8,9},{9,10},{10,1... | collective-permute-start | bytes 393224 | tf_op jit(solution)/shard_map/ppermute | solution.py:316
  33.6 1.1 collective-permute-done.3
  34.7 1.2 collective-permute-done.2
  35.9 1.5 %collective-permute-done.1 = bf16[1,8,8192]{2,1,0:T(8,128)(2,1)S(1)} collective-permute-done((bf16[1,8,8192]{2,1,0:T(8,128)(2,1)S(1)}, bf16[1,8,8192]{2,1,0:T(8,128)(2,1)S(1)}, u32[]{:S(2)}, u32[]{:S(2)}) %collective-permute-start.1) | collective-permute-done | bytes 131104 | tf_op jit(solution)/shard_map/ppermute | solution.py:316
  37.5 1.1 collective-permute-start.7
  38.6 1.3 %collective-permute-start.6 = (bf16[4,8,8192]{2,1,0:T(8,128)(2,1)S(1)}, bf16[4,8,8192]{2,1,0:T(8,128)(2,1)}, u32[]{:S(2)}, u32[]{:S(2)}) collective-permute-start(bf16[4,8,8192]{2,1,0:T(8,128)(2,1)S(1)} %pad_maximum_fusion), channel_id=1, source_target_pairs={{0,80},{1,81},{2,82},{3,83},{4,84},{5,85},{6,86},{7,87},{8,88},{9,... | collective-permute-start | bytes 1572872 | tf_op jit(solution)/shard_map/ppermute | solution.py:316
  40.4 2.7 %collective-permute-start.8 = (bf16[4,8,8192]{2,1,0:T(8,128)(2,1)S(1)}, bf16[4,8,8192]{2,1,0:T(8,128)(2,1)S(1)}, u32[]{:S(2)}, u32[]{:S(2)}) collective-permute-start(bf16[4,8,8192]{2,1,0:T(8,128)(2,1)S(1)} %pad_maximum_fusion), channel_id=1, source_target_pairs={{0,12},{1,13},{2,14},{3,15},{4,0},{5,1},{6,2},{7,3},{8,4},{9,5},{1... | collective-permute-start | bytes 1572872 | tf_op jit(solution)/shard_map/ppermute | solution.py:350
  43.1 4.4 %collective-permute-done.7 = bf16[4,8,8192]{2,1,0:T(8,128)(2,1)} collective-permute-done((bf16[4,8,8192]{2,1,0:T(8,128)(2,1)S(1)}, bf16[4,8,8192]{2,1,0:T(8,128)(2,1)}, u32[]{:S(2)}, u32[]{:S(2)}) %collective-permute-start.7) | collective-permute-done | bytes 524320 | tf_op jit(solution)/shard_map/ppermute | solution.py:316
  47.5 4.1 %collective-permute-done.6 = bf16[4,8,8192]{2,1,0:T(8,128)(2,1)} collective-permute-done((bf16[4,8,8192]{2,1,0:T(8,128)(2,1)S(1)}, bf16[4,8,8192]{2,1,0:T(8,128)(2,1)}, u32[]{:S(2)}, u32[]{:S(2)}) %collective-permute-start.6) | collective-permute-done | bytes 524320 | tf_op jit(solution)/shard_map/ppermute | solution.py:316
  51.6 1.5 %collective-permute-done.5 = bf16[4,8,8192]{2,1,0:T(8,128)(2,1)} collective-permute-done((bf16[4,8,8192]{2,1,0:T(8,128)(2,1)S(1)}, bf16[4,8,8192]{2,1,0:T(8,128)(2,1)}, u32[]{:S(2)}, u32[]{:S(2)}) %collective-permute-start.5) | collective-permute-done | bytes 524320 | tf_op jit(solution)/shard_map/ppermute | solution.py:316
  53.1 1.5 %collective-permute-start.12 = (bf16[4,8,8192]{2,1,0:T(8,128)(2,1)}, bf16[4,8,8192]{2,1,0:T(8,128)(2,1)}, u32[]{:S(2)}, u32[]{:S(2)}) collective-permute-start(bf16[4,8,8192]{2,1,0:T(8,128)(2,1)} %collective-permute-done.4), channel_id=1, source_target_pairs={{0,64},{1,65},{2,66},{3,67},{4,68},{5,69},{6,70},{7,71},{8,72},{9,... | collective-permute-start | bytes 1572872 | tf_op jit(solution)/shard_map/ppermute | solution.py:316
  54.6 1.3 %collective-permute-start.11 = (bf16[4,8,8192]{2,1,0:T(8,128)(2,1)}, bf16[4,8,8192]{2,1,0:T(8,128)(2,1)}, u32[]{:S(2)}, u32[]{:S(2)}) collective-permute-start(bf16[4,8,8192]{2,1,0:T(8,128)(2,1)} %collective-permute-done.4), channel_id=1, source_target_pairs={{0,80},{1,81},{2,82},{3,83},{4,84},{5,85},{6,86},{7,87},{8,88},{9,... | collective-permute-start | bytes 1572872 | tf_op jit(solution)/shard_map/ppermute | solution.py:316
  57.9 1.0 copy-done.2
  58.9 5.7 %collective-permute-start.13 = (bf16[4,8,8192]{2,1,0:T(8,128)(2,1)S(1)}, bf16[4,8,8192]{2,1,0:T(8,128)(2,1)S(1)}, u32[]{:S(2)}, u32[]{:S(2)}) collective-permute-start(bf16[4,8,8192]{2,1,0:T(8,128)(2,1)S(1)} %pad_maximum_fusion), channel_id=1, source_target_pairs={{0,32},{1,33},{2,34},{3,35},{4,36},{5,37},{6,38},{7,39},{8,40},{9,... | collective-permute-start | bytes 1572872 | tf_op jit(solution)/shard_map/ppermute | solution.py:353
  64.6 2.5 %collective-permute-done.9 = bf16[4,8,8192]{2,1,0:T(8,128)(2,1)S(1)} collective-permute-done((bf16[4,8,8192]{2,1,0:T(8,128)(2,1)S(1)}, bf16[4,8,8192]{2,1,0:T(8,128)(2,1)S(1)}, u32[]{:S(2)}, u32[]{:S(2)}) %collective-permute-start.9) | collective-permute-done | bytes 524320 | tf_op jit(solution)/shard_map/ppermute | solution.py:350
  67.1 5.1 %collective-permute-start.14 = (bf16[4,8,8192]{2,1,0:T(8,128)(2,1)}, bf16[4,8,8192]{2,1,0:T(8,128)(2,1)S(1)}, u32[]{:S(2)}, u32[]{:S(2)}) collective-permute-start(bf16[4,8,8192]{2,1,0:T(8,128)(2,1)} %collective-permute-done.5), channel_id=1, source_target_pairs={{0,32},{1,33},{2,34},{3,35},{4,36},{5,37},{6,38},{7,39},{8,40},{9,... | collective-permute-start | bytes 1572872 | tf_op jit(solution)/shard_map/ppermute | solution.py:353
  76.3 1.8 %collective-permute-start.24 = (bf16[4,8,8192]{2,1,0:T(8,128)(2,1)S(1)}, bf16[4,8,8192]{2,1,0:T(8,128)(2,1)}, u32[]{:S(2)}, u32[]{:S(2)}) collective-permute-start(bf16[4,8,8192]{2,1,0:T(8,128)(2,1)S(1)} %collective-permute-done.9), channel_id=1, source_target_pairs={{0,64},{1,65},{2,66},{3,67},{4,68},{5,69},{6,70},{7,71},{8,72},{9,... | collective-permute-start | bytes 1572872 | tf_op jit(solution)/shard_map/ppermute | solution.py:369
  78.1 2.7 %collective-permute-start.25 = (bf16[8,8,8192]{2,1,0:T(8,128)(2,1)S(1)}, bf16[8,8,8192]{2,1,0:T(8,128)(2,1)}, u32[]{:S(2)}, u32[]{:S(2)}) collective-permute-start(bf16[8,8,8192]{2,1,0:T(8,128)(2,1)S(1)} %constant_dynamic-update-slice_fusion), channel_id=1, source_target_pairs={{0,32},{1,33},{2,34},{3,35},{4,36},{5,37},{6,38},{7,39},{8,40},{9,... | collective-permute-start | bytes 3145736 | tf_op jit(solution)/shard_map/ppermute | solution.py:353
  80.8 2.1 %collective-permute-start.22 = (bf16[8,8,8192]{2,1,0:T(8,128)(2,1)S(1)}, bf16[8,8,8192]{2,1,0:T(8,128)(2,1)}, u32[]{:S(2)}, u32[]{:S(2)}) collective-permute-start(bf16[8,8,8192]{2,1,0:T(8,128)(2,1)S(1)} %constant_dynamic-update-slice_fusion), channel_id=1, source_target_pairs={{0,80},{1,81},{2,82},{3,83},{4,84},{5,85},{6,86},{7,87},{8,88},{9,... | collective-permute-start | bytes 3145736 | tf_op jit(solution)/shard_map/ppermute | solution.py:368
  83.7 15.2 %corr.2.refs_13_ = bf16[4096,1024]{1,0:T(8,128)(2,1)} custom-call(s32[129]{0:T(256)} %pad_add_fusion.refs_0_, bf16[32,16384]{1,0:T(8,128)(2,1)} %copy-done.2, bf16[32,8192]{1,0:T(8,128)(2,1)} %bitcast.41, bf16[32,8192]{1,0:T(8,128)(2,1)} %bitcast.7.refs_3_, bf16[32,8192]{1,0:T(8,128)(2,1)} %bitcast.8.refs_4_, bf16[32,8192]{1,0:T(8,128)(2,1)} %bitcast.9.refs_5_, ...), custom_call_target="tpu_custom_call" | custom-call | flops 21474836480 | bytes 12582912 | tf_op jit(solution)/shard_map/corr/pallas_call | solution.py:264
  100.8 2.5 %collective-permute-done.28 = bf16[4,8,8192]{2,1,0:T(8,128)(2,1)} collective-permute-done((bf16[4,8,8192]{2,1,0:T(8,128)(2,1)S(1)}, bf16[4,8,8192]{2,1,0:T(8,128)(2,1)}, u32[]{:S(2)}, u32[]{:S(2)}) %collective-permute-start.28) | collective-permute-done | bytes 524320 | tf_op jit(solution)/shard_map/ppermute | solution.py:353
  103.3 1.7 %collective-permute-done.29 = bf16[4,8,8192]{2,1,0:T(8,128)(2,1)} collective-permute-done((bf16[4,8,8192]{2,1,0:T(8,128)(2,1)}, bf16[4,8,8192]{2,1,0:T(8,128)(2,1)}, u32[]{:S(2)}, u32[]{:S(2)}) %collective-permute-start.29) | collective-permute-done | bytes 524320 | tf_op jit(solution)/shard_map/ppermute | solution.py:353
  105.1 0.9 copy-done.7
  106.0 15.2 %corr.3 = bf16[4096,1024]{1,0:T(8,128)(2,1)} custom-call(s32[129]{0:T(256)} %pad_add_fusion.1.refs_0_, bf16[32,16384]{1,0:T(8,128)(2,1)} %copy-done.2, bf16[64,8192]{1,0:T(8,128)(2,1)} %bitcast.42, bf16[64,8192]{1,0:T(8,128)(2,1)} %bitcast.23.refs_3_, bf16[64,8192]{1,0:T(8,128)(2,1)} %bitcast.24.refs_4_, ...), custom_call_target="tpu_custom_call", output_to_operand_aliasing={{}: (13, {})} | custom-call | flops 21474836480 | bytes 12582912 | tf_op jit(solution)/shard_map/corr/pallas_call | solution.py:264
  (89 shorter events, 11.0 us)
Async XLA Ops:
  1.9 17.1 %all-to-all-start = ((bf16[32,8,512]{2,1,0:T(8,128)(2,1)}), bf16[32,8,512]{2,1,0:T(8,128)(2,1)S(1)}, u32[]{:S(2)}, u32[]{:S(2)}) async-start(bf16[32,8,512]{2,1,0:T(8,128)(2,1)} %fusion), calls=%async_computation | async-start | bytes 524288 | tf_op jit(solution)/shard_map/all_to_all | solution.py:329
  25.5 3.2 %collective-permute-start = (bf16[8,8192]{1,0:T(8,128)(2,1)S(1)}, bf16[8,8192]{1,0:T(8,128)(2,1)S(1)}, u32[]{:S(2)}, u32[]{:S(2)}) collective-permute-start(bf16[8,8192]{1,0:T(8,128)(2,1)S(1)} %get-tuple-element.28), channel_id=1, source_target_pairs={{0,32},{1,33},{2,34},{3,35},{4,36},{5,37},{6,38},{7,39},{8,40},{9,... | collective-permute-start | bytes 393224 | tf_op jit(solution)/shard_map/ppermute | solution.py:335
  28.7 6.0 %collective-permute-start.3 = (bf16[1,8,8192]{2,1,0:T(8,128)(2,1)S(1)}, bf16[1,8,8192]{2,1,0:T(8,128)(2,1)S(1)}, u32[]{:S(2)}, u32[]{:S(2)}) collective-permute-start(bf16[1,8,8192]{2,1,0:T(8,128)(2,1)S(1)} %add_bitcast_fusion), channel_id=1, source_target_pairs={{0,2},{1,3},{2,0},{3,1},{4,6},{5,7},{6,4},{7,5},{8,10},{9,11},{10,... | collective-permute-start | bytes 393224 | tf_op jit(solution)/shard_map/ppermute | solution.py:316
  32.1 3.8 %collective-permute-start.2 = (bf16[1,8,8192]{2,1,0:T(8,128)(2,1)S(1)}, bf16[1,8,8192]{2,1,0:T(8,128)(2,1)S(1)}, u32[]{:S(2)}, u32[]{:S(2)}) collective-permute-start(bf16[1,8,8192]{2,1,0:T(8,128)(2,1)S(1)} %add_bitcast_fusion), channel_id=1, source_target_pairs={{0,3},{1,0},{2,1},{3,2},{4,7},{5,4},{6,5},{7,6},{8,11},{9,8},{10,9... | collective-permute-start | bytes 393224 | tf_op jit(solution)/shard_map/ppermute | solution.py:316
  32.1 5.3 %collective-permute-start.1 = (bf16[1,8,8192]{2,1,0:T(8,128)(2,1)S(1)}, bf16[1,8,8192]{2,1,0:T(8,128)(2,1)S(1)}, u32[]{:S(2)}, u32[]{:S(2)}) collective-permute-start(bf16[1,8,8192]{2,1,0:T(8,128)(2,1)S(1)} %add_bitcast_fusion), channel_id=1, source_target_pairs={{0,1},{1,2},{2,3},{3,0},{4,5},{5,6},{6,7},{7,4},{8,9},{9,10},{10,1... | collective-permute-start | bytes 393224 | tf_op jit(solution)/shard_map/ppermute | solution.py:316
  37.5 46.2 %copy-start.3 = (bf16[4,8,8192]{2,1,0:T(8,128)(2,1)}, bf16[4,8,8192]{2,1,0:T(8,128)(2,1)S(1)}, u32[]{:S(2)}) copy-start(bf16[4,8,8192]{2,1,0:T(8,128)(2,1)S(1)} %pad_maximum_fusion) | copy-start | bytes 1572868
  37.5 10.1 %collective-permute-start.7 = (bf16[4,8,8192]{2,1,0:T(8,128)(2,1)S(1)}, bf16[4,8,8192]{2,1,0:T(8,128)(2,1)}, u32[]{:S(2)}, u32[]{:S(2)}) collective-permute-start(bf16[4,8,8192]{2,1,0:T(8,128)(2,1)S(1)} %pad_maximum_fusion), channel_id=1, source_target_pairs={{0,64},{1,65},{2,66},{3,67},{4,68},{5,69},{6,70},{7,71},{8,72},{9,... | collective-permute-start | bytes 1572872 | tf_op jit(solution)/shard_map/ppermute | solution.py:316
  38.6 13.0 %collective-permute-start.6 = (bf16[4,8,8192]{2,1,0:T(8,128)(2,1)S(1)}, bf16[4,8,8192]{2,1,0:T(8,128)(2,1)}, u32[]{:S(2)}, u32[]{:S(2)}) collective-permute-start(bf16[4,8,8192]{2,1,0:T(8,128)(2,1)S(1)} %pad_maximum_fusion), channel_id=1, source_target_pairs={{0,80},{1,81},{2,82},{3,83},{4,84},{5,85},{6,86},{7,87},{8,88},{9,... | collective-permute-start | bytes 1572872 | tf_op jit(solution)/shard_map/ppermute | solution.py:316
  39.9 13.2 %collective-permute-start.5 = (bf16[4,8,8192]{2,1,0:T(8,128)(2,1)S(1)}, bf16[4,8,8192]{2,1,0:T(8,128)(2,1)}, u32[]{:S(2)}, u32[]{:S(2)}) collective-permute-start(bf16[4,8,8192]{2,1,0:T(8,128)(2,1)S(1)} %pad_maximum_fusion), channel_id=1, source_target_pairs={{0,16},{1,17},{2,18},{3,19},{4,20},{5,21},{6,22},{7,23},{8,24},{9,... | collective-permute-start | bytes 1572872 | tf_op jit(solution)/shard_map/ppermute | solution.py:316
  40.1 13.0 %collective-permute-start.4 = (bf16[4,8,8192]{2,1,0:T(8,128)(2,1)S(1)}, bf16[4,8,8192]{2,1,0:T(8,128)(2,1)}, u32[]{:S(2)}, u32[]{:S(2)}) collective-permute-start(bf16[4,8,8192]{2,1,0:T(8,128)(2,1)S(1)} %pad_maximum_fusion), channel_id=1, source_target_pairs={{0,4},{1,5},{2,6},{3,7},{4,8},{5,9},{6,10},{7,11},{8,12},{9,13},{1... | collective-permute-start | bytes 1572872 | tf_op jit(solution)/shard_map/ppermute | solution.py:350
  40.4 18.5 %collective-permute-start.8 = (bf16[4,8,8192]{2,1,0:T(8,128)(2,1)S(1)}, bf16[4,8,8192]{2,1,0:T(8,128)(2,1)S(1)}, u32[]{:S(2)}, u32[]{:S(2)}) collective-permute-start(bf16[4,8,8192]{2,1,0:T(8,128)(2,1)S(1)} %pad_maximum_fusion), channel_id=1, source_target_pairs={{0,12},{1,13},{2,14},{3,15},{4,0},{5,1},{6,2},{7,3},{8,4},{9,5},{1... | collective-permute-start | bytes 1572872 | tf_op jit(solution)/shard_map/ppermute | solution.py:350
  53.1 19.2 %collective-permute-start.12 = (bf16[4,8,8192]{2,1,0:T(8,128)(2,1)}, bf16[4,8,8192]{2,1,0:T(8,128)(2,1)}, u32[]{:S(2)}, u32[]{:S(2)}) collective-permute-start(bf16[4,8,8192]{2,1,0:T(8,128)(2,1)} %collective-permute-done.4), channel_id=1, source_target_pairs={{0,64},{1,65},{2,66},{3,67},{4,68},{5,69},{6,70},{7,71},{8,72},{9,... | collective-permute-start | bytes 1572872 | tf_op jit(solution)/shard_map/ppermute | solution.py:316
  54.6 17.7 %collective-permute-start.11 = (bf16[4,8,8192]{2,1,0:T(8,128)(2,1)}, bf16[4,8,8192]{2,1,0:T(8,128)(2,1)}, u32[]{:S(2)}, u32[]{:S(2)}) collective-permute-start(bf16[4,8,8192]{2,1,0:T(8,128)(2,1)} %collective-permute-done.4), channel_id=1, source_target_pairs={{0,80},{1,81},{2,82},{3,83},{4,84},{5,85},{6,86},{7,87},{8,88},{9,... | collective-permute-start | bytes 1572872 | tf_op jit(solution)/shard_map/ppermute | solution.py:316
  55.9 16.9 %collective-permute-start.10 = (bf16[4,8,8192]{2,1,0:T(8,128)(2,1)}, bf16[4,8,8192]{2,1,0:T(8,128)(2,1)}, u32[]{:S(2)}, u32[]{:S(2)}) collective-permute-start(bf16[4,8,8192]{2,1,0:T(8,128)(2,1)} %collective-permute-done.4), channel_id=1, source_target_pairs={{0,16},{1,17},{2,18},{3,19},{4,20},{5,21},{6,22},{7,23},{8,24},{9,... | collective-permute-start | bytes 1572872 | tf_op jit(solution)/shard_map/ppermute | solution.py:316
  56.4 10.7 %collective-permute-start.9 = (bf16[4,8,8192]{2,1,0:T(8,128)(2,1)S(1)}, bf16[4,8,8192]{2,1,0:T(8,128)(2,1)S(1)}, u32[]{:S(2)}, u32[]{:S(2)}) collective-permute-start(bf16[4,8,8192]{2,1,0:T(8,128)(2,1)S(1)} %pad_maximum_fusion), channel_id=1, source_target_pairs={{0,8},{1,9},{2,10},{3,11},{4,12},{5,13},{6,14},{7,15},{8,0},{9,1},... | collective-permute-start | bytes 1572872 | tf_op jit(solution)/shard_map/ppermute | solution.py:350
  58.9 14.0 %collective-permute-start.13 = (bf16[4,8,8192]{2,1,0:T(8,128)(2,1)S(1)}, bf16[4,8,8192]{2,1,0:T(8,128)(2,1)S(1)}, u32[]{:S(2)}, u32[]{:S(2)}) collective-permute-start(bf16[4,8,8192]{2,1,0:T(8,128)(2,1)S(1)} %pad_maximum_fusion), channel_id=1, source_target_pairs={{0,32},{1,33},{2,34},{3,35},{4,36},{5,37},{6,38},{7,39},{8,40},{9,... | collective-permute-start | bytes 1572872 | tf_op jit(solution)/shard_map/ppermute | solution.py:353
  67.1 6.9 %collective-permute-start.14 = (bf16[4,8,8192]{2,1,0:T(8,128)(2,1)}, bf16[4,8,8192]{2,1,0:T(8,128)(2,1)S(1)}, u32[]{:S(2)}, u32[]{:S(2)}) collective-permute-start(bf16[4,8,8192]{2,1,0:T(8,128)(2,1)} %collective-permute-done.5), channel_id=1, source_target_pairs={{0,32},{1,33},{2,34},{3,35},{4,36},{5,37},{6,38},{7,39},{8,40},{9,... | collective-permute-start | bytes 1572872 | tf_op jit(solution)/shard_map/ppermute | solution.py:353
  72.3 2.5 %collective-permute-start.15 = (bf16[4,8,8192]{2,1,0:T(8,128)(2,1)}, bf16[4,8,8192]{2,1,0:T(8,128)(2,1)S(1)}, u32[]{:S(2)}, u32[]{:S(2)}) collective-permute-start(bf16[4,8,8192]{2,1,0:T(8,128)(2,1)} %collective-permute-done.6), channel_id=1, source_target_pairs={{0,32},{1,33},{2,34},{3,35},{4,36},{5,37},{6,38},{7,39},{8,40},{9,... | collective-permute-start | bytes 1572872 | tf_op jit(solution)/shard_map/ppermute | solution.py:353
  72.3 3.2 %collective-permute-start.16 = (bf16[4,8,8192]{2,1,0:T(8,128)(2,1)}, bf16[4,8,8192]{2,1,0:T(8,128)(2,1)S(1)}, u32[]{:S(2)}, u32[]{:S(2)}) collective-permute-start(bf16[4,8,8192]{2,1,0:T(8,128)(2,1)} %collective-permute-done.7), channel_id=1, source_target_pairs={{0,32},{1,33},{2,34},{3,35},{4,36},{5,37},{6,38},{7,39},{8,40},{9,... | collective-permute-start | bytes 1572872 | tf_op jit(solution)/shard_map/ppermute | solution.py:353
  72.8 3.5 %collective-permute-start.17 = (bf16[4,8,8192]{2,1,0:T(8,128)(2,1)}, bf16[4,8,8192]{2,1,0:T(8,128)(2,1)S(1)}, u32[]{:S(2)}, u32[]{:S(2)}) collective-permute-start(bf16[4,8,8192]{2,1,0:T(8,128)(2,1)} %collective-permute-done.4), channel_id=1, source_target_pairs={{0,32},{1,33},{2,34},{3,35},{4,36},{5,37},{6,38},{7,39},{8,40},{9,... | collective-permute-start | bytes 1572872 | tf_op jit(solution)/shard_map/ppermute | solution.py:353
  72.9 5.1 %collective-permute-start.18 = (bf16[4,8,8192]{2,1,0:T(8,128)(2,1)}, bf16[4,8,8192]{2,1,0:T(8,128)(2,1)S(1)}, u32[]{:S(2)}, u32[]{:S(2)}) collective-permute-start(bf16[4,8,8192]{2,1,0:T(8,128)(2,1)} %collective-permute-done.10), channel_id=1, source_target_pairs={{0,32},{1,33},{2,34},{3,35},{4,36},{5,37},{6,38},{7,39},{8,40},{9,... | collective-permute-start | bytes 1572872 | tf_op jit(solution)/shard_map/ppermute | solution.py:353
  74.0 6.7 %collective-permute-start.19 = (bf16[4,8,8192]{2,1,0:T(8,128)(2,1)}, bf16[4,8,8192]{2,1,0:T(8,128)(2,1)S(1)}, u32[]{:S(2)}, u32[]{:S(2)}) collective-permute-start(bf16[4,8,8192]{2,1,0:T(8,128)(2,1)} %collective-permute-done.11), channel_id=1, source_target_pairs={{0,32},{1,33},{2,34},{3,35},{4,36},{5,37},{6,38},{7,39},{8,40},{9,... | collective-permute-start | bytes 1572872 | tf_op jit(solution)/shard_map/ppermute | solution.py:353
  74.8 8.1 %collective-permute-start.20 = (bf16[4,8,8192]{2,1,0:T(8,128)(2,1)}, bf16[4,8,8192]{2,1,0:T(8,128)(2,1)S(1)}, u32[]{:S(2)}, u32[]{:S(2)}) collective-permute-start(bf16[4,8,8192]{2,1,0:T(8,128)(2,1)} %collective-permute-done.12), channel_id=1, source_target_pairs={{0,32},{1,33},{2,34},{3,35},{4,36},{5,37},{6,38},{7,39},{8,40},{9,... | collective-permute-start | bytes 1572872 | tf_op jit(solution)/shard_map/ppermute | solution.py:353
  75.5 23.4 %collective-permute-start.23 = (bf16[4,8,8192]{2,1,0:T(8,128)(2,1)}, bf16[4,8,8192]{2,1,0:T(8,128)(2,1)S(1)}, u32[]{:S(2)}, u32[]{:S(2)}) collective-permute-start(bf16[4,8,8192]{2,1,0:T(8,128)(2,1)} %collective-permute-done.7), channel_id=1, source_target_pairs={{0,12},{1,13},{2,14},{3,15},{4,0},{5,1},{6,2},{7,3},{8,4},{9,5},{1... | collective-permute-start | bytes 1572872 | tf_op jit(solution)/shard_map/ppermute | solution.py:350
  76.3 22.7 %collective-permute-start.24 = (bf16[4,8,8192]{2,1,0:T(8,128)(2,1)S(1)}, bf16[4,8,8192]{2,1,0:T(8,128)(2,1)}, u32[]{:S(2)}, u32[]{:S(2)}) collective-permute-start(bf16[4,8,8192]{2,1,0:T(8,128)(2,1)S(1)} %collective-permute-done.9), channel_id=1, source_target_pairs={{0,64},{1,65},{2,66},{3,67},{4,68},{5,69},{6,70},{7,71},{8,72},{9,... | collective-permute-start | bytes 1572872 | tf_op jit(solution)/shard_map/ppermute | solution.py:369
  78.1 25.3 %collective-permute-start.25 = (bf16[8,8,8192]{2,1,0:T(8,128)(2,1)S(1)}, bf16[8,8,8192]{2,1,0:T(8,128)(2,1)}, u32[]{:S(2)}, u32[]{:S(2)}) collective-permute-start(bf16[8,8,8192]{2,1,0:T(8,128)(2,1)S(1)} %constant_dynamic-update-slice_fusion), channel_id=1, source_target_pairs={{0,32},{1,33},{2,34},{3,35},{4,36},{5,37},{6,38},{7,39},{8,40},{9,... | collective-permute-start | bytes 3145736 | tf_op jit(solution)/shard_map/ppermute | solution.py:353
  80.8 18.2 %collective-permute-start.22 = (bf16[8,8,8192]{2,1,0:T(8,128)(2,1)S(1)}, bf16[8,8,8192]{2,1,0:T(8,128)(2,1)}, u32[]{:S(2)}, u32[]{:S(2)}) collective-permute-start(bf16[8,8,8192]{2,1,0:T(8,128)(2,1)S(1)} %constant_dynamic-update-slice_fusion), channel_id=1, source_target_pairs={{0,80},{1,81},{2,82},{3,83},{4,84},{5,85},{6,86},{7,87},{8,88},{9,... | collective-permute-start | bytes 3145736 | tf_op jit(solution)/shard_map/ppermute | solution.py:368
  82.9 16.1 %collective-permute-start.21 = (bf16[8,8,8192]{2,1,0:T(8,128)(2,1)S(1)}, bf16[8,8,8192]{2,1,0:T(8,128)(2,1)}, u32[]{:S(2)}, u32[]{:S(2)}) collective-permute-start(bf16[8,8,8192]{2,1,0:T(8,128)(2,1)S(1)} %constant_dynamic-update-slice_fusion), channel_id=1, source_target_pairs={{0,16},{1,17},{2,18},{3,19},{4,20},{5,21},{6,22},{7,23},{8,24},{9,... | collective-permute-start | bytes 3145736 | tf_op jit(solution)/shard_map/ppermute | solution.py:368
  99.0 6.1 %collective-permute-start.26 = (bf16[8,8,8192]{2,1,0:T(8,128)(2,1)}, bf16[8,8,8192]{2,1,0:T(8,128)(2,1)S(1)}, u32[]{:S(2)}, u32[]{:S(2)}) collective-permute-start(bf16[8,8,8192]{2,1,0:T(8,128)(2,1)} %collective-permute-done.21), channel_id=1, source_target_pairs={{0,32},{1,33},{2,34},{3,35},{4,36},{5,37},{6,38},{7,39},{8,40},{9,... | collective-permute-start | bytes 3145736 | tf_op jit(solution)/shard_map/ppermute | solution.py:353
  99.2 5.8 %collective-permute-start.27 = (bf16[8,8,8192]{2,1,0:T(8,128)(2,1)}, bf16[8,8,8192]{2,1,0:T(8,128)(2,1)}, u32[]{:S(2)}, u32[]{:S(2)}) collective-permute-start(bf16[8,8,8192]{2,1,0:T(8,128)(2,1)} %collective-permute-done.22), channel_id=1, source_target_pairs={{0,32},{1,33},{2,34},{3,35},{4,36},{5,37},{6,38},{7,39},{8,40},{9,... | collective-permute-start | bytes 3145736 | tf_op jit(solution)/shard_map/ppermute | solution.py:353
  99.6 3.8 %collective-permute-start.28 = (bf16[4,8,8192]{2,1,0:T(8,128)(2,1)S(1)}, bf16[4,8,8192]{2,1,0:T(8,128)(2,1)}, u32[]{:S(2)}, u32[]{:S(2)}) collective-permute-start(bf16[4,8,8192]{2,1,0:T(8,128)(2,1)S(1)} %collective-permute-done.23), channel_id=1, source_target_pairs={{0,32},{1,33},{2,34},{3,35},{4,36},{5,37},{6,38},{7,39},{8,40},{9,... | collective-permute-start | bytes 1572872 | tf_op jit(solution)/shard_map/ppermute | solution.py:353
  99.7 5.3 %collective-permute-start.29 = (bf16[4,8,8192]{2,1,0:T(8,128)(2,1)}, bf16[4,8,8192]{2,1,0:T(8,128)(2,1)}, u32[]{:S(2)}, u32[]{:S(2)}) collective-permute-start(bf16[4,8,8192]{2,1,0:T(8,128)(2,1)} %collective-permute-done.24), channel_id=1, source_target_pairs={{0,32},{1,33},{2,34},{3,35},{4,36},{5,37},{6,38},{7,39},{8,40},{9,... | collective-permute-start | bytes 1572872 | tf_op jit(solution)/shard_map/ppermute | solution.py:353
  (16 other events, 160.2 us)
